TPU v7x, 32 devices: a whole 2x2x4 slice. The times are simulated.
32 devices in a mesh: dp: 8 (over z, y), vocab: 4 (over x, core).
Axes of the slice: x: 2, y: 2, z: 4, core: 2. Of those that a mesh axis runs over, the one named last changes fastest.
Arguments:
- token_ids: int32 [32, 512], P(('dp', 'vocab')), may hold values from 0 to 30719
- segment_ids: int32 [32, 512], P(('dp', 'vocab')), may hold values from 0 to 7, never falling along the last dimension, each value on 1 to 256 neighbouring positions
- labels: int32 [32, 512], P(('dp', 'vocab')), may hold values from 0 to 30719
- loss_mask: int32 [32, 512], P(('dp', 'vocab')), may hold values from 0 to 1, as said below
- teacher_group: int32 [32], P(('dp', 'vocab')), may hold values from 0 to 2
- teacher_inputs: bfloat16 [32, 512, 768], P(('dp', 'vocab')), may hold values from -6 to 6
- teacher_table: bfloat16 [3, 768, 30720], P(None, None, 'vocab'), may hold values from -0.4375 to 0.4375
- teacher_qkv: bfloat16 [3, 768, 2304], P(None, ('dp', 'vocab')), may hold values from -0.21875 to 0.21875
- teacher_out: bfloat16 [3, 768, 768], P(None, ('dp', 'vocab')), may hold values from -0.875 to 0.875
- teacher_up: bfloat16 [3, 768, 3072], P(None, ('dp', 'vocab')), may hold values from -0.21875 to 0.21875
- teacher_down: bfloat16 [3, 3072, 768], P(None, ('dp', 'vocab')), may hold values from -0.109375 to 0.109375
- teacher_gains: float32 [3, 6, 768], replicated, may hold values from 0.5 to 1.5
- step_count: int32 [], replicated, may hold values from 2 to 20
- embed_w: float32 [30720, 512], P('vocab', 'dp'), may hold values from -0.5 to 0.5
- embed_m: float32 [30720, 512], P('vocab', 'dp'), may hold values from -1.9073486e-06 to 1.9073486e-06
- embed_v: float32 [30720, 512], P('vocab', 'dp'), may hold values from 6.5309676e-16 to 1.0449548e-14
- pos_w: float32 [512, 512], P(('dp', 'vocab')), may hold values from -0.5 to 0.5
- pos_m: float32 [512, 512], P(('dp', 'vocab')), may hold values from -1.9073486e-06 to 1.9073486e-06
- pos_v: float32 [512, 512], P(('dp', 'vocab')), may hold values from 6.5309676e-16 to 1.0449548e-14
- qkv_w: float32 [512, 1536], P(('dp', 'vocab')), may hold values from -0.25 to 0.25
- qkv_m: float32 [512, 1536], P(('dp', 'vocab')), may hold values from -1.9073486e-06 to 1.9073486e-06
- qkv_v: float32 [512, 1536], P(('dp', 'vocab')), may hold values from 6.5309676e-16 to 1.0449548e-14
- out_w: float32 [512, 512], P(('dp', 'vocab')), may hold values from -1 to 1
- out_m: float32 [512, 512], P(('dp', 'vocab')), may hold values from -1.9073486e-06 to 1.9073486e-06
- out_v: float32 [512, 512], P(('dp', 'vocab')), may hold values from 6.5309676e-16 to 1.0449548e-14
- up_w: float32 [512, 2048], P(('dp', 'vocab')), may hold values from -0.25 to 0.25
- up_m: float32 [512, 2048], P(('dp', 'vocab')), may hold values from -1.9073486e-06 to 1.9073486e-06
- up_v: float32 [512, 2048], P(('dp', 'vocab')), may hold values from 6.5309676e-16 to 1.0449548e-14
- down_w: float32 [2048, 512], P(('dp', 'vocab')), may hold values from -0.125 to 0.125
- down_m: float32 [2048, 512], P(('dp', 'vocab')), may hold values from -1.9073486e-06 to 1.9073486e-06
- down_v: float32 [2048, 512], P(('dp', 'vocab')), may hold values from 6.5309676e-16 to 1.0449548e-14
- gains_w: float32 [6, 512], replicated, may hold values from 0.5 to 1.5
- gains_m: float32 [6, 512], replicated, may hold values from -7.6293945e-06 to 7.6293945e-06
- gains_v: float32 [6, 512], replicated, may hold values from 1.0449548e-14 to 1.6719277e-13
Outputs:
- loss: float32 [], replicated
- grad_norm: float32 [], replicated
- embed_m_new: float32 [30720, 512], P('vocab', 'dp')
- embed_v_new: float32 [30720, 512], P('vocab', 'dp')
- embed_w_new: float32 [30720, 512], P('vocab', 'dp')
- pos_m_new: float32 [512, 512], P(('dp', 'vocab'))
- pos_v_new: float32 [512, 512], P(('dp', 'vocab'))
- pos_w_new: float32 [512, 512], P(('dp', 'vocab'))
- qkv_m_new: float32 [512, 1536], P(('dp', 'vocab'))
- qkv_v_new: float32 [512, 1536], P(('dp', 'vocab'))
- qkv_w_new: float32 [512, 1536], P(('dp', 'vocab'))
- out_m_new: float32 [512, 512], P(('dp', 'vocab'))
- out_v_new: float32 [512, 512], P(('dp', 'vocab'))
- out_w_new: float32 [512, 512], P(('dp', 'vocab'))
- up_m_new: float32 [512, 2048], P(('dp', 'vocab'))
- up_v_new: float32 [512, 2048], P(('dp', 'vocab'))
- up_w_new: float32 [512, 2048], P(('dp', 'vocab'))
- down_m_new: float32 [2048, 512], P(('dp', 'vocab'))
- down_v_new: float32 [2048, 512], P(('dp', 'vocab'))
- down_w_new: float32 [2048, 512], P(('dp', 'vocab'))
- gains_m_new: float32 [6, 512], replicated
- gains_v_new: float32 [6, 512], replicated
- gains_w_new: float32 [6, 512], replicated
Inputs may be any that keep to these rules, and one draw needn't show every extreme that they name: `segment_ids`: within a row segment numbers never fall; each segment holds 1 to 256 positions. `loss_mask`: 1 marks a position that counts.
All inputs are finite; a program needn't handle non-finite values.
Results may differ from a plain program's by a relative error of at most 0.0072.
Values may be sent and summed in bfloat16 or wider, within the bound.
A program may use at most 320 MiB of HBM per device.

v0:
```python
import jax
import jax.numpy as jnp
from jax import lax
from jax.sharding import PartitionSpec as P

SEGS = 8


NORM_EPS = 1e-05
MIX_ALPHA = 0.5
CLIP_NORM = 0.005
LEARN_RATE = 0.03
GAIN_RATE = 0.4
BETA_ONE = 0.9
BETA_TWO = 0.999
ADAM_EPS = 1e-08
WEIGHT_DECAY = 0.01
GELU_C = 0.7978845608028654


def combined_all(part, axis, combine):
    gathered = jax.tree.map(lambda a: lax.all_gather(a, axis), part)

    def take(source):
        return jax.tree.map(lambda a: lax.dynamic_index_in_dim(a, source, 0, False), gathered)

    return lax.fori_loop(
        1, lax.axis_size(axis), lambda source, state: combine(state, take(source)), take(0)
    )


def norm_rows(values, gain, shift):
    center = values - jnp.mean(values, -1, keepdims=True)
    scaler = lax.rsqrt(jnp.mean(center * center, -1, keepdims=True) + NORM_EPS)
    normed = center * scaler
    return (normed * gain + shift, normed, scaler)


def norm_back(grad, normed, scaler, gain):
    scaled = grad * gain
    inward = scaler * (
        scaled
        - jnp.mean(scaled, -1, keepdims=True)
        - normed * jnp.mean(scaled * normed, -1, keepdims=True)
    )
    return (inward, jnp.sum(grad * normed, 0), jnp.sum(grad, 0))


def gelu_tanh(values):
    return 0.5 * values * (1.0 + jnp.tanh(GELU_C * (values + 0.044715 * values * values * values)))


def gelu_slope(values):
    tangent = jnp.tanh(GELU_C * (values + 0.044715 * values * values * values))
    return 0.5 * (1.0 + tangent) + 0.5 * values * (1.0 - tangent * tangent) * GELU_C * (
        1.0 + 3.0 * 0.044715 * values * values
    )


def positions(segment):
    codes = jnp.arange(SEGS, dtype=jnp.int32)
    starts = jnp.sum((segment[None, :] < codes[:, None]).astype(jnp.int32), 1)
    member = (segment[:, None] == codes[None, :]).astype(jnp.int32)
    return jnp.arange(segment.shape[0], dtype=jnp.int32) - jnp.sum(member * starts[None, :], 1)


def split_heads(packed):
    seq_len = packed.shape[0]
    width = packed.shape[1] // 3
    block = min(512, seq_len)
    parts = [packed[:, i * width : (i + 1) * width].reshape(seq_len, -1, 64) for i in range(3)]
    return (parts[0].reshape(-1, block, parts[0].shape[1], 64), parts[1], parts[2], block)


def block_scores(query_block, segment_block, keys_all, segment):
    scores = (
        jnp.einsum("qhd,khd->hqk", query_block, keys_all, preferred_element_type=jnp.float32)
        * 0.125
    )
    return jnp.where((segment_block[:, None] == segment[None, :])[None], scores, -1e30)


def attend(item):
    packed, segment = item
    blocks, keys_all, values_all, block = split_heads(packed)

    def one_block(pair):
        query_block, segment_block = pair
        scores = block_scores(query_block, segment_block, keys_all, segment)
        top = jnp.max(scores, -1, keepdims=True)
        expd = jnp.exp(scores - top)
        total = jnp.sum(expd, -1, keepdims=True)
        probs = (expd / total).astype(jnp.bfloat16)
        context = jnp.einsum("hqk,khd->qhd", probs, values_all, preferred_element_type=jnp.float32)
        return (context, (top + jnp.log(total))[..., 0])

    context, lse = lax.map(one_block, (blocks, segment.reshape(-1, block)))
    return (context.reshape(packed.shape[0], -1), lse)


def attend_back(item):
    packed, segment, lse, dcontext = item
    blocks, keys_all, values_all, block = split_heads(packed)
    seq_len = packed.shape[0]
    dblocks = dcontext.reshape(-1, block, keys_all.shape[1], 64)

    def one_block(carry, quad):
        dkeys, dvalues = carry
        query_block, segment_block, lse_block, grad_block = quad
        scores = block_scores(query_block, segment_block, keys_all, segment)
        probs = jnp.exp(scores - lse_block[..., None])
        dprobs = jnp.einsum(
            "qhd,khd->hqk", grad_block, values_all, preferred_element_type=jnp.float32
        )
        dscore = (probs * (dprobs - jnp.sum(probs * dprobs, -1, keepdims=True)) * 0.125).astype(
            jnp.bfloat16
        )
        dquery = jnp.einsum("hqk,khd->qhd", dscore, keys_all, preferred_element_type=jnp.float32)
        dkeys = dkeys + jnp.einsum(
            "hqk,qhd->khd", dscore, query_block, preferred_element_type=jnp.float32
        )
        dvalues = dvalues + jnp.einsum(
            "hqk,qhd->khd",
            probs.astype(jnp.bfloat16),
            grad_block,
            preferred_element_type=jnp.float32,
        )
        return ((dkeys, dvalues), dquery)

    zeros = jnp.zeros(keys_all.shape, jnp.float32)
    (dkeys, dvalues), dquery = lax.scan(
        one_block, (zeros, zeros), (blocks, segment.reshape(-1, block), lse, dblocks)
    )
    return jnp.concatenate(
        [dquery.reshape(seq_len, -1), dkeys.reshape(seq_len, -1), dvalues.reshape(seq_len, -1)], 1
    )


def layer_forward(hidden, segment_ids, weights, gains):
    qkv_t, out_t, up_t, down_t = weights
    row_count, seq_len = segment_ids.shape
    h_zero, normed_a, scaler_a = norm_rows(hidden, gains[0], gains[1])
    zero_b = h_zero.astype(jnp.bfloat16)
    packed = jnp.dot(zero_b, qkv_t, preferred_element_type=jnp.float32).astype(jnp.bfloat16)
    packed = packed.reshape(row_count, seq_len, -1)
    context, lse = lax.map(attend, (packed, segment_ids))
    context_b = context.reshape(row_count * seq_len, -1).astype(jnp.bfloat16)
    h_one, normed_b, scaler_b = norm_rows(
        h_zero + jnp.dot(context_b, out_t, preferred_element_type=jnp.float32), gains[2], gains[3]
    )
    one_b = h_one.astype(jnp.bfloat16)
    inner = jnp.dot(one_b, up_t, preferred_element_type=jnp.float32)
    active = gelu_tanh(inner).astype(jnp.bfloat16)
    h_two, normed_c, scaler_c = norm_rows(
        h_one + jnp.dot(active, down_t, preferred_element_type=jnp.float32), gains[4], gains[5]
    )
    kept = (
        normed_a,
        scaler_a,
        zero_b,
        packed,
        lse,
        context_b,
        normed_b,
        scaler_b,
        one_b,
        inner,
        active,
        normed_c,
        scaler_c,
    )
    return (kept, h_two)


def layer_backward(dtwo, segment_ids, weights, gains, kept):
    qkv_t, out_t, up_t, down_t = weights
    (
        normed_a,
        scaler_a,
        zero_b,
        packed,
        lse,
        context_b,
        normed_b,
        scaler_b,
        one_b,
        inner,
        active,
        normed_c,
        scaler_c,
    ) = kept
    row_count, seq_len = segment_ids.shape
    dz_two, gain_c, shift_c = norm_back(dtwo, normed_c, scaler_c, gains[4])
    dbranch = dz_two.astype(jnp.bfloat16)
    grad_down = jnp.einsum("nf,nd->fd", active, dbranch, preferred_element_type=jnp.float32)
    dinner = (
        jnp.dot(dbranch, down_t.T, preferred_element_type=jnp.float32) * gelu_slope(inner)
    ).astype(jnp.bfloat16)
    grad_up = jnp.einsum("nd,nf->df", one_b, dinner, preferred_element_type=jnp.float32)
    dh_one = dz_two + jnp.dot(dinner, up_t.T, preferred_element_type=jnp.float32)
    dz_one, gain_b, shift_b = norm_back(dh_one, normed_b, scaler_b, gains[2])
    dproj = dz_one.astype(jnp.bfloat16)
    grad_out = jnp.einsum("nc,nd->cd", context_b, dproj, preferred_element_type=jnp.float32)
    dcontext = jnp.dot(dproj, out_t.T, preferred_element_type=jnp.float32).astype(jnp.bfloat16)
    dpacked = lax.map(
        attend_back, (packed, segment_ids, lse, dcontext.reshape(row_count, seq_len, -1))
    )
    dpacked = dpacked.reshape(row_count * seq_len, -1).astype(jnp.bfloat16)
    grad_qkv = jnp.einsum("nd,ne->de", zero_b, dpacked, preferred_element_type=jnp.float32)
    dh_zero = dz_one + jnp.dot(dpacked, qkv_t.T, preferred_element_type=jnp.float32)
    dhidden, gain_a, shift_a = norm_back(dh_zero, normed_a, scaler_a, gains[0])
    grad_gains = jnp.stack([gain_a, shift_a, gain_b, shift_b, gain_c, shift_c])
    return (dhidden, (grad_qkv, grad_out, grad_up, grad_down), grad_gains)


def adam(weight, first, second, grad, fix_one, fix_two, rate):
    first = BETA_ONE * first + (1.0 - BETA_ONE) * grad
    second = BETA_TWO * second + (1.0 - BETA_TWO) * grad * grad
    update = first / fix_one / (jnp.sqrt(second / fix_two) + ADAM_EPS)
    return (first, second, weight - rate * (update + WEIGHT_DECAY * weight))


def on_device(
    token_ids,
    segment_ids,
    labels,
    loss_mask,
    teacher_group,
    teacher_inputs,
    teacher_table,
    teacher_qkv,
    teacher_out,
    teacher_up,
    teacher_down,
    teacher_gains,
    step_count,
    embed_w,
    embed_m,
    embed_v,
    pos_w,
    pos_m,
    pos_v,
    qkv_w,
    qkv_m,
    qkv_v,
    out_w,
    out_m,
    out_v,
    up_w,
    up_m,
    up_v,
    down_w,
    down_m,
    down_v,
    gains_w,
    gains_m,
    gains_v,
):
    shards = (pos_w, qkv_w, out_w, up_w, down_w)
    gathered = (
        lax.all_gather(pos_w.astype(jnp.bfloat16), ("dp", "vocab"), axis=0, tiled=True),
        lax.all_gather(qkv_w.astype(jnp.bfloat16), ("dp", "vocab"), axis=0, tiled=True),
        lax.all_gather(out_w.astype(jnp.bfloat16), ("dp", "vocab"), axis=0, tiled=True),
        lax.all_gather(up_w.astype(jnp.bfloat16), ("dp", "vocab"), axis=0, tiled=True),
        lax.all_gather(down_w.astype(jnp.bfloat16), ("dp", "vocab"), axis=0, tiled=True),
        lax.all_gather(teacher_qkv, ("dp", "vocab"), axis=1, tiled=True),
        lax.all_gather(teacher_out, ("dp", "vocab"), axis=1, tiled=True),
        lax.all_gather(teacher_up, ("dp", "vocab"), axis=1, tiled=True),
        lax.all_gather(teacher_down, ("dp", "vocab"), axis=1, tiled=True),
    )
    pos_t = gathered[0]
    weights = gathered[1:5]
    teacher_stack = gathered[5:]
    table = lax.all_gather(embed_w.astype(jnp.bfloat16), "dp", axis=1, tiled=True)
    ids_all, labels_all, mask_all, group_all = (
        lax.all_gather(token_ids, "vocab", axis=0, tiled=True),
        lax.all_gather(labels, "vocab", axis=0, tiled=True),
        lax.all_gather(loss_mask, "vocab", axis=0, tiled=True),
        lax.all_gather(teacher_group, "vocab", axis=0, tiled=True),
    )
    row_count, seq_len = token_ids.shape
    slice_len, width = table.shape
    offset = lax.axis_index("vocab") * slice_len
    vocab_ids = offset + jnp.arange(slice_len, dtype=jnp.int32)
    flat_ids = ids_all.reshape(-1)
    local = flat_ids - offset
    inside = (local >= 0) & (local < slice_len)
    picked = jnp.take(table, jnp.clip(local, 0, slice_len - 1), axis=0).astype(jnp.float32)
    embedded = lax.psum_scatter(
        jnp.where(inside[:, None], picked, 0.0).astype(jnp.bfloat16),
        "vocab",
        scatter_dimension=0,
        tiled=True,
    ).astype(jnp.float32)
    places = jax.vmap(positions)(segment_ids).reshape(-1)
    onehot = (places[:, None] == jnp.arange(pos_t.shape[0], dtype=jnp.int32)[None, :]).astype(
        jnp.bfloat16
    )
    hidden = embedded + jnp.dot(onehot, pos_t, preferred_element_type=jnp.float32)
    kept, h_two = layer_forward(hidden, segment_ids, weights, gains_w)

    def teach_row(item):
        inputs_row, segment_row, group = item
        chosen = tuple(
            (lax.dynamic_index_in_dim(stack, group, 0, keepdims=False) for stack in teacher_stack)
        )
        gains_row = lax.dynamic_index_in_dim(teacher_gains, group, 0, keepdims=False)
        unused, teacher_top = layer_forward(
            inputs_row.astype(jnp.float32), segment_row[None, :], chosen, gains_row
        )
        return teacher_top.astype(jnp.bfloat16)

    teacher_hidden = lax.map(teach_row, (teacher_inputs, segment_ids, teacher_group))
    hidden_all = lax.all_gather(
        h_two.astype(jnp.bfloat16).reshape(row_count, seq_len, width), "vocab", axis=0, tiled=True
    )
    chosen = group_all
    tables = jnp.take(teacher_table, chosen, axis=0)
    teacher_all = jnp.einsum(
        "rlt,rtv->rlv",
        lax.all_gather(teacher_hidden, "vocab", axis=0, tiled=True),
        tables,
        preferred_element_type=jnp.float32,
    ).astype(jnp.bfloat16)

    def row_stats(item):
        hidden_row, teacher_row, label_row = item
        student = jnp.einsum("ld,vd->lv", hidden_row, table, preferred_element_type=jnp.float32)
        teacher = teacher_row.astype(jnp.float32)
        tmax = jnp.max(teacher, -1)
        texp = jnp.exp(teacher - tmax[:, None])
        smax = jnp.max(student, -1)
        ssum = jnp.sum(jnp.exp(student - smax[:, None]), -1)
        picked = jnp.sum(jnp.where(label_row[:, None] == vocab_ids[None, :], student, 0.0), -1)
        return (
            tmax,
            jnp.sum(texp, -1),
            jnp.sum(texp * (teacher - student), -1),
            smax,
            ssum,
            picked,
        )

    stats = lax.map(row_stats, (hidden_all, teacher_all, labels_all))

    def combine(left, right):
        tmax = jnp.maximum(left[0], right[0])
        t_left = jnp.exp(left[0] - tmax)
        t_right = jnp.exp(right[0] - tmax)
        smax = jnp.maximum(left[3], right[3])
        s_left = jnp.exp(left[3] - smax)
        s_right = jnp.exp(right[3] - smax)
        return (
            tmax,
            left[1] * t_left + right[1] * t_right,
            left[2] * t_left + right[2] * t_right,
            smax,
            left[4] * s_left + right[4] * s_right,
            left[5] + right[5],
        )

    tmax, tsum, tcross, smax, ssum, picked = combined_all(stats, "vocab", combine)
    teacher_lse = tmax + jnp.log(tsum)
    student_lse = smax + jnp.log(ssum)
    counts = mask_all.astype(jnp.float32)
    row_terms = counts * (
        MIX_ALPHA * (tcross / tsum - teacher_lse + student_lse) + student_lse - picked
    )
    total, counted = lax.psum((jnp.sum(row_terms), jnp.sum(counts)), "dp")
    counted = jnp.maximum(counted, 1.0)
    loss = total / counted

    def head_step(grad_table, item):
        hidden_row, teacher_row, label_row, count_row, t_lse, s_lse = item
        student = jnp.einsum("ld,vd->lv", hidden_row, table, preferred_element_type=jnp.float32)
        soft = jnp.exp(student - s_lse[:, None])
        target = jnp.exp(teacher_row.astype(jnp.float32) - t_lse[:, None])
        onehot_rows = (label_row[:, None] == vocab_ids[None, :]).astype(jnp.float32)
        dlogits = (
            (count_row / counted)[:, None] * (MIX_ALPHA * (soft - target) + soft - onehot_rows)
        ).astype(jnp.bfloat16)
        grad_table = grad_table + jnp.einsum(
            "lv,ld->vd", dlogits, hidden_row, preferred_element_type=jnp.float32
        )
        return (grad_table, jnp.dot(dlogits, table, preferred_element_type=jnp.float32))

    grad_head, dhidden_all = lax.scan(
        head_step,
        jnp.zeros((slice_len, width), jnp.float32),
        (hidden_all, teacher_all, labels_all, counts, teacher_lse, student_lse),
    )
    dtwo = lax.psum_scatter(dhidden_all, "vocab", scatter_dimension=0, tiled=True).reshape(
        -1, width
    )
    dhidden, dense_grads, grad_gains = layer_backward(dtwo, segment_ids, weights, gains_w, kept)
    grad_pos = jax.ops.segment_sum(dhidden, places, num_segments=pos_t.shape[0])
    local = ids_all.reshape(-1) - offset
    inside = (local >= 0) & (local < slice_len)
    values = jnp.where(
        inside[:, None],
        lax.all_gather(
            dhidden.reshape(row_count, seq_len, width), "vocab", axis=0, tiled=True
        ).reshape(-1, width),
        0.0,
    )
    grad_look = jax.ops.segment_sum(
        values, jnp.clip(local, 0, slice_len - 1), num_segments=slice_len
    )
    grad_embed = lax.psum_scatter(grad_head + grad_look, "dp", scatter_dimension=1, tiled=True)
    grad_qkv, grad_out, grad_up, grad_down = dense_grads
    summed = lax.psum((grad_pos, grad_qkv, grad_out, grad_up, grad_down), ("dp", "vocab"))
    place = lax.axis_index(("dp", "vocab"))
    owned = tuple(
        (
            lax.dynamic_slice_in_dim(full, place * shard.shape[0], shard.shape[0])
            for full, shard in zip(summed, shards)
        )
    )
    squares = jnp.sum(grad_embed * grad_embed)
    for grad in owned:
        squares = squares + jnp.sum(grad * grad)
    squares, gains_grad = lax.psum((squares, grad_gains), ("dp", "vocab"))
    grad_norm = jnp.sqrt(squares + jnp.sum(gains_grad * gains_grad))
    factor = CLIP_NORM / jnp.maximum(grad_norm, CLIP_NORM)
    count_f = step_count.astype(jnp.float32)
    fix_one = 1.0 - jnp.power(BETA_ONE, count_f)
    fix_two = 1.0 - jnp.power(BETA_TWO, count_f)
    e_m, e_v, e_w = adam(
        embed_w, embed_m, embed_v, grad_embed * factor, fix_one, fix_two, LEARN_RATE
    )
    p_m, p_v, p_w = adam(pos_w, pos_m, pos_v, owned[0] * factor, fix_one, fix_two, LEARN_RATE)
    q_m, q_v, q_w = adam(qkv_w, qkv_m, qkv_v, owned[1] * factor, fix_one, fix_two, LEARN_RATE)
    o_m, o_v, o_w = adam(out_w, out_m, out_v, owned[2] * factor, fix_one, fix_two, LEARN_RATE)
    u_m, u_v, u_w = adam(up_w, up_m, up_v, owned[3] * factor, fix_one, fix_two, LEARN_RATE)
    d_m, d_v, d_w = adam(down_w, down_m, down_v, owned[4] * factor, fix_one, fix_two, LEARN_RATE)
    g_m, g_v, g_w = adam(
        gains_w, gains_m, gains_v, gains_grad * factor, fix_one, fix_two, GAIN_RATE
    )
    return (
        loss,
        grad_norm,
        e_m,
        e_v,
        e_w,
        p_m,
        p_v,
        p_w,
        q_m,
        q_v,
        q_w,
        o_m,
        o_v,
        o_w,
        u_m,
        u_v,
        u_w,
        d_m,
        d_v,
        d_w,
        g_m,
        g_v,
        g_w,
    )


def solution(mesh):
    placed = (
        P(("dp", "vocab"), None),
        P(("dp", "vocab"), None),
        P(("dp", "vocab"), None),
        P(("dp", "vocab"), None),
        P(("dp", "vocab")),
        P(("dp", "vocab"), None, None),
        P(None, None, "vocab"),
        P(None, ("dp", "vocab"), None),
        P(None, ("dp", "vocab"), None),
        P(None, ("dp", "vocab"), None),
        P(None, ("dp", "vocab"), None),
        P(),
        P(),
        P("vocab", "dp"),
        P("vocab", "dp"),
        P("vocab", "dp"),
        P(("dp", "vocab"), None),
        P(("dp", "vocab"), None),
        P(("dp", "vocab"), None),
        P(("dp", "vocab"), None),
        P(("dp", "vocab"), None),
        P(("dp", "vocab"), None),
        P(("dp", "vocab"), None),
        P(("dp", "vocab"), None),
        P(("dp", "vocab"), None),
        P(("dp", "vocab"), None),
        P(("dp", "vocab"), None),
        P(("dp", "vocab"), None),
        P(("dp", "vocab"), None),
        P(("dp", "vocab"), None),
        P(("dp", "vocab"), None),
        P(),
        P(),
        P(),
    )
    return jax.shard_map(
        on_device,
        mesh=mesh,
        in_specs=placed,
        out_specs=(
            P(),
            P(),
            P("vocab", "dp"),
            P("vocab", "dp"),
            P("vocab", "dp"),
            P(("dp", "vocab"), None),
            P(("dp", "vocab"), None),
            P(("dp", "vocab"), None),
            P(("dp", "vocab"), None),
            P(("dp", "vocab"), None),
            P(("dp", "vocab"), None),
            P(("dp", "vocab"), None),
            P(("dp", "vocab"), None),
            P(("dp", "vocab"), None),
            P(("dp", "vocab"), None),
            P(("dp", "vocab"), None),
            P(("dp", "vocab"), None),
            P(("dp", "vocab"), None),
            P(("dp", "vocab"), None),
            P(("dp", "vocab"), None),
            P(),
            P(),
            P(),
        ),
        check_vma=False,
    )
```

profile of v0, /device:TPU:0, one launch (start us, length us, event | category | flops | bytes accessed | tf_op | source)
XLA Modules:
  0.0 1791.6 jit_solution(11644261655332558577)
XLA Ops:
  17.7 115.0 %all-gather.38.cloned.1.call-done = bf16[7680,512]{0,1:T(8,128)(2,1)} async-done(((bf16[7680,64]{0,1:T(8,128)(2,1)}), bf16[7680,512]{0,1:T(8,128)(2,1)}) %all-gather.38.cloned.1.call-update) | async-done | bytes 7864336 | tf_op jit(solution)/shard_map/all_gather | solution.py:274
  175.8 40.2 %all_gather.96 = bf16[512,512]{1,0:T(8,128)(2,1)S(1)} all-gather(bf16[16,512]{1,0:T(8,128)(2,1)S(1)} %convert_element_type.188), channel_id=1, replica_groups=mesh['dp'=8,'vocab'=4] {'dp','vocab'}, dimensions={0}, use_global_device_ids=true | all-gather | bytes 540672 | tf_op jit(solution)/shard_map/all_gather | solution.py:261
  216.0 38.4 %all_gather.98 = bf16[512,512]{1,0:T(8,128)(2,1)S(1)} all-gather(bf16[16,512]{1,0:T(8,128)(2,1)S(1)} %convert_element_type.196), channel_id=1, replica_groups=mesh['dp'=8,'vocab'=4] {'dp','vocab'}, dimensions={0}, use_global_device_ids=true | all-gather | bytes 540672 | tf_op jit(solution)/shard_map/all_gather | solution.py:263
  284.9 53.8 %all-gather.44.cloned.1.call-done = bf16[2048,512]{1,0:T(8,128)(2,1)} async-done(((bf16[64,512]{1,0:T(8,128)(2,1)}), bf16[2048,512]{1,0:T(8,128)(2,1)}) %all-gather.44.cloned.1.call-update) | async-done | bytes 2097168 | tf_op jit(solution)/shard_map/all_gather | solution.py:265
  345.9 81.6 %all-gather.30.cloned.1.call-done = bf16[3,768,2304]{2,1,0:T(8,128)(2,1)} async-done(((bf16[3,24,2304]{2,1,0:T(8,128)(2,1)}), bf16[3,768,2304]{2,1,0:T(8,128)(2,1)}) %all-gather.30.cloned.1.call-update) | async-done | bytes 10616848 | tf_op jit(solution)/shard_map/all_gather | solution.py:266
  446.9 42.7 %all-gather.32.cloned.1.call-done = bf16[3,768,768]{2,1,0:T(8,128)(2,1)} async-done(((bf16[3,24,768]{2,1,0:T(8,128)(2,1)}), bf16[3,768,768]{2,1,0:T(8,128)(2,1)}) %all-gather.32.cloned.1.call-update) | async-done | bytes 3538960 | tf_op jit(solution)/shard_map/all_gather | solution.py:267
  493.4 100.7 %all-gather.36.cloned.1.call-done = bf16[3,3072,768]{2,1,0:T(8,128)(2,1)} async-done(((bf16[3,96,768]{2,1,0:T(8,128)(2,1)}), bf16[3,3072,768]{2,1,0:T(8,128)(2,1)}) %all-gather.36.cloned.1.call-update) | async-done | bytes 14155792 | tf_op jit(solution)/shard_map/all_gather | solution.py:269
  594.0 103.9 %all-gather.34.cloned.1.call-done = bf16[3,768,3072]{2,1,0:T(8,128)(2,1)} async-done(((bf16[3,24,3072]{2,1,0:T(8,128)(2,1)}), bf16[3,768,3072]{2,1,0:T(8,128)(2,1)}) %all-gather.34.cloned.1.call-update) | async-done | bytes 14155792 | tf_op jit(solution)/shard_map/all_gather | solution.py:268
  709.6 24.7 %fusion.223 = (bf16[3,768,1280]{2,1,0:T(8,128)(2,1)}, bf16[3,768,1280]{2,1,0:T(8,128)(2,1)}, bf16[3,768,1280]{2,1,0:T(8,128)(2,1)}, bf16[3,768,1280]{2,1,0:T(8,1...) fusion(bf16[3,768,7680]{2,1,0:T(8,128)(2,1)} %param.46), kind=kLoop, calls=%fused_computation.336 | loop fusion | bytes 70778880 | tf_op jit(solution)/shard_map/jit(_take)/gather | solution.py:318
  828.0 34.9 %fusion.37 = bf16[4,512,7680]{2,1,0:T(8,128)(2,1)} fusion(bf16[4,512,768]{2,1,0:T(8,128)(2,1)} %bitcast.371, bf16[4,768,7680]{2,1,0:T(8,128)(2,1)} %constant_dynamic-update-slice_fusion, pred[4]{0:T(512)(128)(4,1)S(1)} %compare_and_fusion.1), kind=kOutput, calls=%fused_computation.68 | convolution fusion | flops 24198512640 | bytes 81788928 | tf_op jit(solution)/shard_map/rlt,rtv->rlv/dot_general | solution.py:319
  863.0 90.9 %while.64 = (s32[]{:T(128)}, f32[4,512]{1,0:T(4,128)S(1)}, f32[4,512]{1,0:T(4,128)S(1)}, f32[4,512]{1,0:T(4,128)S(1)}, f32[4,512]{1,0:T(4,128)S(1)}, /*index=5*/...) while((s32[]{:T(128)}, f32[4,512]{1,0:T(4,128)S(1)}, ...), condition=%wide.region_26.27_spmd.clone, body=%wide.region_19.26_spmd.clone.sunk | while | flops 4077655040 | bytes 55685304 | solution.py:344
  986.0 20.5 %all-reduce.3 = (f32[]{:T(128)}, f32[]{:T(128)}) all-reduce(f32[]{:T(128)} %get-tuple-element.1146, f32[]{:T(128)} %convert_reduce_fusion.2), channel_id=1, replica_groups=mesh['dp'=8,'vocab'=4] {'dp'}, use_global_device_ids=true, to_apply=%region_30.31 | all-reduce | flops 2 | bytes 16 | tf_op jit(solution)/shard_map/psum | solution.py:369
  1007.1 158.4 %while.71 = (s32[]{:T(128)}, f32[7680,512]{1,0:T(8,128)}, f32[4,512,512]{1,2,0:T(8,128)}, f32[4,512]{1,0:T(4,128)S(1)}, f32[]{:T(128)}, /*index=5*/bf16[4,512,51...) while((s32[]{:T(128)}, f32[7680,512]{1,0:T(8,128)}, ...), condition=%wide.region_34.35_spmd.clone, body=%wide.region_33.34_spmd.clone.sunk | while | flops 12130721792 | bytes 112284872 | solution.py:387
  1007.2 15.3 fusion.298
  1058.6 17.8 select_add_fusion.2
  1084.1 15.3 fusion.298
  1099.4 17.8 select_add_fusion.2
  1124.9 15.3 fusion.298
  1140.1 17.8 select_add_fusion.2
  1166.3 40.4 %reduce-scatter.8.cloned.1.call-done = f32[1,512,512]{1,2,0:T(8,128)} async-done(((f32[4,512,512]{1,2,0:T(8,128)}), f32[1,512,512]{1,2,0:T(8,128)}) %reduce-scatter.8.cloned.1.call-update) | async-done | bytes 1048592 | tf_op jit(solution)/shard_map/reduce_scatter | solution.py:392
  1303.4 25.4 %scatter_fusion = f32[7680,512]{1,0:T(8,128)} fusion(f32[7680,512]{1,0:T(8,128)} %get-tuple-element.755, s32[2048]{0:T(1024)S(1)} %bitcast.320, f32[2048,512]{1,0:T(8,128)} %copy.184), kind=kCustom, calls=%fused_computation.7 | custom fusion | flops 1048576 | bytes 12591104 | tf_op jit(solution)/shard_map/scatter-add | solution.py:406
  1328.8 15.7 copy.194
  1345.9 359.4 %all-reduce.6.cloned.1.call-done = (f32[512,512]{1,0:T(8,128)}, f32[512,1536]{1,0:T(8,128)}, f32[512,512]{1,0:T(8,128)}, f32[512,2048]{1,0:T(8,128)}, f32[2048,512]{1,0:T(8,128)}) async-done(((f32[512,512]{1,0:T(8,128)}, f32[512,1536]{1,0:T(8,128)}, f32[512,512]{1,0:T(8,128)}, f32[512,2048]{1,0:T(8,128)}, f32[2048,512]{1,0:T(8,128)}), (f32[512,512]{1,0:T(8,128)}, f32[512,1536]{1,0:T(8,128)}, ...) | async-done | bytes 13631504 | tf_op jit(solution)/shard_map/psum | solution.py:411
  1725.1 40.4 %all-reduce.1 = (f32[]{:T(128)}, f32[6,512]{1,0:T(8,128)S(1)}) all-reduce(f32[]{:T(128)S(6)} %add.577, f32[6,512]{1,0:T(8,128)S(1)} %stack.27), channel_id=1, replica_groups=mesh['dp'=8,'vocab'=4] {'dp','vocab'}, use_global_device_ids=true, to_apply=%region_57.58 | all-reduce | flops 3073 | bytes 24584 | tf_op jit(solution)/shard_map/psum | solution.py:422
  (493 shorter events, 527.2 us)
Async XLA Ops:
  8.0 124.7 %all-gather.38.cloned.1.call-start = ((), (), s32[]{:S(2)}) async-start(), calls=%async_computation.7 | async-start | bytes 8847360 | tf_op jit(solution)/shard_map/all_gather | solution.py:274
  10.7 243.7 %reduce-scatter.6.cloned.1.call-start = ((), (), s32[]{:S(2)}) async-start(), calls=%async_computation.8 | async-start | bytes 2621440 | tf_op jit(solution)/shard_map/reduce_scatter | solution.py:289
  17.1 140.6 %copy-start.76 = (pred[1,4,4,128]{3,1,2,0:T(4,128)(4,1)}, pred[1,4,4,128]{3,1,2,0:T(4,128)(4,1)S(1)}, u32[]{:S(2)}) copy-start(pred[1,4,4,128]{3,1,2,0:T(4,128)(4,1)S(1)} %copy.237) | copy-start | bytes 6148
  161.5 95.1 %all-gather.40.cloned.1.call-start = ((), (), s32[]{:S(2)}) async-start(), calls=%async_computation.9 | async-start | bytes 1622016 | tf_op jit(solution)/shard_map/all_gather | solution.py:262
  162.2 117.8 %all-gather.42.cloned.1.call-start = ((), (), s32[]{:S(2)}) async-start(), calls=%async_computation.10 | async-start | bytes 2162688 | tf_op jit(solution)/shard_map/all_gather | solution.py:264
  162.9 175.8 %all-gather.44.cloned.1.call-start = ((), (), s32[]{:S(2)}) async-start(), calls=%async_computation.11 | async-start | bytes 2162688 | tf_op jit(solution)/shard_map/all_gather | solution.py:265
  163.6 263.8 %all-gather.30.cloned.1.call-start = ((), (), s32[]{:S(2)}) async-start(), calls=%async_computation.3 | async-start | bytes 10948608 | tf_op jit(solution)/shard_map/all_gather | solution.py:266
  164.4 325.2 %all-gather.32.cloned.1.call-start = ((), (), s32[]{:S(2)}) async-start(), calls=%async_computation.4 | async-start | bytes 3649536 | tf_op jit(solution)/shard_map/all_gather | solution.py:267
  165.1 428.9 %all-gather.36.cloned.1.call-start = ((), (), s32[]{:S(2)}) async-start(), calls=%async_computation.6 | async-start | bytes 14598144 | tf_op jit(solution)/shard_map/all_gather | solution.py:269
  165.9 532.1 %all-gather.34.cloned.1.call-start = ((), (), s32[]{:S(2)}) async-start(), calls=%async_computation.5 | async-start | bytes 14598144 | tf_op jit(solution)/shard_map/all_gather | solution.py:268
  166.5 657.4 %all-gather.48.cloned.1.call-start = ((), (), s32[]{:S(2)}) async-start(), calls=%async_computation.14 | async-start | bytes 2621440 | tf_op jit(solution)/shard_map/all_gather | solution.py:314
  175.5 97.8 %copy-start.80 = (f32[1,512]{1,0:T(1,128)}, f32[1,512]{1,0:T(1,128)S(1)}, u32[]{:S(2)}) copy-start(f32[1,512]{1,0:T(1,128)S(1)} %get-tuple-element.1170) | copy-start | bytes 6148
  175.5 97.8 %copy-start.92 = (f32[1,512]{1,0:T(1,128)}, f32[1,512]{1,0:T(1,128)S(1)}, u32[]{:S(2)}) copy-start(f32[1,512]{1,0:T(1,128)S(1)} %get-tuple-element.1169) | copy-start | bytes 6148
  175.5 163.2 %copy-start.51 = (f32[1,512]{1,0:T(1,128)}, f32[1,512]{1,0:T(1,128)S(1)}, u32[]{:S(2)}) copy-start(f32[1,512]{1,0:T(1,128)S(1)} %get-tuple-element.1168) | copy-start | bytes 6148
  175.5 163.2 %copy-start.55 = (f32[1,512]{1,0:T(1,128)}, f32[1,512]{1,0:T(1,128)S(1)}, u32[]{:S(2)}) copy-start(f32[1,512]{1,0:T(1,128)S(1)} %get-tuple-element.1167) | copy-start | bytes 6148
  175.5 168.2 %copy-start.70 = (f32[1,512]{1,0:T(1,128)}, f32[1,512]{1,0:T(1,128)S(1)}, u32[]{:S(2)}) copy-start(f32[1,512]{1,0:T(1,128)S(1)} %get-tuple-element.1166) | copy-start | bytes 6148
  175.8 93.4 %copy-start.16 = (pred[512,512]{0,1:T(8,128)(4,1)}, pred[512,512]{0,1:T(8,128)(4,1)S(1)}, u32[]{:S(2)}) copy-start(pred[512,512]{0,1:T(8,128)(4,1)S(1)} %broadcast_compare_fusion) | copy-start | bytes 786436
  274.3 69.2 %copy-start.53 = (f32[512]{0:T(512)}, f32[512]{0:T(512)S(1)}, u32[]{:S(2)}) copy-start(f32[512]{0:T(512)S(1)} %add_rsqrt_fusion.1) | copy-start | bytes 6148
  343.8 87.9 %copy-start.74 = (f32[512]{0:T(512)}, f32[512]{0:T(512)S(1)}, u32[]{:S(2)}) copy-start(f32[512]{0:T(512)S(1)} %add_rsqrt_fusion) | copy-start | bytes 6148
  345.6 482.4 %all-gather.46.cloned.1.call-start = ((), (), s32[]{:S(2)}) async-start(), calls=%async_computation.13 | async-start | bytes 3932160 | tf_op jit(solution)/shard_map/all_gather | solution.py:321
  709.6 497.2 %reduce-scatter.8.cloned.1.call-start = ((), (), s32[]{:S(2)}) async-start(), calls=%async_computation.12 | async-start | bytes 5242880 | tf_op jit(solution)/shard_map/reduce_scatter | solution.py:392
  1165.6 127.4 %all-gather.50.cloned.1.call-start = ((), (), s32[]{:S(2)}) async-start(), calls=%async_computation.15 | async-start | bytes 5242880 | tf_op jit(solution)/shard_map/all_gather | solution.py:401
  1258.1 447.2 %all-reduce.6.cloned.1.call-start = ((), (), s32[]{:S(2)}) async-start(), calls=%async_computation.17 | async-start | bytes 27262976 | tf_op jit(solution)/shard_map/psum | solution.py:411
  1280.2 432.5 %reduce-scatter.10.cloned.1.call-start = ((), (), s32[]{:S(2)}) async-start(), calls=%async_computation.16 | async-start | bytes 17694720
  (98 other events, 2142.2 us)
Sparse Core Ops, SparseCore 0:
  11.6 121.0 all-gather.37
  161.6 31.9 reduce-scatter.5
  1165.7 40.9 reduce-scatter.7
  1258.2 34.6 all-gather.49
  1344.6 279.2 reduce-scatter.9
Sparse Core Ops, SparseCore 1:
  165.4 55.5 all-gather.39
  224.3 55.6 all-gather.41
  283.3 55.3 all-gather.43
  341.7 85.7 all-gather.29
  430.5 59.1 all-gather.31
  492.6 101.4 all-gather.35
  596.9 101.0 all-gather.33
  699.5 20.6 all-gather.47
  722.2 28.3 all-gather.45
  1280.3 425.0 all-reduce.5
where the time goes:
time: 1800 us; the launch traced here: 1790 us
  waiting for transfers between devices  919 us (51%)
  matrix products  330 us (18%)
  blocking collectives  192 us (11%)
  local copies, waits for them, and re-layouts  178 us (10%)
  other arithmetic  144 us (8%)
  between operations  27.3 us (2%)
    psum x1, waiting for transfers between devices, on_device(): lax.psum((grad_pos, grad_qkv, grad_out, grad_up, grad_down), ('dp', 'voca...  359 us
    all_gather x1, waiting for transfers between devices, on_device(): lax.all_gather(embed_w.astype(jnp.bfloat16), 'dp', axis=1, tiled=True)  115 us
    all_gather x1, waiting for transfers between devices, on_device(): lax.all_gather(teacher_up, ('dp', 'vocab'), axis=1, tiled=True)  104 us
    all_gather x1, waiting for transfers between devices, on_device(): lax.all_gather(teacher_down, ('dp', 'vocab'), axis=1, tiled=True)  101 us
    all_gather x1, waiting for transfers between devices, on_device(): lax.all_gather(teacher_qkv, ('dp', 'vocab'), axis=1, tiled=True)  81.6 us
    unnamed x221, local copies, waits for them, and re-layouts  67.7 us
    gather x7, local copies, waits for them, and re-layouts, on_device(): tables = jnp.take(teacher_table, chosen, axis=0)  67 us
    dot_general x4, matrix products, head_step(): jnp.einsum('lv,ld->vd', dlogits, hidden_row, preferred_element_type=jnp.f...  66.7 us
  transfers between devices with their start and end apart: 15, of which 10 were waited for; matrix products, arithmetic and copies ran while one was open for 14% of the time, Pallas kernels for 0%

commit v1 on v0

v1 whole, which is shorter than its diff:
```python
import functools

import jax
import jax.numpy as jnp
from jax import lax
from jax.experimental import pallas as pl
from jax.experimental.pallas import tpu as pltpu
from jax.sharding import PartitionSpec as P

SEGS = 8
NORM_EPS = 1e-05
MIX_ALPHA = 0.5
CLIP_NORM = 0.005
LEARN_RATE = 0.03
GAIN_RATE = 0.4
BETA_ONE = 0.9
BETA_TWO = 0.999
ADAM_EPS = 1e-08
WEIGHT_DECAY = 0.01
GELU_C = 0.7978845608028654
MESH = pl.DeviceIdType.MESH
F32 = jnp.float32
B16 = jnp.bfloat16
ANYWHERE = pl.BlockSpec(memory_space=pl.ANY)
IN_VMEM = pl.BlockSpec(memory_space=pltpu.VMEM)
MIB = 1 << 20

CYCLES = (
    (0, 1, 3, 2, 6, 7, 5, 9, 11, 10, 14, 15, 13, 12, 8, 4),
    (0, 1, 5, 4, 6, 10, 8, 9, 13, 12, 14, 15, 11, 7, 3, 2),
    (0, 2, 6, 7, 3, 1, 5, 9, 13, 15, 11, 10, 14, 12, 8, 4),
)


def chip_cycle(count, which):
    return CYCLES[which] if count == 16 else tuple(range(count))


def dp_cycle(count):
    return tuple(range(0, count, 2)) + tuple(range(count - 1 - count % 2, 0, -2))


def lookup(table, index):
    out = jnp.int32(table[0])
    for k in range(1, len(table)):
        out = jnp.where(index == k, table[k], out)
    return out


class Ring:
    def __init__(self, D, V, which):
        self.D, self.V = D, V
        d, v = lax.axis_index("dp"), lax.axis_index("vocab")
        self.core, self.v = lax.rem(v, 2), v
        self.over_dp = which == "dp"
        self.n = D if self.over_dp else D * V // 2
        self.table = dp_cycle(D) if self.over_dp else chip_cycle(self.n, which)
        self.me = d if self.over_dp else d * (V // 2) + v // 2
        inverse = tuple(self.table.index(k) for k in range(self.n))
        self.pos = lookup(inverse, self.me)

    def at(self, ahead):
        return lookup(self.table, lax.rem(self.pos + ahead + self.n, self.n))

    def device(self, place):
        if self.over_dp:
            return (place, self.v)
        half = self.V // 2
        return (place // half, lax.rem(place, half) * 2 + self.core)

    def hops(self, parity):
        more, less = self.n // 2, self.n - 1 - self.n // 2
        return (more, less) if parity == 0 else (less, more)


def sibling():
    v = lax.axis_index("vocab")
    return (lax.axis_index("dp"), v + 1 - 2 * lax.rem(v, 2))


def greet(devices):
    barrier = pltpu.get_barrier_semaphore()
    for device in devices:
        pl.semaphore_signal(barrier, inc=1, device_id=device, device_id_type=MESH)
    pl.semaphore_wait(barrier, len(devices))


def on_condition(condition, body):
    if condition is True:
        body()
    elif condition is not False:
        pl.when(condition)(body)


def gather_kernel(D, V, spec, count, *refs):
    ins, outs = refs[:count], refs[count : 2 * count]
    ssem, rsem, xssem, xrsem, lsem = refs[2 * count :]
    rings = {w: Ring(D, V, w) for w in dict.fromkeys(p[3] for p in spec)}
    core = lax.rem(lax.axis_index("vocab"), 2)
    sib = sibling()
    nexts = {w: (r.at(1), r.at(-1)) for w, r in rings.items()}
    both = any(p[3] != "dp" for p in spec)
    greet(
        [r.device(place) for w, r in rings.items() for place in nexts[w]]
        + ([sib] if both else [])
    )

    def dst(piece, slot):
        which, k, lead, _, _ = piece
        return outs[which].at[k, slot] if lead else outs[which].at[slot, k]

    def slot_of(ring, place):
        return place if ring.over_dp else place * 2 + core

    streams = []
    for number, piece in enumerate(spec):
        ring = rings[piece[3]]
        for turn, hops in zip((0, 1), ring.hops(piece[4])):
            streams.append((piece, ring, turn, hops, number))

    def origin(stream, s):
        _, ring, turn, _, _ = stream
        return slot_of(ring, ring.at(-s) if turn == 0 else ring.at(s))

    def remote(i, s, src, slot):
        piece, ring, turn, _, _ = streams[i]
        return pltpu.make_async_remote_copy(
            src_ref=src,
            dst_ref=dst(piece, slot),
            send_sem=ssem.at[s, i],
            recv_sem=rsem.at[s, i],
            device_id=ring.device(nexts[piece[3]][turn]),
            device_id_type=MESH,
        )

    def across(i, s, src, slot):
        return pltpu.make_async_remote_copy(
            src_ref=src,
            dst_ref=dst(streams[i][0], slot),
            send_sem=xssem.at[s, i],
            recv_sem=xrsem.at[s, i],
            device_id=sib,
            device_id_type=MESH,
        )

    def own(i):
        piece, ring, _, _, _ = streams[i]
        return ins[piece[0]].at[piece[1]], slot_of(ring, ring.me)

    for i in range(len(streams)):
        remote(i, 0, *own(i)).start()
    for i, stream in enumerate(streams):
        if stream[2] == 0:
            src, slot = own(i)
            pltpu.make_async_copy(src, dst(stream[0], slot), lsem.at[stream[4]]).start()
            if not stream[1].over_dp:
                across(i, 0, src, slot).start()
    longest = max(s[3] for s in streams)

    def within(s, hops):
        return True if hops == longest else s <= hops

    def body(s, carry):
        for i, stream in enumerate(streams):

            def take(i=i, stream=stream):
                slot = origin(stream, s)
                block = dst(stream[0], slot)
                remote(i, s - 1, block, slot).wait_recv()
                pl.when(s < stream[3])(lambda: remote(i, s, block, slot).start())
                if not stream[1].over_dp:
                    across(i, s, block, slot).start()

            on_condition(within(s, stream[3]), take)
        return carry

    lax.fori_loop(1, longest + 1, body, 0)

    def finish(s, carry):
        for i, stream in enumerate(streams):

            def end(i=i, stream=stream):
                slot = origin(stream, s)
                block = dst(stream[0], slot)
                pl.when(s < stream[3])(lambda: remote(i, s, block, slot).wait_send())
                if not stream[1].over_dp:

                    def crossed():
                        across(i, s, block, slot).wait_send()
                        theirs = slot + 1 - 2 * core
                        across(i, s, block, theirs).wait_recv()

                    on_condition(True if stream[2] == 0 else s > 0, crossed)

            on_condition(within(s, stream[3]), end)
        return carry

    lax.fori_loop(0, longest + 1, finish, 0)
    for i, stream in enumerate(streams):
        if stream[2] == 0:
            src, slot = own(i)
            pltpu.make_async_copy(src, dst(stream[0], slot), lsem.at[stream[4]]).wait()


def ring_gather(D, V, arrays, spec, ident):
    shapes = []
    for which, array in enumerate(arrays):
        piece = next(p for p in spec if p[0] == which)
        places = D if piece[3] == "dp" else D * V
        lead = array.shape[:1]
        shape = lead + (places,) if piece[2] else (places,) + lead
        shapes.append(jax.ShapeDtypeStruct(shape + array.shape[1:], array.dtype))
    longest = max((D if p[3] == "dp" else D * V // 2) // 2 for p in spec) + 1
    sems = pltpu.SemaphoreType.DMA((longest, 2 * len(spec)))
    return pl.pallas_call(
        functools.partial(gather_kernel, D, V, spec, len(arrays)),
        out_shape=shapes,
        in_specs=[ANYWHERE] * len(arrays),
        out_specs=[ANYWHERE] * len(arrays),
        scratch_shapes=[sems] * 4 + [pltpu.SemaphoreType.DMA((len(spec),))],
        compiler_params=pltpu.CompilerParams(collective_id=ident, has_side_effects=True),
    )(*arrays)


def scatter_kernel(D, V, spec, *refs):
    count = len(spec)
    ins, outs = refs[:count], refs[count : 2 * count]
    scratch = list(refs[2 * count :])
    ssem, rsem, xssem, xrsem = scratch[-4:]
    rings = {w: Ring(D, V, w) for w in dict.fromkeys(p[0] for p in spec)}
    core = lax.rem(lax.axis_index("vocab"), 2)
    sib = sibling()
    nexts = {w: (r.at(1), r.at(-1)) for w, r in rings.items()}
    crossing = any(w != "dp" for w in rings)
    greet(
        [r.device(place) for w, r in rings.items() for place in nexts[w]]
        + ([sib] if crossing else [])
    )
    sums, slots = [], []
    for number, (which, parity) in enumerate(spec):
        if which == "dp":
            sums.append(ins[number])
        else:
            sums.append(scratch.pop(0))
        slots.append((scratch.pop(0), scratch.pop(0)))
    streams = []
    for number, (which, parity) in enumerate(spec):
        for turn, hops in zip((0, 1), rings[which].hops(parity)):
            streams.append((number, rings[which], turn, hops, which))
    streams = [s for s in streams if s[3] > 0]

    def place(stream, ahead):
        return stream[1].at(ahead) if stream[2] == 0 else stream[1].at(-ahead)

    def remote(i, s, src):
        number, ring, turn, hops, which = streams[i]
        return pltpu.make_async_remote_copy(
            src_ref=src,
            dst_ref=slots[number][turn].at[s],
            send_sem=ssem.at[s, i],
            recv_sem=rsem.at[s, i],
            device_id=ring.device(nexts[which][turn]),
            device_id_type=MESH,
        )

    def across(number):
        return pltpu.make_async_remote_copy(
            src_ref=ins[number].at[:, 1 - core],
            dst_ref=sums[number],
            send_sem=xssem.at[number],
            recv_sem=xrsem.at[number],
            device_id=sib,
            device_id_type=MESH,
        )

    def first(i):
        number, _, _, hops, _ = streams[i]
        return remote(i, 0, sums[number].at[place(streams[i], hops)])

    for number, (which, _) in enumerate(spec):
        if which != "dp":
            across(number).start()
    for i, stream in enumerate(streams):
        if stream[4] == "dp":
            first(i).start()
    for number, (which, _) in enumerate(spec):
        if which != "dp":
            across(number).wait_recv()

            def add(k, carry, number=number):
                total = sums[number][k].astype(F32) + ins[number][k, core].astype(F32)
                sums[number][k] = total.astype(B16)
                return carry

            lax.fori_loop(0, rings[which].n, add, 0)
            for i, stream in enumerate(streams):
                if stream[0] == number:
                    first(i).start()
    longest = max(s[3] for s in streams)
    stride = {w: max(1, longest // max(max(r.hops(0)), 1)) for w, r in rings.items()}

    def body(s, carry):
        for i, stream in enumerate(streams):
            number, ring, turn, hops, which = stream
            by = stride[which]

            def take(i=i, stream=stream, number=number, turn=turn, hops=hops, by=by):
                step = s // by
                block = slots[number][turn].at[step - 1]
                remote(i, step - 1, block).wait_recv()

                def onward():
                    mine = sums[number].at[place(stream, hops - step)]
                    block[...] = (block[...].astype(F32) + mine[...].astype(F32)).astype(B16)
                    remote(i, step, block).start()

                pl.when(step < hops)(onward)

            condition = True
            if by > 1 or hops * by < longest:
                condition = (lax.rem(s, by) == 0) & (s // by <= hops)
            on_condition(condition, take)
        return carry

    lax.fori_loop(1, longest + 1, body, 0)
    for number, (which, parity) in enumerate(spec):
        total = sums[number][rings[which].me].astype(F32)
        for turn, hops in zip((0, 1), rings[which].hops(parity)):
            if hops > 0:
                total = total + slots[number][turn][hops - 1].astype(F32)
        outs[number][...] = total
    for i, stream in enumerate(streams):
        number, ring, turn, hops, which = stream
        first(i).wait_send()

        def sent(s, carry, i=i, number=number, turn=turn):
            remote(i, s, slots[number][turn].at[s - 1]).wait_send()
            return carry

        lax.fori_loop(1, hops, sent, 0)
    for number, (which, _) in enumerate(spec):
        if which != "dp":
            across(number).wait_send()


def ring_scatter(D, V, arrays, spec, ident):
    scratch, shapes = [], []
    for array, (which, parity) in zip(arrays, spec):
        block = array.shape[-2:]
        n = D if which == "dp" else D * V // 2
        if which != "dp":
            scratch.append(pltpu.VMEM((n,) + block, B16))
        more, less = n // 2, n - 1 - n // 2
        scratch += [pltpu.VMEM((max(k, 1),) + block, B16) for k in ((more, less), (less, more))[parity]]
        shapes.append(jax.ShapeDtypeStruct(block, F32))
    longest = max((D if w == "dp" else D * V // 2) // 2 for w, _ in spec)
    sems = pltpu.SemaphoreType.DMA((longest, 2 * len(spec)))
    single = pltpu.SemaphoreType.DMA((len(spec),))
    return pl.pallas_call(
        functools.partial(scatter_kernel, D, V, spec),
        out_shape=shapes,
        in_specs=[IN_VMEM] * len(arrays),
        out_specs=[IN_VMEM] * len(arrays),
        scratch_shapes=scratch + [sems, sems, single, single],
        compiler_params=pltpu.CompilerParams(
            collective_id=ident, has_side_effects=True, vmem_limit_bytes=56 * MIB
        ),
    )(*arrays)


def vocab_gather_kernel(V, count, *refs):
    ins, outs = refs[:count], refs[count : 2 * count]
    ssem, rsem, xssem, xrsem, lsem = refs[2 * count :]
    d, v = lax.axis_index("dp"), lax.axis_index("vocab")
    half = V // 2
    core, chip = lax.rem(v, 2), v // 2
    sib = sibling()

    def other(k):
        return lax.rem(chip + k + half, half) * 2 + core

    greet([(d, other(k)) for k in range(1, half)] + [sib])

    def send(q, k):
        return pltpu.make_async_remote_copy(
            src_ref=ins[q],
            dst_ref=outs[q].at[v],
            send_sem=ssem.at[q, k],
            recv_sem=rsem.at[q, k],
            device_id=(d, other(k)),
            device_id_type=MESH,
        )

    def across(q, k, src, slot):
        return pltpu.make_async_remote_copy(
            src_ref=src,
            dst_ref=outs[q].at[slot],
            send_sem=xssem.at[q, k],
            recv_sem=xrsem.at[q, k],
            device_id=sib,
            device_id_type=MESH,
        )

    for q in range(count):
        for k in range(1, half):
            send(q, k).start()
    for q in range(count):
        across(q, 0, ins[q], v).start()
        pltpu.make_async_copy(ins[q], outs[q].at[v], lsem.at[q]).start()
    for q in range(count):
        for k in range(1, half):
            slot = other(-k)
            send(q, k).wait_recv()
            across(q, k, outs[q].at[slot], slot).start()
    for q in range(count):
        pltpu.make_async_copy(ins[q], outs[q].at[v], lsem.at[q]).wait()
        for k in range(half):
            slot = other(-k)
            if k:
                send(q, k).wait_send()
            across(q, k, outs[q].at[slot], slot).wait_send()
            across(q, k, outs[q].at[slot], slot + 1 - 2 * core).wait_recv()


def vocab_gather(V, arrays, ident):
    count = len(arrays)
    sems = pltpu.SemaphoreType.DMA((count, V // 2))
    return pl.pallas_call(
        functools.partial(vocab_gather_kernel, V, count),
        out_shape=[jax.ShapeDtypeStruct((V,) + a.shape, a.dtype) for a in arrays],
        in_specs=[ANYWHERE] * count,
        out_specs=[ANYWHERE] * count,
        scratch_shapes=[sems] * 4 + [pltpu.SemaphoreType.DMA((count,))],
        compiler_params=pltpu.CompilerParams(collective_id=ident, has_side_effects=True),
    )(*arrays)


def vocab_scatter_kernel(V, in_ref, out_ref, sums, taken, ssem, rsem, xsem):
    d, v = lax.axis_index("dp"), lax.axis_index("vocab")
    half = V // 2
    core, chip = lax.rem(v, 2), v // 2
    sib = sibling()

    def other(k):
        return lax.rem(chip + k + half, half)

    greet([(d, other(k) * 2 + core) for k in range(1, half)] + [sib])
    across = pltpu.make_async_remote_copy(
        src_ref=in_ref.at[:, 1 - core],
        dst_ref=sums,
        send_sem=xsem.at[0],
        recv_sem=xsem.at[1],
        device_id=sib,
        device_id_type=MESH,
    )
    across.start()
    across.wait_recv()

    def send(k):
        return pltpu.make_async_remote_copy(
            src_ref=sums.at[other(k)],
            dst_ref=taken.at[k - 1],
            send_sem=ssem.at[k - 1],
            recv_sem=rsem.at[k - 1],
            device_id=(d, other(k) * 2 + core),
            device_id_type=MESH,
        )

    for k in [*range(1, half), 0]:
        to = other(k)
        total = sums[to].astype(F32) + in_ref[to, core].astype(F32)
        sums[to] = total.astype(B16)
        if k:
            send(k).start()
    total = sums[chip].astype(F32)
    for k in range(1, half):
        send(k).wait_recv()
        total = total + taken[k - 1].astype(F32)
    out_ref[...] = total
    for k in range(1, half):
        send(k).wait_send()
    across.wait_send()


def vocab_scatter(V, array, ident):
    half = V // 2
    block = array.shape[1:]
    sems = pltpu.SemaphoreType.DMA((max(half - 1, 1),))
    return pl.pallas_call(
        functools.partial(vocab_scatter_kernel, V),
        out_shape=jax.ShapeDtypeStruct(block, F32),
        in_specs=[IN_VMEM],
        out_specs=IN_VMEM,
        scratch_shapes=[
            pltpu.VMEM((half,) + block, B16),
            pltpu.VMEM((max(half - 1, 1),) + block, B16),
            sems,
            sems,
            pltpu.SemaphoreType.DMA((2,)),
        ],
        compiler_params=pltpu.CompilerParams(
            collective_id=ident, has_side_effects=True, vmem_limit_bytes=40 * MIB
        ),
    )(array.reshape((half, 2) + block))


def total_kernel(D, V, in_ref, out_ref, first, second, ssem, rsem):
    d, v = lax.axis_index("dp"), lax.axis_index("vocab")
    peers = [(d, lax.rem(v + k, V)) for k in range(1, V)]
    peers += [(lax.rem(d + k, D), v) for k in range(1, D)]
    greet(peers)

    def send(k):
        over = first if k < V - 1 else second
        mine = v if k < V - 1 else d
        return pltpu.make_async_remote_copy(
            src_ref=over.at[mine],
            dst_ref=over.at[mine],
            send_sem=ssem.at[k],
            recv_sem=rsem.at[k],
            device_id=peers[k],
            device_id_type=MESH,
        )

    def stage(slots, mine, value, low, high):
        slots[mine] = value
        for k in range(low, high):
            send(k).start()
        for k in range(low, high):
            send(k).wait_recv()
        total = slots[0]
        for k in range(1, slots.shape[0]):
            total = total + slots[k]
        return total

    total = stage(first, v, in_ref[...], 0, V - 1)
    out_ref[...] = stage(second, d, total, V - 1, V + D - 2)
    for k in range(V + D - 2):
        send(k).wait_send()


def total_all(D, V, array, ident):
    sems = pltpu.SemaphoreType.DMA((V + D - 2,))
    return pl.pallas_call(
        functools.partial(total_kernel, D, V),
        out_shape=jax.ShapeDtypeStruct(array.shape, F32),
        in_specs=[IN_VMEM],
        out_specs=IN_VMEM,
        scratch_shapes=[pltpu.VMEM((V,) + array.shape, F32), pltpu.VMEM((D,) + array.shape, F32), sems, sems],
        compiler_params=pltpu.CompilerParams(collective_id=ident, has_side_effects=True),
    )(array)


def tile_of(size):
    return next(t for t in (1280, 768, 512, 256, 128) if size % t == 0)


def lane_fold(values, combine):
    out = values[:, :128]
    for k in range(1, values.shape[1] // 128):
        out = combine(out, values[:, k * 128 : (k + 1) * 128])
    return out


def running(values, top_ref, sum_ref, rows):
    old = top_ref[rows, :]
    top = jnp.maximum(old, lane_fold(values, jnp.maximum))
    fade = jnp.exp(old - top)
    expd = jnp.concatenate(
        [jnp.exp(values[:, k * 128 : (k + 1) * 128] - top) for k in range(values.shape[1] // 128)], 1
    )
    top_ref[rows, :] = top
    sum_ref[rows, :] = sum_ref[rows, :] * fade + lane_fold(expd, jnp.add)
    return expd, fade


def pack_rows(columns):
    lane = lax.broadcasted_iota(jnp.int32, (columns[0].shape[0], 128), 1)
    packed = jnp.zeros(lane.shape, F32)
    for k, column in enumerate(columns):
        packed = jnp.where(lane == k, column, packed)
    return packed.T[:8]


def student_stats_kernel(block, hidden_ref, table_ref, out_ref, top_ref, sum_ref):
    step = pl.program_id(0)

    @pl.when(step == 0)
    def _():
        top_ref[...] = jnp.full(top_ref.shape, -jnp.inf, F32)
        sum_ref[...] = jnp.zeros(sum_ref.shape, F32)

    def one(k, carry):
        rows = pl.ds(pl.multiple_of(k * block, block), block)
        logits = jnp.dot(hidden_ref[rows, :], table_ref[...], preferred_element_type=F32)
        running(logits, top_ref, sum_ref, rows)
        return carry

    lax.fori_loop(0, hidden_ref.shape[0] // block, one, 0)

    @pl.when(step == pl.num_programs(0) - 1)
    def _():
        top = jnp.max(top_ref[...], 1, keepdims=True)
        total = jnp.sum(sum_ref[...] * jnp.exp(top_ref[...] - top), 1, keepdims=True)
        out_ref[...] = pack_rows([top, total])


def student_stats(hidden, table):
    tokens, width = hidden.shape
    size = table.shape[1]
    tile = tile_of(size)
    return pl.pallas_call(
        functools.partial(student_stats_kernel, 256),
        grid=(size // tile,),
        out_shape=jax.ShapeDtypeStruct((8, tokens), F32),
        in_specs=[
            pl.BlockSpec((tokens, width), lambda j: (0, 0)),
            pl.BlockSpec((width, tile), lambda j: (0, j)),
        ],
        out_specs=pl.BlockSpec((8, tokens), lambda j: (0, 0)),
        scratch_shapes=[pltpu.VMEM((tokens, 128), F32)] * 2,
        compiler_params=pltpu.CompilerParams(vmem_limit_bytes=48 * MIB),
    )(hidden, table)


def student_grad_kernel(
    block, hidden_ref, turned_ref, table_ref, lse_ref, weight_ref, label_ref, dh_ref, grad_ref, pick_ref
):
    step = pl.program_id(0)
    tile = table_ref.shape[1]

    @pl.when(step == 0)
    def _():
        dh_ref[...] = jnp.zeros(dh_ref.shape, F32)
        pick_ref[...] = jnp.zeros(pick_ref.shape, F32)

    grad_ref[...] = jnp.zeros(grad_ref.shape, F32)

    def one(k, carry):
        rows = pl.ds(pl.multiple_of(k * block, block), block)
        logits = jnp.dot(hidden_ref[rows, :], table_ref[...], preferred_element_type=F32)
        soft = jnp.exp(logits - lse_ref[rows, :])
        weight = weight_ref[rows, :]
        lane = lax.broadcasted_iota(jnp.int32, logits.shape, 1)
        hit = lane == label_ref[rows, :] - step * tile
        dlogits = (((1.0 + MIX_ALPHA) * weight) * soft - jnp.where(hit, weight, 0.0)).astype(B16)
        pick_ref[rows, :] += lane_fold(jnp.where(hit, logits, 0.0), jnp.add)
        dh_ref[rows, :] += lax.dot_general(
            dlogits, table_ref[...], (((1,), (1,)), ((), ())), preferred_element_type=F32
        )
        grad_ref[...] += jnp.dot(turned_ref[:, rows], dlogits, preferred_element_type=F32)
        return carry

    lax.fori_loop(0, hidden_ref.shape[0] // block, one, 0)


def student_grad(hidden, turned, table, lse, weight, label):
    tokens, width = hidden.shape
    size = table.shape[1]
    tile = tile_of(size)
    whole = lambda *shape: pl.BlockSpec(shape, lambda j: (0, 0))
    return pl.pallas_call(
        functools.partial(student_grad_kernel, 512),
        grid=(size // tile,),
        out_shape=[
            jax.ShapeDtypeStruct((tokens, width), F32),
            jax.ShapeDtypeStruct((width, size), F32),
            jax.ShapeDtypeStruct((tokens, 128), F32),
        ],
        in_specs=[
            whole(tokens, width),
            whole(width, tokens),
            pl.BlockSpec((width, tile), lambda j: (0, j)),
            whole(tokens, 1),
            whole(tokens, 1),
            whole(tokens, 1),
        ],
        out_specs=[
            whole(tokens, width),
            pl.BlockSpec((width, tile), lambda j: (0, j)),
            whole(tokens, 128),
        ],
        compiler_params=pltpu.CompilerParams(vmem_limit_bytes=56 * MIB),
    )(hidden, turned, table, lse, weight, label)


def teacher_stats_kernel(group_ref, hidden_ref, table_ref, out_ref, stats_ref, top_ref, sum_ref, cross_ref):
    step, row = pl.program_id(0), pl.program_id(1)
    length = hidden_ref.shape[1]
    rows = pl.ds(pl.multiple_of(row * length, length), length)

    @pl.when(step == 0)
    def _():
        top_ref[rows, :] = jnp.full((length, 128), -jnp.inf, F32)
        sum_ref[rows, :] = jnp.zeros((length, 128), F32)
        cross_ref[rows, :] = jnp.zeros((length, 128), F32)

    rounded = jnp.dot(hidden_ref[0], table_ref[0], preferred_element_type=F32).astype(B16)
    out_ref[0] = rounded
    values = rounded.astype(F32)
    expd, fade = running(values, top_ref, sum_ref, rows)
    cross_ref[rows, :] = cross_ref[rows, :] * fade + lane_fold(expd * values, jnp.add)

    @pl.when((step == pl.num_programs(0) - 1) & (row == pl.num_programs(1) - 1))
    def _():
        top = jnp.max(top_ref[...], 1, keepdims=True)
        scale = jnp.exp(top_ref[...] - top)
        total = jnp.sum(sum_ref[...] * scale, 1, keepdims=True)
        cross = jnp.sum(cross_ref[...] * scale, 1, keepdims=True)
        stats_ref[...] = pack_rows([top, total, cross])


def teacher_stats(groups, hidden, tables):
    count, length, width = hidden.shape
    size = tables.shape[2]
    tile = tile_of(size)
    tokens = count * length
    return pl.pallas_call(
        teacher_stats_kernel,
        grid_spec=pltpu.PrefetchScalarGridSpec(
            num_scalar_prefetch=1,
            grid=(size // tile, count),
            in_specs=[
                pl.BlockSpec((1, length, width), lambda j, r, g: (r, 0, 0)),
                pl.BlockSpec((1, width, tile), lambda j, r, g: (g[r], 0, j)),
            ],
            out_specs=[
                pl.BlockSpec((1, length, tile), lambda j, r, g: (r, 0, j)),
                pl.BlockSpec((8, tokens), lambda j, r, g: (0, 0)),
            ],
            scratch_shapes=[pltpu.VMEM((tokens, 128), F32)] * 3,
        ),
        out_shape=[
            jax.ShapeDtypeStruct((count, length, size), B16),
            jax.ShapeDtypeStruct((8, tokens), F32),
        ],
        compiler_params=pltpu.CompilerParams(vmem_limit_bytes=48 * MIB),
    )(groups, hidden, tables)


def teacher_grad_kernel(teacher_ref, turned_ref, table_ref, lse_ref, weight_ref, gradin_ref, dh_ref, grad_ref):
    step = pl.program_id(0)
    count, length = teacher_ref.shape[:2]

    @pl.when(step == 0)
    def _():
        dh_ref[...] = jnp.zeros(dh_ref.shape, F32)

    grad_ref[...] = gradin_ref[...]

    def one(k, carry):
        rows = pl.ds(pl.multiple_of(k * length, length), length)
        target = jnp.exp(teacher_ref[k].astype(F32) - lse_ref[rows, :])
        dlogits = ((-MIX_ALPHA * weight_ref[rows, :]) * target).astype(B16)
        dh_ref[rows, :] += lax.dot_general(
            dlogits, table_ref[...], (((1,), (1,)), ((), ())), preferred_element_type=F32
        )
        grad_ref[...] += jnp.dot(turned_ref[:, rows], dlogits, preferred_element_type=F32)
        return carry

    lax.fori_loop(0, count, one, 0)


def teacher_grad(teacher, turned, table, lse, weight, grad):
    count, length, size = teacher.shape
    width, tokens = turned.shape
    tile = tile_of(size)
    whole = lambda *shape: pl.BlockSpec(shape, lambda j: (0, 0))
    return pl.pallas_call(
        teacher_grad_kernel,
        grid=(size // tile,),
        out_shape=[jax.ShapeDtypeStruct((tokens, width), F32), jax.ShapeDtypeStruct((width, size), F32)],
        in_specs=[
            pl.BlockSpec((count, length, tile), lambda j: (0, 0, j)),
            whole(width, tokens),
            pl.BlockSpec((width, tile), lambda j: (0, j)),
            whole(tokens, 1),
            whole(tokens, 1),
            pl.BlockSpec((width, tile), lambda j: (0, j)),
        ],
        out_specs=[whole(tokens, width), pl.BlockSpec((width, tile), lambda j: (0, j))],
        compiler_params=pltpu.CompilerParams(vmem_limit_bytes=60 * MIB),
    )(teacher, turned, table, lse, weight, grad)


def pick_kernel(block, ids_ref, table_ref, out_ref):
    step = pl.program_id(0)
    tile = table_ref.shape[1]

    @pl.when(step == 0)
    def _():
        out_ref[...] = jnp.zeros(out_ref.shape, F32)

    def one(k, carry):
        rows = pl.ds(pl.multiple_of(k * block, block), block)
        lane = lax.broadcasted_iota(jnp.int32, (block, tile), 1)
        hit = jnp.where(lane == ids_ref[rows, :] - step * tile, 1.0, 0.0).astype(B16)
        out_ref[rows, :] += lax.dot_general(
            hit, table_ref[...], (((1,), (1,)), ((), ())), preferred_element_type=F32
        )
        return carry

    lax.fori_loop(0, ids_ref.shape[0] // block, one, 0)


def pick_rows(ids, table):
    tokens = ids.shape[0]
    width, size = table.shape
    tile = tile_of(size)
    return pl.pallas_call(
        functools.partial(pick_kernel, 512),
        grid=(size // tile,),
        out_shape=jax.ShapeDtypeStruct((tokens, width), F32),
        in_specs=[
            pl.BlockSpec((tokens, 1), lambda j: (0, 0)),
            pl.BlockSpec((width, tile), lambda j: (0, j)),
        ],
        out_specs=pl.BlockSpec((tokens, width), lambda j: (0, 0)),
        compiler_params=pltpu.CompilerParams(vmem_limit_bytes=48 * MIB),
    )(ids, table)


def spread_kernel(ids_ref, turned_ref, grad_ref, out_ref):
    step = pl.program_id(0)
    tile = grad_ref.shape[1]
    count, _, length = turned_ref.shape

    def one(k, total):
        rows = pl.ds(pl.multiple_of(k * length, length), length)
        lane = lax.broadcasted_iota(jnp.int32, (length, tile), 1)
        hit = jnp.where(lane == ids_ref[rows, :] - step * tile, 1.0, 0.0).astype(B16)
        return total + jnp.dot(turned_ref[k], hit, preferred_element_type=F32)

    out_ref[...] = lax.fori_loop(0, count, one, grad_ref[...]).astype(B16)


def spread_rows(ids, turned, grad):
    tokens = ids.shape[0]
    width, size = grad.shape
    tile = tile_of(size)
    return pl.pallas_call(
        spread_kernel,
        grid=(size // tile,),
        out_shape=jax.ShapeDtypeStruct((width, size), B16),
        in_specs=[
            pl.BlockSpec((tokens, 1), lambda j: (0, 0)),
            pl.BlockSpec(turned.shape, lambda j: (0, 0, 0)),
            pl.BlockSpec((width, tile), lambda j: (0, j)),
        ],
        out_specs=pl.BlockSpec((width, tile), lambda j: (0, j)),
        compiler_params=pltpu.CompilerParams(vmem_limit_bytes=48 * MIB),
    )(ids, turned, grad)


def norm_rows(values, gain, shift):
    center = values - jnp.mean(values, -1, keepdims=True)
    scaler = lax.rsqrt(jnp.mean(center * center, -1, keepdims=True) + NORM_EPS)
    normed = center * scaler
    return (normed * gain + shift, normed, scaler)


def norm_back(grad, normed, scaler, gain):
    scaled = grad * gain
    inward = scaler * (
        scaled
        - jnp.mean(scaled, -1, keepdims=True)
        - normed * jnp.mean(scaled * normed, -1, keepdims=True)
    )
    return (inward, jnp.sum(grad * normed, 0), jnp.sum(grad, 0))


def gelu_tanh(values):
    return 0.5 * values * (1.0 + jnp.tanh(GELU_C * (values + 0.044715 * values * values * values)))


def gelu_slope(values):
    tangent = jnp.tanh(GELU_C * (values + 0.044715 * values * values * values))
    return 0.5 * (1.0 + tangent) + 0.5 * values * (1.0 - tangent * tangent) * GELU_C * (
        1.0 + 3.0 * 0.044715 * values * values
    )


def positions(segment):
    codes = jnp.arange(SEGS, dtype=jnp.int32)
    starts = jnp.sum((segment[None, :] < codes[:, None]).astype(jnp.int32), 1)
    member = (segment[:, None] == codes[None, :]).astype(jnp.int32)
    return jnp.arange(segment.shape[0], dtype=jnp.int32) - jnp.sum(member * starts[None, :], 1)


def split_heads(packed):
    width = packed.shape[1] // 3
    return [packed[:, i * width : (i + 1) * width].reshape(packed.shape[0], -1, 64) for i in range(3)]


def masked_scores(queries, keys, segment):
    scores = jnp.einsum("qhd,khd->hqk", queries, keys, preferred_element_type=F32) * 0.125
    return jnp.where((segment[:, None] == segment[None, :])[None], scores, -1e30)


def attend(packed, segment):
    queries, keys, values = split_heads(packed)
    scores = masked_scores(queries, keys, segment)
    top = jnp.max(scores, -1, keepdims=True)
    expd = jnp.exp(scores - top)
    total = jnp.sum(expd, -1, keepdims=True)
    probs = (expd / total).astype(B16)
    context = jnp.einsum("hqk,khd->qhd", probs, values, preferred_element_type=F32)
    return context.reshape(packed.shape[0], -1).astype(B16), (top + jnp.log(total))[..., 0]


def attend_back(packed, segment, lse, dcontext):
    queries, keys, values = split_heads(packed)
    length = packed.shape[0]
    grads = dcontext.reshape(queries.shape)
    probs = jnp.exp(masked_scores(queries, keys, segment) - lse[..., None])
    dprobs = jnp.einsum("qhd,khd->hqk", grads, values, preferred_element_type=F32)
    inner = jnp.sum(probs * dprobs, -1, keepdims=True)
    dscore = (probs * (dprobs - inner) * 0.125).astype(B16)
    parts = (
        jnp.einsum("hqk,khd->qhd", dscore, keys, preferred_element_type=F32),
        jnp.einsum("hqk,qhd->khd", dscore, queries, preferred_element_type=F32),
        jnp.einsum("hqk,qhd->khd", probs.astype(B16), grads, preferred_element_type=F32),
    )
    return jnp.concatenate([p.reshape(length, -1) for p in parts], 1)


def layer_forward(hidden, segment, weights, gains):
    qkv_t, out_t, up_t, down_t = weights
    h_zero, normed_a, scaler_a = norm_rows(hidden, gains[0], gains[1])
    zero_b = h_zero.astype(B16)
    packed = jnp.dot(zero_b, qkv_t, preferred_element_type=F32).astype(B16)
    context_b, lse = attend(packed, segment)
    h_one, normed_b, scaler_b = norm_rows(
        h_zero + jnp.dot(context_b, out_t, preferred_element_type=F32), gains[2], gains[3]
    )
    one_b = h_one.astype(B16)
    inner = jnp.dot(one_b, up_t, preferred_element_type=F32)
    active = gelu_tanh(inner).astype(B16)
    h_two, normed_c, scaler_c = norm_rows(
        h_one + jnp.dot(active, down_t, preferred_element_type=F32), gains[4], gains[5]
    )
    kept = (normed_a, scaler_a, zero_b, packed, lse, context_b, normed_b, scaler_b, one_b, inner, active, normed_c, scaler_c)
    return (kept, h_two)


def layer_backward(dtwo, segment, weights, gains, kept):
    qkv_t, out_t, up_t, down_t = weights
    (normed_a, scaler_a, zero_b, packed, lse, context_b, normed_b, scaler_b, one_b, inner, active, normed_c, scaler_c) = kept
    dz_two, gain_c, shift_c = norm_back(dtwo, normed_c, scaler_c, gains[4])
    dbranch = dz_two.astype(B16)
    grad_down = jnp.einsum("nf,nd->fd", active, dbranch, preferred_element_type=F32)
    dinner = (jnp.dot(dbranch, down_t.T, preferred_element_type=F32) * gelu_slope(inner)).astype(B16)
    grad_up = jnp.einsum("nd,nf->df", one_b, dinner, preferred_element_type=F32)
    dh_one = dz_two + jnp.dot(dinner, up_t.T, preferred_element_type=F32)
    dz_one, gain_b, shift_b = norm_back(dh_one, normed_b, scaler_b, gains[2])
    dproj = dz_one.astype(B16)
    grad_out = jnp.einsum("nc,nd->cd", context_b, dproj, preferred_element_type=F32)
    dcontext = jnp.dot(dproj, out_t.T, preferred_element_type=F32).astype(B16)
    dpacked = attend_back(packed, segment, lse, dcontext).astype(B16)
    grad_qkv = jnp.einsum("nd,ne->de", zero_b, dpacked, preferred_element_type=F32)
    dh_zero = dz_one + jnp.dot(dpacked, qkv_t.T, preferred_element_type=F32)
    dhidden, gain_a, shift_a = norm_back(dh_zero, normed_a, scaler_a, gains[0])
    grad_gains = jnp.stack([gain_a, shift_a, gain_b, shift_b, gain_c, shift_c])
    return (dhidden, (grad_qkv, grad_out, grad_up, grad_down), grad_gains)


def adam(weight, first, second, grad, fix_one, fix_two, rate):
    first = BETA_ONE * first + (1.0 - BETA_ONE) * grad
    second = BETA_TWO * second + (1.0 - BETA_TWO) * grad * grad
    update = first / fix_one / (jnp.sqrt(second / fix_two) + ADAM_EPS)
    return (first, second, weight - rate * (update + WEIGHT_DECAY * weight))


def on_device(
    D, V,
    token_ids, segment_ids, labels, loss_mask, teacher_group, teacher_inputs, teacher_table,
    teacher_qkv, teacher_out, teacher_up, teacher_down, teacher_gains, step_count,
    embed_w, embed_m, embed_v, pos_w, pos_m, pos_v, qkv_w, qkv_m, qkv_v,
    out_w, out_m, out_v, up_w, up_m, up_v, down_w, down_m, down_v, gains_w, gains_m, gains_v,
):
    length = token_ids.shape[1]
    slice_len, columns = embed_w.shape
    width = gains_w.shape[1]
    d, v = lax.axis_index("dp"), lax.axis_index("vocab")
    segment = segment_ids[0]

    turned_table = embed_w.astype(B16).T.reshape(2, columns // 2, slice_len)
    attention = jnp.concatenate([qkv_w, out_w], 1).astype(B16)[None]
    integers = jnp.concatenate(
        [token_ids, labels, loss_mask, jnp.broadcast_to(teacher_group[:, None], (1, length)),
         jnp.zeros((4, length), jnp.int32)], 0
    )[None]
    table, attention, up_t, down_t, pos_t, integers = ring_gather(
        D, V,
        [turned_table, attention, up_w.astype(B16)[None], down_w.astype(B16)[None], pos_w.astype(B16)[None], integers],
        ((0, 0, False, "dp", 0), (0, 1, False, "dp", 1), (5, 0, True, 2, 1), (1, 0, True, 0, 0), (2, 0, True, 1, 1),
         (3, 0, True, 2, 0), (4, 0, True, 1, 0)),
        1,
    )
    table = table.reshape(width, slice_len)
    attention = attention.reshape(width, -1)
    qkv_t, out_t = attention[:, : 3 * width], attention[:, 3 * width :]
    up_t, down_t, pos_t = up_t.reshape(width, -1), down_t.reshape(-1, width), pos_t.reshape(-1, width)
    weights = (qkv_t, out_t, up_t, down_t)
    integers = integers.reshape(D, V, 8, length)
    counted = jnp.maximum(jnp.sum(integers[:, :, 2].astype(F32)), 1.0)
    group_ints = lax.dynamic_index_in_dim(integers, d, 0, False)
    offset = v * slice_len
    ids_here = (group_ints[:, 0].reshape(-1, 1) - offset)
    labels_here = (group_ints[:, 1].reshape(-1, 1) - offset)
    counts = group_ints[:, 2].reshape(-1).astype(F32)
    groups = group_ints[:, 3, 0]

    picked = pick_rows(ids_here, table).astype(B16).reshape(V, length, width)
    embedded = vocab_scatter(V, picked, 2)
    places = positions(segment)
    onehot = (places[:, None] == jnp.arange(pos_t.shape[0], dtype=jnp.int32)[None, :]).astype(B16)
    hidden = embedded + jnp.dot(onehot, pos_t, preferred_element_type=F32)
    kept, h_two = layer_forward(hidden, segment, weights, gains_w)
    two_b = h_two.astype(B16)

    (hidden_all,) = vocab_gather(V, [two_b], 3)
    hidden_all = hidden_all.reshape(V * length, width)
    turned = hidden_all.T
    stats = lax.all_gather(student_stats(hidden_all, table), "vocab")
    top = jnp.max(stats[:, 0], 0)
    student_lse = top + jnp.log(jnp.sum(stats[:, 1] * jnp.exp(stats[:, 0] - top), 0))
    weight = counts / counted
    dh_student, grad_head, pick_lanes = student_grad(
        hidden_all, turned, table, student_lse[:, None], weight[:, None], labels_here
    )

    first = jnp.concatenate([teacher_qkv, teacher_out, teacher_up], 2)
    first, second = ring_gather(
        D, V, [first, teacher_down], tuple((q, r, True, r, q) for r in range(3) for q in range(2)), 4
    )
    mine = teacher_group[0]
    tw = teacher_qkv.shape[2] // 3
    first = lax.dynamic_index_in_dim(first, mine, 0, False).reshape(tw, -1)
    second = lax.dynamic_index_in_dim(second, mine, 0, False).reshape(-1, tw)
    chosen = (first[:, : 3 * tw], first[:, 3 * tw : 4 * tw], first[:, 4 * tw :], second)
    gains_row = lax.dynamic_index_in_dim(teacher_gains, mine, 0, False)
    _, teacher_top = layer_forward(teacher_inputs[0].astype(F32), segment, chosen, gains_row)
    (teacher_hidden,) = vocab_gather(V, [teacher_top.astype(B16)], 5)

    teacher, stats = teacher_stats(groups, teacher_hidden, teacher_table)
    stats = lax.all_gather(stats, "vocab")
    top = jnp.max(stats[:, 0], 0)
    scale = jnp.exp(stats[:, 0] - top)
    tsum = jnp.sum(stats[:, 1] * scale, 0)
    tcross = jnp.sum(stats[:, 2] * scale, 0) / tsum
    teacher_lse = top + jnp.log(tsum)
    dh_teacher, grad_head = teacher_grad(
        teacher, turned, table, teacher_lse[:, None], weight[:, None], grad_head
    )
    everywhere = jnp.sum(hidden_all.astype(F32) * dh_teacher) - jnp.sum(weight[:, None] * pick_lanes)
    once = jnp.sum(weight * (MIX_ALPHA * (tcross - teacher_lse + student_lse) + student_lse))
    loss_part = everywhere + jnp.where(v == 0, once, 0.0)

    dtwo = vocab_scatter(V, (dh_student + dh_teacher).astype(B16).reshape(V, length, width), 6)
    dhidden, dense_grads, grad_gains = layer_backward(dtwo, segment, weights, gains_w, kept)
    dhidden_b = dhidden.astype(B16)
    grad_pos = lax.dot_general(onehot, dhidden_b, (((0,), (0,)), ((), ())), preferred_element_type=F32)
    (turned_grads,) = vocab_gather(V, [dhidden_b.T], 7)
    grad_embed = spread_rows(ids_here, turned_grads, grad_head)

    grad_qkv, grad_out, grad_up, grad_down = dense_grads
    owners = lambda g: g.astype(B16).reshape(D * V // 2, 2, -1, g.shape[1])
    grad_embed = grad_embed.reshape(D, 2, columns // 2, slice_len)
    sums = ring_scatter(
        D, V,
        [grad_embed[:, 0], grad_embed[:, 1], owners(jnp.concatenate([grad_qkv, grad_out], 1)), owners(grad_up),
         owners(grad_down), owners(grad_pos)],
        (("dp", 0), ("dp", 1), (0, 0), (1, 1), (2, 0), (1, 0)),
        8,
    )
    grad_embed = jnp.concatenate(sums[:2], 0)
    owned = (sums[5], sums[2][:, : 3 * width], sums[2][:, 3 * width :], sums[3], sums[4])
    squares = jnp.sum(grad_embed * grad_embed)
    for grad in (sums[2], sums[3], sums[4], sums[5]):
        squares = squares + jnp.sum(grad * grad)
    lane = lax.broadcasted_iota(jnp.int32, (2, width), 1)
    scalars = jnp.where(lane == 0, squares, jnp.where(lane == 1, loss_part, 0.0))
    totals = total_all(D, V, jnp.concatenate([grad_gains, scalars], 0), 9)
    gains_grad, squares, loss = totals[:6], totals[6, 0], totals[6, 1]

    grad_norm = jnp.sqrt(squares + jnp.sum(gains_grad * gains_grad))
    factor = CLIP_NORM / jnp.maximum(grad_norm, CLIP_NORM)
    count_f = step_count.astype(F32)
    fix_one = 1.0 - jnp.power(BETA_ONE, count_f)
    fix_two = 1.0 - jnp.power(BETA_TWO, count_f)

    def update(weight, first, second, grad, rate):
        return adam(weight, first, second, grad * factor, fix_one, fix_two, rate)

    out = [loss, grad_norm]
    out += update(embed_w, embed_m, embed_v, grad_embed.T, LEARN_RATE)
    out += update(pos_w, pos_m, pos_v, owned[0], LEARN_RATE)
    out += update(qkv_w, qkv_m, qkv_v, owned[1], LEARN_RATE)
    out += update(out_w, out_m, out_v, owned[2], LEARN_RATE)
    out += update(up_w, up_m, up_v, owned[3], LEARN_RATE)
    out += update(down_w, down_m, down_v, owned[4], LEARN_RATE)
    out += update(gains_w, gains_m, gains_v, gains_grad, GAIN_RATE)
    return tuple(out)


def solution(mesh):
    rows, whole = P(("dp", "vocab"), None), P()
    split = P(None, ("dp", "vocab"), None)
    embed = P("vocab", "dp")
    return jax.shard_map(
        functools.partial(on_device, mesh.shape["dp"], mesh.shape["vocab"]),
        mesh=mesh,
        in_specs=(rows, rows, rows, rows, P(("dp", "vocab")), P(("dp", "vocab"), None, None), P(None, None, "vocab"),
                  split, split, split, split, whole, whole)
        + (embed,) * 3 + (rows,) * 15 + (whole,) * 3,
        out_specs=(whole, whole) + (embed,) * 3 + (rows,) * 15 + (whole,) * 3,
        check_vma=False,
    )
```

time: 1800 us -> 1010 us (0.56)
  waiting for transfers between devices: 919 us -> 0 us
  Pallas kernels: 0 us -> 753 us
  matrix products: 330 us -> 106 us
  blocking collectives: 192 us -> 12 us
  local copies, waits for them, and re-layouts: 178 us -> 56.3 us
  other arithmetic: 144 us -> 62.1 us
    pallas_call x0 -> x15, Pallas kernels: none -> 753 us  [the longest x2 272 us: ring_gather(): pl.pallas_call(functools.partial(gather_kernel, D, V, spec, len(arrays)),...]
    all_gather x11 -> x0, waiting for transfers between devices: 516 us -> none  [the longest x1 115 us: on_device(): lax.all_gather(embed_w.astype(jnp.bfloat16), 'dp', axis=1, tiled=True)]
    psum x1 -> x0, waiting for transfers between devices: 359 us -> none  [on_device(): lax.psum((grad_pos, grad_qkv, grad_out, grad_up, grad_down), ('dp', 'voca...]
    dot_general x40 -> x24, matrix products: 322 us -> 95.7 us  [the longest x1 14.3 us: attend_back(): jnp.einsum('hqk,qhd->khd', dscore, queries, preferred_element_type=F32)]
    all_gather x11 -> x2, blocking collectives: 126 us -> 12 us  [the longest x1 6.24 us: on_device(): stats = lax.all_gather(student_stats(hidden_all, table), 'vocab')]
    gather x9 -> x0, local copies, waits for them, and re-layouts: 81.3 us -> none  [the longest x7 67 us: on_device(): tables = jnp.take(teacher_table, chosen, axis=0)]
    psum x2 -> x0, blocking collectives: 60.9 us -> none  [the longest x1 40.4 us: on_device(): squares, gains_grad = lax.psum((squares, grad_gains), ('dp', 'vocab'))]
    unnamed x221 -> x142, local copies, waits for them, and re-layouts: 67.7 us -> 13.3 us
  transfers between devices with their start and end apart: 15 -> 0, of which waited for: 10 -> 0; matrix products, arithmetic and copies ran while one was open for 14% -> 0% of each run, Pallas kernels for 0% -> 0%
where the time goes in v1:
time: 1010 us; the launch traced here: 1000 us
  Pallas kernels  753 us (75%)
  matrix products  106 us (10%)
  other arithmetic  62.1 us (6%)
  local copies, waits for them, and re-layouts  56.3 us (6%)
  blocking collectives  12 us (1%)
  between operations  11.8 us (1%)
    pallas_call x2, Pallas kernels, ring_gather(): pl.pallas_call(functools.partial(gather_kernel, D, V, spec, len(arrays)),...  272 us
    pallas_call x1, Pallas kernels, ring_scatter(): pl.pallas_call(functools.partial(scatter_kernel, D, V, spec), out_shape=s...  113 us
    pallas_call x1, Pallas kernels, student_grad(): pl.pallas_call(functools.partial(student_grad_kernel, 512), grid=(size //...  68.5 us
    pallas_call x3, Pallas kernels, vocab_gather(): pl.pallas_call(functools.partial(vocab_gather_kernel, V, count), out_shap...  61.7 us
    pallas_call x1, Pallas kernels, teacher_grad(): pl.pallas_call(teacher_grad_kernel, grid=(size // tile,), out_shape=[jax....  48.9 us
    pallas_call x1, Pallas kernels, teacher_stats(): pl.pallas_call(teacher_stats_kernel, grid_spec=pltpu.PrefetchScalarGridSp...  48.4 us
    pallas_call x1, Pallas kernels, spread_rows(): pl.pallas_call(spread_kernel, grid=(size // tile,), out_shape=jax.ShapeDt...  37 us
    pallas_call x1, Pallas kernels, student_stats(): pl.pallas_call(functools.partial(student_stats_kernel, 256), grid=(size /...  34.7 us

profile of v1, /device:TPU:0, one launch (start us, length us, event | category | flops | bytes accessed | tf_op | source)
XLA Modules:
  0.0 1001.0 jit_solution(16717922567048175886)
XLA Ops:
  22.8 116.7 %shard_map.497 = (bf16[8,2,32,7680]{3,2,1,0:T(8,128)(2,1)}, bf16[1,32,16,2048]{3,2,1,0:T(8,128)(2,1)}, bf16[1,32,16,2048]{3,2,1,0:T(8,128)(2,1)}, bf16[1,32,64,5...) custom-call(bf16[2,32,7680]{2,1,0:T(8,128)(2,1)} %bitcast.221, ...), custom_call_target="tpu_custom_call" | custom-call | tf_op jit(solution)/shard_map/pallas_call | solution.py:215
  144.8 22.9 %shard_map.498 = f32[2048,512]{1,0:T(8,128)S(1)} custom-call(s32[2048,1]{1,0:T(8,128)S(1)} %bitcast.201, bf16[512,7680]{1,0:T(8,128)(2,1)} %bitcast.205), custom_call_target="tpu_custom_call" | custom-call | tf_op jit(solution)/shard_map/pallas_call | solution.py:810
  168.0 17.1 %shard_map.499 = f32[512,512]{1,0:T(8,128)S(1)} custom-call(bf16[2,2,512,512]{3,2,1,0:T(8,128)(2,1)S(1)} %bitcast.204), custom_call_target="tpu_custom_call" | custom-call | tf_op jit(solution)/shard_map/pallas_call | solution.py:489
  204.7 17.6 %shard_map.500 = bf16[4,512,512]{2,1,0:T(8,128)(2,1)} custom-call(bf16[512,512]{1,0:T(8,128)(2,1)} %copy.166.refs_0_), custom_call_target="tpu_custom_call" | custom-call | tf_op jit(solution)/shard_map/pallas_call | solution.py:428
  223.9 34.7 %shard_map.501 = f32[8,2048]{1,0:T(8,128)S(1)} custom-call(bf16[2048,512]{1,0:T(8,128)(2,1)S(1)} %bitcast.199, bf16[512,7680]{1,0:T(8,128)(2,1)} %bitcast.206), custom_call_target="tpu_custom_call" | custom-call | tf_op jit(solution)/shard_map/pallas_call | solution.py:612
  258.6 6.2 all-gather
  267.3 155.6 %shard_map.503 = (bf16[3,32,24,6144]{3,2,1,0:T(8,128)(2,1)}, bf16[3,32,96,768]{3,2,1,0:T(8,128)(2,1)}) custom-call(bf16[3,24,6144]{2,1,0:T(8,128)(2,1)} %pad_maximum_fusion.2.refs_0_, bf16[3,96,768]{2,1,0:T(8,128)(2,1)} %refs_1_.1), custom_call_target="tpu_custom_call" | custom-call | tf_op jit(solution)/shard_map/pallas_call | solution.py:215
  422.9 8.6 constant_dynamic-slice_fusion.1
  442.4 10.4 %fusion.187 = (f32[12,512]{1,0:T(8,128)S(1)}, f32[12,512,512]{1,2,0:T(8,128)}) fusion(pred[512,512]{0,1:T(8,128)(4,1)} %copy-done.18, bf16[512,12,64]{0,2,1:T(8,128)(2,1)S(1)} %bitcast.238, bf16[512,12,64]{0,2,1:T(8,128)(2,1)} %bitcast.236), kind=kOutput, calls=%fused_computation.284 | convolution fusion | flops 415236608 | bytes 14442496 | tf_op jit(solution)/shard_map/sub | solution.py:904
  452.9 5.9 fusion.72
  462.3 10.3 %fusion.189 = (f32[512]{0:T(512)S(1)}, f32[512,768]{1,0:T(8,128)S(1)}) fusion(bf16[3072,768]{1,0:T(8,128)(2,1)} %bitcast.219, bf16[768,6144]{1,0:T(8,128)(2,1)} %bitcast.218, f32[512,768]{1,0:T(8,128)} %copy-done.30, f32[768]{0:T(1024)S(1)} %get-tuple-element.77, f32[768]{0:T(1024)S(1)} %copy-done.52, f32[512]{0:T(512)S(1)} %add_rsqrt_fusion.1, ...), kind=kOutput, calls=%fused_computation.286 | convolution fusion | flops 4850318848 | bytes 14182400 | tf_op jit(solution)/shard_map/dot_general | solution.py:940
  474.1 26.1 %shard_map.504.hidden_ref = bf16[4,512,768]{2,1,0:T(8,128)(2,1)} custom-call(bf16[512,768]{1,0:T(8,128)(2,1)} %add_convert_fusion.1.refs_0_), custom_call_target="tpu_custom_call" | custom-call | tf_op jit(solution)/shard_map/pallas_call | solution.py:428
  502.1 48.4 %shard_map.505 = (bf16[4,512,7680]{2,1,0:T(8,128)(2,1)}, f32[8,2048]{1,0:T(8,128)S(1)}) custom-call(s32[4]{0:T(128)S(1)} %slice_reduce_fusion.group_ref, bf16[4,512,768]{2,1,0:T(8,128)(2,1)S(1)} %copy-done.2, bf16[3,768,7680]{2,1,0:T(8,128)(2,1)} %table_ref.1), custom_call_target="tpu_custom_call" | custom-call | tf_op jit(solution)/shard_map/pallas_call | solution.py:718
  550.5 5.8 all-gather.1
  563.0 68.5 %shard_map.502 = (f32[2048,512]{1,0:T(8,128)}, f32[512,7680]{1,0:T(8,128)}, f32[2048,128]{1,0:T(8,128)}) custom-call(bf16[2048,512]{1,0:T(8,128)(2,1)} %bitcast.198, bf16[512,2048]{1,0:T(8,128)(2,1)} %bitcast.211, bf16[512,7680]{1,0:T(8,128)(2,1)} %bitcast.207, f32[2048,1]{1,0:T(8,128)} %copy.171.lse_ref, f32[2048,1]{1,0:T(8,128)} %bitcast.214, ...), custom_call_target="tpu_custom_call" | custom-call | tf_op jit(solution)/shard_map/pallas_call | solution.py:662
  633.6 48.9 %shard_map.506 = (f32[2048,512]{1,0:T(8,128)}, f32[512,7680]{1,0:T(8,128)}) custom-call(bf16[4,512,7680]{2,1,0:T(8,128)(2,1)} %get-tuple-element.53.teacher_ref, bf16[512,2048]{1,0:T(8,128)(2,1)} %bitcast.212, bf16[512,7680]{1,0:T(8,128)(2,1)} %bitcast.208, f32[2048,1]{1,0:T(8,128)} %copy.180.lse_ref, f32[2048,1]{1,0:T(8,128)} %bitcast.215, ...), custom_call_target="tpu_custom_call" | custom-call | tf_op jit(solution)/shard_map/pallas_call | solution.py:769
  686.8 17.1 %shard_map.507 = f32[512,512]{1,0:T(8,128)S(1)} custom-call(bf16[2,2,512,512]{3,2,1,0:T(8,128)(2,1)S(1)} %bitcast.203), custom_call_target="tpu_custom_call" | custom-call | tf_op jit(solution)/shard_map/pallas_call | solution.py:489
  738.5 5.9 fusion.194
  744.3 14.3 %fusion.85 = bf16[8,64,512]{2,1,0:T(8,128)(2,1)} fusion(bf16[512,8,64]{0,2,1:T(8,128)(2,1)S(1)} %bitcast.227, f32[8,512,512]{1,2,0:T(8,128)} %fusion.194, f32[8,512,512]{1,2,0:T(8,128)} %copy-done.6, f32[8,512]{1,0:T(8,128)S(1)} %log_add_fusion, pred[512,512]{0,1:T(8,128)(4,1)S(1)} %copy-done.19), kind=kOutput, calls=%fused_computation.100 | convolution fusion | flops 291770880 | bytes 18104320 | tf_op jit(solution)/shard_map/hqk,khd->qhd/dot_general | solution.py:920
  758.6 14.3 %fusion.88 = bf16[8,64,512]{2,1,0:T(8,128)(2,1)} fusion(bf16[512,8,64]{0,2,1:T(8,128)(2,1)S(1)} %bitcast.225, f32[8,512,512]{1,2,0:T(8,128)} %fusion.194, f32[8,512,512]{1,2,0:T(8,128)} %copy-done.6, f32[8,512]{1,0:T(8,128)S(1)} %log_add_fusion, pred[512,512]{0,1:T(8,128)(4,1)S(1)} %copy-done.19), kind=kOutput, calls=%fused_computation.101 | convolution fusion | flops 291770880 | bytes 18104320 | tf_op jit(solution)/shard_map/hqk,qhd->khd/dot_general | solution.py:921
  781.1 18.0 %shard_map.508.turned_ref = bf16[4,512,512]{2,1,0:T(8,128)(2,1)} custom-call(bf16[512,512]{1,0:T(8,128)(2,1)} %bitcast.232), custom_call_target="tpu_custom_call" | custom-call | tf_op jit(solution)/shard_map/pallas_call | solution.py:428
  800.7 37.0 %shard_map.509 = bf16[512,7680]{1,0:T(8,128)(2,1)} custom-call(s32[2048,1]{1,0:T(8,128)S(1)} %bitcast.202, bf16[4,512,512]{2,1,0:T(8,128)(2,1)S(1)} %copy-done.5, f32[512,7680]{1,0:T(8,128)} %get-tuple-element.57.grad_ref), custom_call_target="tpu_custom_call" | custom-call | tf_op jit(solution)/shard_map/pallas_call | solution.py:841
  843.2 113.2 %shard_map.510 = (f32[32,7680]{1,0:T(8,128)}, f32[32,7680]{1,0:T(8,128)}, f32[16,2048]{1,0:T(8,128)}, f32[16,2048]{1,0:T(8,128)}, f32[64,512]{1,0:T(8,128)}, /*index=5*/f32[16,512]{1,0:T(8,128)}) custom-call(bf16[8,32,7680]{2,1,0:T(8,128)(2,1)} %get-tuple-element.106.refs_0_, bf16[8,32,7680]{2,1,0:T(8,128)(2,1)} %get-tuple-element.105.refs_1_, ...), custom_call_target="tpu_custom_call" | custom-call | tf_op jit(solution)/shard_map/pallas_call | solution.py:359
  972.4 10.7 %shard_map.511 = f32[8,512]{1,0:T(8,128)} custom-call(f32[8,512]{1,0:T(8,128)} %concatenate.47.in_ref), custom_call_target="tpu_custom_call" | custom-call | tf_op jit(solution)/shard_map/pallas_call | solution.py:544
  (267 shorter events, 154.9 us)
Async XLA Ops:
  0.7 21.1 %copy-start.12 = (f32[7680,64]{0,1:T(8,128)S(1)}, f32[7680,64]{0,1:T(8,128)}, u32[]{:S(2)}) copy-start(f32[7680,64]{0,1:T(8,128)} %param.47) | copy-start | bytes 5898244
  4.3 181.2 %copy-start.50 = (s32[512]{0:T(512)}, s32[512]{0:T(512)S(1)}, u32[]{:S(2)}) copy-start(s32[512]{0:T(512)S(1)} %iota_subtract_fusion) | copy-start | bytes 6148
  10.0 187.4 %copy-start.57 = (f32[1,512]{1,0:T(1,128)}, f32[1,512]{1,0:T(1,128)S(1)}, u32[]{:S(2)}) copy-start(f32[1,512]{1,0:T(1,128)S(1)} %get-tuple-element.132) | copy-start | bytes 6148
  19.5 173.7 %copy-start.18 = (pred[512,512]{0,1:T(8,128)(4,1)}, pred[512,512]{0,1:T(8,128)(4,1)S(1)}, u32[]{:S(2)}) copy-start(pred[512,512]{0,1:T(8,128)(4,1)S(1)} %broadcast_compare_fusion) | copy-start | bytes 786436
  143.4 24.3 %copy-start.3 = (s32[1,2048]{0,1:T(8,128)}, s32[1,2048]{0,1:T(8,128)S(1)}, u32[]{:S(2)}) copy-start(s32[1,2048]{0,1:T(8,128)S(1)} %copy.214) | copy-start | bytes 24580
  168.0 17.5 %copy-start.31 = (bf16[1,32,16,512]{3,2,1,0:T(8,128)(2,1)S(1)}, bf16[1,32,16,512]{3,2,1,0:T(8,128)(2,1)}, u32[]{:S(2)}) copy-start(bf16[1,32,16,512]{3,2,1,0:T(8,128)(2,1)} %get-tuple-element.46) | copy-start | bytes 1572868
  223.9 40.9 %copy-start.1 = (bf16[4,512,512]{2,1,0:T(8,128)(2,1)S(1)}, bf16[4,512,512]{2,1,0:T(8,128)(2,1)}, u32[]{:S(2)}) copy-start(bf16[4,512,512]{2,1,0:T(8,128)(2,1)} %shard_map.500) | copy-start | bytes 6291460
  779.3 19.8 %copy-start.4 = (s32[1,2048]{0,1:T(8,128)S(1)}, s32[1,2048]{0,1:T(8,128)}, u32[]{:S(2)}) copy-start(s32[1,2048]{0,1:T(8,128)} %copy-done.3) | copy-start | bytes 24580
  956.4 30.7 %copy-start.49 = (f32[6,512]{1,0:T(8,128)S(1)}, f32[6,512]{1,0:T(8,128)}, u32[]{:S(2)}) copy-start(f32[6,512]{1,0:T(8,128)} %param.65) | copy-start | bytes 36868
  956.4 32.2 %copy-start.40 = (f32[16,512]{1,0:T(8,128)S(1)}, f32[16,512]{1,0:T(8,128)}, u32[]{:S(2)}) copy-start(f32[16,512]{1,0:T(8,128)} %param.50) | copy-start | bytes 98308
  956.4 32.2 %copy-start.42 = (f32[16,512]{1,0:T(8,128)S(1)}, f32[16,512]{1,0:T(8,128)}, u32[]{:S(2)}) copy-start(f32[16,512]{1,0:T(8,128)} %get-tuple-element.63) | copy-start | bytes 98308
  956.5 33.6 %copy-start.32 = (f32[16,2048]{1,0:T(8,128)S(1)}, f32[16,2048]{1,0:T(8,128)}, u32[]{:S(2)}) copy-start(f32[16,2048]{1,0:T(8,128)} %get-tuple-element.60) | copy-start | bytes 393220
  956.5 33.6 %copy-start.41 = (f32[16,512]{1,0:T(8,128)S(1)}, f32[16,512]{1,0:T(8,128)}, u32[]{:S(2)}) copy-start(f32[16,512]{1,0:T(8,128)} %param.56) | copy-start | bytes 98308
  956.5 35.0 %copy-start.39 = (f32[16,1536]{1,0:T(8,128)S(1)}, f32[16,1536]{1,0:T(8,128)}, u32[]{:S(2)}) copy-start(f32[16,1536]{1,0:T(8,128)} %param.53) | copy-start | bytes 294916
  956.5 35.0 %copy-start.47 = (f32[16,1536]{1,0:T(8,128)S(1)}, f32[16,1536]{1,0:T(8,128)}, u32[]{:S(2)}) copy-start(f32[16,1536]{1,0:T(8,128)} %param.55) | copy-start | bytes 294916
  956.5 35.0 %copy-start.48 = (f32[16,1536]{1,0:T(8,128)S(1)}, f32[16,1536]{1,0:T(8,128)}, u32[]{:S(2)}) copy-start(f32[16,1536]{1,0:T(8,128)} %param.54) | copy-start | bytes 294916
  956.5 35.8 %copy-start.33 = (f32[16,2048]{1,0:T(8,128)S(1)}, f32[16,2048]{1,0:T(8,128)}, u32[]{:S(2)}) copy-start(f32[16,2048]{1,0:T(8,128)} %param.59) | copy-start | bytes 393220
  956.5 35.8 %copy-start.36 = (f32[16,2048]{1,0:T(8,128)S(1)}, f32[16,2048]{1,0:T(8,128)}, u32[]{:S(2)}) copy-start(f32[16,2048]{1,0:T(8,128)} %get-tuple-element.61) | copy-start | bytes 393220
  956.5 35.8 %copy-start.43 = (f32[16,2048]{1,0:T(8,128)S(1)}, f32[16,2048]{1,0:T(8,128)}, u32[]{:S(2)}) copy-start(f32[16,2048]{1,0:T(8,128)} %param.61) | copy-start | bytes 393220
  956.5 35.7 %copy-start.44 = (f32[16,2048]{1,0:T(8,128)S(1)}, f32[16,2048]{1,0:T(8,128)}, u32[]{:S(2)}) copy-start(f32[16,2048]{1,0:T(8,128)} %param.60) | copy-start | bytes 393220
  961.2 31.9 %copy-start.34 = (f32[64,512]{1,0:T(8,128)S(1)}, f32[64,512]{1,0:T(8,128)}, u32[]{:S(2)}) copy-start(f32[64,512]{1,0:T(8,128)} %param.62) | copy-start | bytes 393220
  961.2 31.9 %copy-start.35 = (f32[64,512]{1,0:T(8,128)S(1)}, f32[64,512]{1,0:T(8,128)}, u32[]{:S(2)}) copy-start(f32[64,512]{1,0:T(8,128)} %get-tuple-element.62) | copy-start | bytes 393220
  961.2 31.9 %copy-start.45 = (f32[64,512]{1,0:T(8,128)S(1)}, f32[64,512]{1,0:T(8,128)}, u32[]{:S(2)}) copy-start(f32[64,512]{1,0:T(8,128)} %param.64) | copy-start | bytes 393220
  961.2 31.9 %copy-start.46 = (f32[64,512]{1,0:T(8,128)S(1)}, f32[64,512]{1,0:T(8,128)}, u32[]{:S(2)}) copy-start(f32[64,512]{1,0:T(8,128)} %param.63) | copy-start | bytes 393220
  (43 other events, 194.5 us)

commit v2 on v1

--- a/solution.py
+++ b/solution.py
@@ -92,117 +92,129 @@
         pl.when(condition)(body)
 
 
-def gather_kernel(D, V, spec, count, *refs):
-    ins, outs = refs[:count], refs[count : 2 * count]
-    ssem, rsem, xssem, xrsem, lsem = refs[2 * count :]
-    rings = {w: Ring(D, V, w) for w in dict.fromkeys(p[3] for p in spec)}
-    core = lax.rem(lax.axis_index("vocab"), 2)
-    sib = sibling()
-    nexts = {w: (r.at(1), r.at(-1)) for w, r in rings.items()}
-    both = any(p[3] != "dp" for p in spec)
-    greet(
-        [r.device(place) for w, r in rings.items() for place in nexts[w]]
-        + ([sib] if both else [])
-    )
-
-    def dst(piece, slot):
+class Gather:
+    def __init__(self, D, V, spec, ins, outs, sems):
+        self.spec, self.ins, self.outs = spec, ins, outs
+        self.ssem, self.rsem, self.xssem, self.xrsem, self.lsem = sems
+        rings = {w: Ring(D, V, w) for w in dict.fromkeys(p[3] for p in spec)}
+        self.core = lax.rem(lax.axis_index("vocab"), 2)
+        self.sib = sibling()
+        self.nexts = {w: (r.at(1), r.at(-1)) for w, r in rings.items()}
+        self.neighbours = [r.device(place) for w, r in rings.items() for place in self.nexts[w]]
+        if any(p[3] != "dp" for p in spec):
+            self.neighbours.append(self.sib)
+        self.streams = []
+        for number, piece in enumerate(spec):
+            ring = rings[piece[3]]
+            for turn, hops in zip((0, 1), ring.hops(piece[4])):
+                self.streams.append((piece, ring, turn, hops, number))
+        self.longest = max(s[3] for s in self.streams)
+
+    def dst(self, piece, slot):
         which, k, lead, _, _ = piece
-        return outs[which].at[k, slot] if lead else outs[which].at[slot, k]
-
-    def slot_of(ring, place):
-        return place if ring.over_dp else place * 2 + core
-
-    streams = []
-    for number, piece in enumerate(spec):
-        ring = rings[piece[3]]
-        for turn, hops in zip((0, 1), ring.hops(piece[4])):
-            streams.append((piece, ring, turn, hops, number))
-
-    def origin(stream, s):
+        return self.outs[which].at[k, slot] if lead else self.outs[which].at[slot, k]
+
+    def slot_of(self, ring, place):
+        return place if ring.over_dp else place * 2 + self.core
+
+    def origin(self, stream, s):
         _, ring, turn, _, _ = stream
-        return slot_of(ring, ring.at(-s) if turn == 0 else ring.at(s))
-
-    def remote(i, s, src, slot):
-        piece, ring, turn, _, _ = streams[i]
+        return self.slot_of(ring, ring.at(-s) if turn == 0 else ring.at(s))
+
+    def remote(self, i, s, src, slot):
+        piece, ring, turn, _, _ = self.streams[i]
         return pltpu.make_async_remote_copy(
             src_ref=src,
-            dst_ref=dst(piece, slot),
-            send_sem=ssem.at[s, i],
-            recv_sem=rsem.at[s, i],
-            device_id=ring.device(nexts[piece[3]][turn]),
+            dst_ref=self.dst(piece, slot),
+            send_sem=self.ssem.at[s, i],
+            recv_sem=self.rsem.at[s, i],
+            device_id=ring.device(self.nexts[piece[3]][turn]),
             device_id_type=MESH,
         )
 
-    def across(i, s, src, slot):
+    def across(self, i, s, src, slot):
         return pltpu.make_async_remote_copy(
             src_ref=src,
-            dst_ref=dst(streams[i][0], slot),
-            send_sem=xssem.at[s, i],
-            recv_sem=xrsem.at[s, i],
-            device_id=sib,
+            dst_ref=self.dst(self.streams[i][0], slot),
+            send_sem=self.xssem.at[s, i],
+            recv_sem=self.xrsem.at[s, i],
+            device_id=self.sib,
             device_id_type=MESH,
         )
 
-    def own(i):
-        piece, ring, _, _, _ = streams[i]
-        return ins[piece[0]].at[piece[1]], slot_of(ring, ring.me)
-
-    for i in range(len(streams)):
-        remote(i, 0, *own(i)).start()
-    for i, stream in enumerate(streams):
-        if stream[2] == 0:
-            src, slot = own(i)
-            pltpu.make_async_copy(src, dst(stream[0], slot), lsem.at[stream[4]]).start()
-            if not stream[1].over_dp:
-                across(i, 0, src, slot).start()
-    longest = max(s[3] for s in streams)
-
-    def within(s, hops):
-        return True if hops == longest else s <= hops
-
-    def body(s, carry):
-        for i, stream in enumerate(streams):
+    def own(self, i):
+        piece, ring, _, _, _ = self.streams[i]
+        return self.ins[piece[0]].at[piece[1]], self.slot_of(ring, ring.me)
+
+    def begin(self):
+        for i in range(len(self.streams)):
+            self.remote(i, 0, *self.own(i)).start()
+        for i, stream in enumerate(self.streams):
+            if stream[2] == 0:
+                src, slot = self.own(i)
+                pltpu.make_async_copy(src, self.dst(stream[0], slot), self.lsem.at[stream[4]]).start()
+                if not stream[1].over_dp:
+                    self.across(i, 0, src, slot).start()
+
+    def within(self, s, hops):
+        return True if hops == self.longest else s <= hops
+
+    def serve(self, s):
+        for i, stream in enumerate(self.streams):
 
             def take(i=i, stream=stream):
-                slot = origin(stream, s)
-                block = dst(stream[0], slot)
-                remote(i, s - 1, block, slot).wait_recv()
-                pl.when(s < stream[3])(lambda: remote(i, s, block, slot).start())
+                slot = self.origin(stream, s)
+                block = self.dst(stream[0], slot)
+                self.remote(i, s - 1, block, slot).wait_recv()
+                pl.when(s < stream[3])(lambda: self.remote(i, s, block, slot).start())
                 if not stream[1].over_dp:
-                    across(i, s, block, slot).start()
-
-            on_condition(within(s, stream[3]), take)
-        return carry
-
-    lax.fori_loop(1, longest + 1, body, 0)
-
-    def finish(s, carry):
-        for i, stream in enumerate(streams):
-
-            def end(i=i, stream=stream):
-                slot = origin(stream, s)
-                block = dst(stream[0], slot)
-                pl.when(s < stream[3])(lambda: remote(i, s, block, slot).wait_send())
-                if not stream[1].over_dp:
-
-                    def crossed():
-                        across(i, s, block, slot).wait_send()
-                        theirs = slot + 1 - 2 * core
-                        across(i, s, block, theirs).wait_recv()
-
-                    on_condition(True if stream[2] == 0 else s > 0, crossed)
-
-            on_condition(within(s, stream[3]), end)
-        return carry
-
-    lax.fori_loop(0, longest + 1, finish, 0)
-    for i, stream in enumerate(streams):
-        if stream[2] == 0:
-            src, slot = own(i)
-            pltpu.make_async_copy(src, dst(stream[0], slot), lsem.at[stream[4]]).wait()
-
-
-def ring_gather(D, V, arrays, spec, ident):
+                    self.across(i, s, block, slot).start()
+
+            on_condition(self.within(s, stream[3]), take)
+
+    def serve_range(self, low, high):
+        def body(s, carry):
+            self.serve(s)
+            return carry
+
+        lax.fori_loop(low, high, body, 0)
+
+    def finish(self):
+        def last(s, carry):
+            for i, stream in enumerate(self.streams):
+
+                def end(i=i, stream=stream):
+                    slot = self.origin(stream, s)
+                    block = self.dst(stream[0], slot)
+                    pl.when(s < stream[3])(lambda: self.remote(i, s, block, slot).wait_send())
+                    if not stream[1].over_dp:
+
+                        def crossed():
+                            self.across(i, s, block, slot).wait_send()
+                            theirs = slot + 1 - 2 * self.core
+                            self.across(i, s, block, theirs).wait_recv()
+
+                        on_condition(True if stream[2] == 0 else s > 0, crossed)
+
+                on_condition(self.within(s, stream[3]), end)
+            return carry
+
+        lax.fori_loop(0, self.longest + 1, last, 0)
+        for i, stream in enumerate(self.streams):
+            if stream[2] == 0:
+                src, slot = self.own(i)
+                pltpu.make_async_copy(src, self.dst(stream[0], slot), self.lsem.at[stream[4]]).wait()
+
+
+def gather_kernel(D, V, spec, count, *refs):
+    gather = Gather(D, V, spec, refs[:count], refs[count : 2 * count], refs[2 * count :])
+    greet(gather.neighbours)
+    gather.begin()
+    gather.serve_range(1, gather.longest + 1)
+    gather.finish()
+
+
+def gather_plan(D, V, arrays, spec):
     shapes = []
     for which, array in enumerate(arrays):
         piece = next(p for p in spec if p[0] == which)
@@ -212,12 +224,17 @@
         shapes.append(jax.ShapeDtypeStruct(shape + array.shape[1:], array.dtype))
     longest = max((D if p[3] == "dp" else D * V // 2) // 2 for p in spec) + 1
     sems = pltpu.SemaphoreType.DMA((longest, 2 * len(spec)))
+    return shapes, [sems] * 4 + [pltpu.SemaphoreType.DMA((len(spec),))]
+
+
+def ring_gather(D, V, arrays, spec, ident):
+    shapes, sems = gather_plan(D, V, arrays, spec)
     return pl.pallas_call(
         functools.partial(gather_kernel, D, V, spec, len(arrays)),
         out_shape=shapes,
         in_specs=[ANYWHERE] * len(arrays),
         out_specs=[ANYWHERE] * len(arrays),
-        scratch_shapes=[sems] * 4 + [pltpu.SemaphoreType.DMA((len(spec),))],
+        scratch_shapes=sems,
         compiler_params=pltpu.CompilerParams(collective_id=ident, has_side_effects=True),
     )(*arrays)
 
@@ -551,8 +568,8 @@
     )(array)
 
 
-def tile_of(size):
-    return next(t for t in (1280, 768, 512, 256, 128) if size % t == 0)
+def tile_of(size, tokens=1):
+    return next(t for t in (1280, 768, 640, 512, 256, 128) if size % t == 0 and (t * tokens <= 1280 * 2048 or t == 128))
 
 
 def lane_fold(values, combine):
@@ -582,106 +599,160 @@
     return packed.T[:8]
 
 
-def student_stats_kernel(block, hidden_ref, table_ref, out_ref, top_ref, sum_ref):
-    step = pl.program_id(0)
-
-    @pl.when(step == 0)
-    def _():
-        top_ref[...] = jnp.full(top_ref.shape, -jnp.inf, F32)
-        sum_ref[...] = jnp.zeros(sum_ref.shape, F32)
-
-    def one(k, carry):
-        rows = pl.ds(pl.multiple_of(k * block, block), block)
-        logits = jnp.dot(hidden_ref[rows, :], table_ref[...], preferred_element_type=F32)
-        running(logits, top_ref, sum_ref, rows)
+def study_kernel(D, V, spec, *refs):
+    first_ref, second_ref, own_ref, table_ref, given_ref = refs[:5]
+    first_out, second_out, hidden_ref, turned_out, dh_ref, grad_ref, rows_out = refs[5:12]
+    top_ref, sum_ref, dl_ref, slots, hs, hr, xs, xr, ps, pr = refs[12:22]
+    gather = Gather(D, V, spec, (first_ref, second_ref), (first_out, second_out), refs[22:])
+    d, v = lax.axis_index("dp"), lax.axis_index("vocab")
+    half = V // 2
+    core, chip = lax.rem(v, 2), v // 2
+    length, width = own_ref.shape
+    tokens, size = V * length, table_ref.shape[1]
+    tile, block = tile_of(size, tokens), min(256, length)
+    tiles, blocks = size // tile, tokens // block
+    peers = [(d, lax.rem(v + k, V)) for k in range(1, V)]
+    greet(gather.neighbours + peers)
+
+    def other(k):
+        return lax.rem(chip + k + half, half) * 2 + core
+
+    def place(slot):
+        return hidden_ref.at[pl.ds(pl.multiple_of(slot * length, length), length)]
+
+    def send(k):
+        return pltpu.make_async_remote_copy(
+            src_ref=own_ref, dst_ref=place(v), send_sem=hs.at[k], recv_sem=hr.at[k],
+            device_id=(d, other(k)), device_id_type=MESH,
+        )
+
+    def across(k, src, slot):
+        return pltpu.make_async_remote_copy(
+            src_ref=src, dst_ref=place(slot), send_sem=xs.at[k], recv_sem=xr.at[k],
+            device_id=sibling(), device_id_type=MESH,
+        )
+
+    for k in range(1, half):
+        send(k).start()
+    across(0, own_ref, v).start()
+    gather.begin()
+    place(v)[...] = own_ref[...]
+    top_ref[...] = jnp.full(top_ref.shape, -jnp.inf, F32)
+    sum_ref[...] = jnp.zeros(sum_ref.shape, F32)
+    dh_ref[...] = jnp.zeros(dh_ref.shape, F32)
+    for k in range(1, half):
+        slot = other(-k)
+        send(k).wait_recv()
+        across(k, place(slot), slot).start()
+    for k in range(half):
+        across(k, place(other(-k)), other(-k) + 1 - 2 * core).wait_recv()
+
+    def columns(t):
+        return pl.ds(pl.multiple_of(t * tile, tile), tile)
+
+    early = max(1, gather.longest // 4)
+    late = gather.longest - early
+
+    def pass_one(t, carry):
+        for k in range(blocks):
+            rows = slice(k * block, (k + 1) * block)
+            logits = jnp.dot(hidden_ref[rows, :], table_ref[:, columns(t)], preferred_element_type=F32)
+            running(logits, top_ref, sum_ref, rows)
+        gather.serve_range(1 + t * early // tiles, 1 + (t + 1) * early // tiles)
         return carry
 
-    lax.fori_loop(0, hidden_ref.shape[0] // block, one, 0)
-
-    @pl.when(step == pl.num_programs(0) - 1)
-    def _():
-        top = jnp.max(top_ref[...], 1, keepdims=True)
-        total = jnp.sum(sum_ref[...] * jnp.exp(top_ref[...] - top), 1, keepdims=True)
-        out_ref[...] = pack_rows([top, total])
-
-
-def student_stats(hidden, table):
-    tokens, width = hidden.shape
-    size = table.shape[1]
-    tile = tile_of(size)
+    lax.fori_loop(0, tiles, pass_one, 0)
+    top = jnp.max(top_ref[...], 1, keepdims=True)
+    total = jnp.sum(sum_ref[...] * jnp.exp(top_ref[...] - top), 1, keepdims=True)
+    slots[v] = pack_rows([top, total])
+
+    def tell(k):
+        return pltpu.make_async_remote_copy(
+            src_ref=slots.at[v], dst_ref=slots.at[v], send_sem=ps.at[k], recv_sem=pr.at[k],
+            device_id=peers[k], device_id_type=MESH,
+        )
+
+    for k in range(V - 1):
+        tell(k).start()
+    for q in range(tokens // length):
+        rows = slice(q * length, (q + 1) * length)
+        turned_out[:, rows] = hidden_ref[rows, :].T
+    for k in range(V - 1):
+        tell(k).wait_recv()
+    top = slots[0, 0:1, :]
+    for k in range(1, V):
+        top = jnp.maximum(top, slots[k, 0:1, :])
+    total = jnp.zeros(top.shape, F32)
+    for k in range(V):
+        total = total + slots[k, 1:2, :] * jnp.exp(slots[k, 0:1, :] - top)
+    lse = top + jnp.log(total)
+    rows_out[...] = jnp.broadcast_to(lse, rows_out.shape)
+    lse_ref, pick_ref = top_ref, sum_ref
+    lse_ref[...] = jnp.broadcast_to(lse, (128, tokens)).T
+    pick_ref[...] = jnp.zeros(pick_ref.shape, F32)
+
+    def pass_two(t, carry):
+        for k in range(blocks):
+            rows = slice(k * block, (k + 1) * block)
+            logits = jnp.dot(hidden_ref[rows, :], table_ref[:, columns(t)], preferred_element_type=F32)
+            weight = given_ref[rows, 0:1]
+            soft = jnp.exp(logits - lse_ref[rows, :1]) * ((1.0 + MIX_ALPHA) * weight)
+            lane = lax.broadcasted_iota(jnp.int32, logits.shape, 1)
+            hit = lane == given_ref[rows, 1:2].astype(jnp.int32) - t * tile
+            dl_ref[rows, :] = jnp.where(hit, soft - weight, soft).astype(B16)
+            pick_ref[rows, :] += lane_fold(jnp.where(hit, logits, 0.0), jnp.add)
+        for k in range(tokens // length):
+            rows = slice(k * length, (k + 1) * length)
+            dh_ref[rows, :] += lax.dot_general(
+                dl_ref[rows, :], table_ref[:, columns(t)], (((1,), (1,)), ((), ())), preferred_element_type=F32
+            )
+        grad_ref[:, columns(t)] = jnp.dot(
+            turned_out[...], dl_ref[...], preferred_element_type=F32
+        ).astype(B16)
+        gather.serve_range(1 + early + t * late // tiles, 1 + early + (t + 1) * late // tiles)
+        return carry
+
+    lax.fori_loop(0, tiles, pass_two, 0)
+    picks = pack_rows([jnp.sum(pick_ref[...], 1, keepdims=True)])
+    rows_out[1:2, :] = picks[0:1]
+    for k in range(1, half):
+        send(k).wait_send()
+    for k in range(half):
+        across(k, place(other(-k)), other(-k)).wait_send()
+    for k in range(V - 1):
+        tell(k).wait_send()
+    gather.finish()
+
+
+def study(D, V, first, second, own, table, given, ident):
+    spec = tuple((q, r, True, r, q) for r in range(3) for q in range(2))
+    shapes, sems = gather_plan(D, V, [first, second], spec)
+    length, width = own.shape
+    tokens, size = V * length, table.shape[1]
+    tile = tile_of(size, tokens)
+    halves, singles = pltpu.SemaphoreType.DMA((V // 2,)), pltpu.SemaphoreType.DMA((V,))
+    column = pltpu.VMEM((tokens, 128), F32)
     return pl.pallas_call(
-        functools.partial(student_stats_kernel, 256),
-        grid=(size // tile,),
-        out_shape=jax.ShapeDtypeStruct((8, tokens), F32),
-        in_specs=[
-            pl.BlockSpec((tokens, width), lambda j: (0, 0)),
-            pl.BlockSpec((width, tile), lambda j: (0, j)),
+        functools.partial(study_kernel, D, V, spec),
+        out_shape=shapes
+        + [
+            jax.ShapeDtypeStruct((tokens, width), B16),
+            jax.ShapeDtypeStruct((width, tokens), B16),
+            jax.ShapeDtypeStruct((tokens, width), F32),
+            jax.ShapeDtypeStruct((width, size), B16),
+            jax.ShapeDtypeStruct((8, tokens), F32),
         ],
-        out_specs=pl.BlockSpec((8, tokens), lambda j: (0, 0)),
-        scratch_shapes=[pltpu.VMEM((tokens, 128), F32)] * 2,
-        compiler_params=pltpu.CompilerParams(vmem_limit_bytes=48 * MIB),
-    )(hidden, table)
-
-
-def student_grad_kernel(
-    block, hidden_ref, turned_ref, table_ref, lse_ref, weight_ref, label_ref, dh_ref, grad_ref, pick_ref
-):
-    step = pl.program_id(0)
-    tile = table_ref.shape[1]
-
-    @pl.when(step == 0)
-    def _():
-        dh_ref[...] = jnp.zeros(dh_ref.shape, F32)
-        pick_ref[...] = jnp.zeros(pick_ref.shape, F32)
-
-    grad_ref[...] = jnp.zeros(grad_ref.shape, F32)
-
-    def one(k, carry):
-        rows = pl.ds(pl.multiple_of(k * block, block), block)
-        logits = jnp.dot(hidden_ref[rows, :], table_ref[...], preferred_element_type=F32)
-        soft = jnp.exp(logits - lse_ref[rows, :])
-        weight = weight_ref[rows, :]
-        lane = lax.broadcasted_iota(jnp.int32, logits.shape, 1)
-        hit = lane == label_ref[rows, :] - step * tile
-        dlogits = (((1.0 + MIX_ALPHA) * weight) * soft - jnp.where(hit, weight, 0.0)).astype(B16)
-        pick_ref[rows, :] += lane_fold(jnp.where(hit, logits, 0.0), jnp.add)
-        dh_ref[rows, :] += lax.dot_general(
-            dlogits, table_ref[...], (((1,), (1,)), ((), ())), preferred_element_type=F32
-        )
-        grad_ref[...] += jnp.dot(turned_ref[:, rows], dlogits, preferred_element_type=F32)
-        return carry
-
-    lax.fori_loop(0, hidden_ref.shape[0] // block, one, 0)
-
-
-def student_grad(hidden, turned, table, lse, weight, label):
-    tokens, width = hidden.shape
-    size = table.shape[1]
-    tile = tile_of(size)
-    whole = lambda *shape: pl.BlockSpec(shape, lambda j: (0, 0))
-    return pl.pallas_call(
-        functools.partial(student_grad_kernel, 512),
-        grid=(size // tile,),
-        out_shape=[
-            jax.ShapeDtypeStruct((tokens, width), F32),
-            jax.ShapeDtypeStruct((width, size), F32),
-            jax.ShapeDtypeStruct((tokens, 128), F32),
-        ],
-        in_specs=[
-            whole(tokens, width),
-            whole(width, tokens),
-            pl.BlockSpec((width, tile), lambda j: (0, j)),
-            whole(tokens, 1),
-            whole(tokens, 1),
-            whole(tokens, 1),
-        ],
-        out_specs=[
-            whole(tokens, width),
-            pl.BlockSpec((width, tile), lambda j: (0, j)),
-            whole(tokens, 128),
-        ],
-        compiler_params=pltpu.CompilerParams(vmem_limit_bytes=56 * MIB),
-    )(hidden, turned, table, lse, weight, label)
+        in_specs=[ANYWHERE] * 2 + [IN_VMEM] * 3,
+        out_specs=[ANYWHERE] * 2 + [IN_VMEM] * 5,
+        scratch_shapes=[column] * 2
+        + [pltpu.VMEM((tokens, tile), B16), pltpu.VMEM((V, 8, tokens), F32)]
+        + [halves] * 4
+        + [singles] * 2
+        + sems,
+        compiler_params=pltpu.CompilerParams(
+            collective_id=ident, has_side_effects=True, vmem_limit_bytes=60 * MIB
+        ),
+    )(first, second, own, table, given)
 
 
 def teacher_stats_kernel(group_ref, hidden_ref, table_ref, out_ref, stats_ref, top_ref, sum_ref, cross_ref):
@@ -746,7 +817,7 @@
     def _():
         dh_ref[...] = jnp.zeros(dh_ref.shape, F32)
 
-    grad_ref[...] = gradin_ref[...]
+    grad_ref[...] = gradin_ref[...].astype(F32)
 
     def one(k, carry):
         rows = pl.ds(pl.multiple_of(k * length, length), length)
@@ -1019,21 +1090,13 @@
     kept, h_two = layer_forward(hidden, segment, weights, gains_w)
     two_b = h_two.astype(B16)
 
-    (hidden_all,) = vocab_gather(V, [two_b], 3)
-    hidden_all = hidden_all.reshape(V * length, width)
-    turned = hidden_all.T
-    stats = lax.all_gather(student_stats(hidden_all, table), "vocab")
-    top = jnp.max(stats[:, 0], 0)
-    student_lse = top + jnp.log(jnp.sum(stats[:, 1] * jnp.exp(stats[:, 0] - top), 0))
     weight = counts / counted
-    dh_student, grad_head, pick_lanes = student_grad(
-        hidden_all, turned, table, student_lse[:, None], weight[:, None], labels_here
-    )
-
+    given = jnp.concatenate([weight[:, None], labels_here.astype(F32)], 1)
     first = jnp.concatenate([teacher_qkv, teacher_out, teacher_up], 2)
-    first, second = ring_gather(
-        D, V, [first, teacher_down], tuple((q, r, True, r, q) for r in range(3) for q in range(2)), 4
-    )
+    first, second, hidden_all, turned, dh_student, grad_head, told = study(
+        D, V, first, teacher_down, two_b, table, given, 4
+    )
+    student_lse, picked = told[0], told[1]
     mine = teacher_group[0]
     tw = teacher_qkv.shape[2] // 3
     first = lax.dynamic_index_in_dim(first, mine, 0, False).reshape(tw, -1)
@@ -1053,7 +1116,7 @@
     dh_teacher, grad_head = teacher_grad(
         teacher, turned, table, teacher_lse[:, None], weight[:, None], grad_head
     )
-    everywhere = jnp.sum(hidden_all.astype(F32) * dh_teacher) - jnp.sum(weight[:, None] * pick_lanes)
+    everywhere = jnp.sum(hidden_all.astype(F32) * dh_teacher) - jnp.sum(weight * picked)
     once = jnp.sum(weight * (MIX_ALPHA * (tcross - teacher_lse + student_lse) + student_lse))
     loss_part = everywhere + jnp.where(v == 0, once, 0.0)
 

time: 1010 us -> 924 us (0.915)
  Pallas kernels: 753 us -> 665 us
    pallas_call x2 -> x1, Pallas kernels: 272 us -> 117 us  [ring_gather(): pl.pallas_call(functools.partial(gather_kernel, D, V, spec, len(arrays)),...]
    pallas_call x2 -> x1, Pallas kernels: 103 us -> 188 us  [study(): pl.pallas_call(functools.partial(study_kernel, D, V, spec), out_shape=sha...]
    pallas_call x3 -> x2, Pallas kernels: 61.7 us -> 45 us  [vocab_gather(): pl.pallas_call(functools.partial(vocab_gather_kernel, V, count), out_shap...]
where the time goes in v2:
time: 924 us; the launch traced here: 912 us
  Pallas kernels  665 us (72%)
  matrix products  107 us (12%)
  other arithmetic  64.1 us (7%)
  local copies, waits for them, and re-layouts  57.7 us (6%)
  between operations  12 us (1%)
    pallas_call x1, Pallas kernels, study(): pl.pallas_call(functools.partial(study_kernel, D, V, spec), out_shape=sha...  188 us
    pallas_call x1, Pallas kernels, ring_gather(): pl.pallas_call(functools.partial(gather_kernel, D, V, spec, len(arrays)),...  117 us
    pallas_call x1, Pallas kernels, ring_scatter(): pl.pallas_call(functools.partial(scatter_kernel, D, V, spec), out_shape=s...  112 us
    pallas_call x1, Pallas kernels, teacher_stats(): pl.pallas_call(teacher_stats_kernel, grid_spec=pltpu.PrefetchScalarGridSp...  49.5 us
    pallas_call x1, Pallas kernels, teacher_grad(): pl.pallas_call(teacher_grad_kernel, grid=(size // tile,), out_shape=[jax....  48.4 us
    pallas_call x2, Pallas kernels, vocab_gather(): pl.pallas_call(functools.partial(vocab_gather_kernel, V, count), out_shap...  45 us
    pallas_call x1, Pallas kernels, spread_rows(): pl.pallas_call(spread_kernel, grid=(size // tile,), out_shape=jax.ShapeDt...  37 us
    pallas_call x2, Pallas kernels, vocab_scatter(): pl.pallas_call(functools.partial(vocab_scatter_kernel, V), out_shape=jax....  34.3 us

profile of v2, /device:TPU:0, one launch (start us, length us, event | category | flops | bytes accessed | tf_op | source)
XLA Modules:
  0.0 912.0 jit_solution(5179740797090067049)
XLA Ops:
  22.7 116.7 %shard_map.497 = (bf16[8,2,32,7680]{3,2,1,0:T(8,128)(2,1)}, bf16[1,32,16,2048]{3,2,1,0:T(8,128)(2,1)}, bf16[1,32,16,2048]{3,2,1,0:T(8,128)(2,1)}, bf16[1,32,64,5...) custom-call(bf16[2,32,7680]{2,1,0:T(8,128)(2,1)} %bitcast.197, ...), custom_call_target="tpu_custom_call" | custom-call | tf_op jit(solution)/shard_map/pallas_call | solution.py:232
  146.1 22.9 %shard_map.498 = f32[2048,512]{1,0:T(8,128)S(1)} custom-call(s32[2048,1]{1,0:T(8,128)S(1)} %bitcast.183, bf16[512,7680]{1,0:T(8,128)(2,1)} %bitcast.187), custom_call_target="tpu_custom_call" | custom-call | tf_op jit(solution)/shard_map/pallas_call | solution.py:881
  169.2 17.1 %shard_map.499 = f32[512,512]{1,0:T(8,128)S(1)} custom-call(bf16[2,2,512,512]{3,2,1,0:T(8,128)(2,1)S(1)} %bitcast.186), custom_call_target="tpu_custom_call" | custom-call | tf_op jit(solution)/shard_map/pallas_call | solution.py:506
  211.3 188.3 %shard_map.500 = (bf16[3,32,24,6144]{3,2,1,0:T(8,128)(2,1)}, bf16[3,32,96,768]{3,2,1,0:T(8,128)(2,1)}, bf16[2048,512]{1,0:T(8,128)(2,1)}, bf16[512,2048]{1,0:T(8...) custom-call(bf16[3,24,6144]{2,1,0:T(8,128)(2,1)} %pad_maximum_fusion.2.refs_0_, ...), custom_call_target="tpu_custom_call" | custom-call | tf_op jit(solution)/shard_map/pallas_call | solution.py:735
  400.6 4.8 constant_dynamic-slice_fusion
  405.4 8.6 constant_dynamic-slice_fusion.1
  425.3 10.6 %fusion.183 = (f32[12,512]{1,0:T(8,128)S(1)}, f32[12,512,512]{1,2,0:T(8,128)}) fusion(pred[512,512]{0,1:T(8,128)(4,1)S(1)} %broadcast_compare_fusion, bf16[512,12,64]{0,2,1:T(8,128)(2,1)} %bitcast.214, bf16[512,12,64]{0,2,1:T(8,128)(2,1)} %bitcast.212), kind=kOutput, calls=%fused_computation.279 | convolution fusion | flops 415236608 | bytes 14442496 | tf_op jit(solution)/shard_map/sub | solution.py:975
  435.9 5.9 fusion.72
  445.6 11.6 %fusion.185 = (f32[512]{0:T(512)S(1)}, f32[512,768]{1,0:T(8,128)}) fusion(bf16[3072,768]{1,0:T(8,128)(2,1)} %bitcast.196, bf16[768,6144]{1,0:T(8,128)(2,1)} %bitcast.195, f32[512,768]{1,0:T(8,128)} %copy-done.23, f32[768]{0:T(1024)S(1)} %get-tuple-element.81, f32[768]{0:T(1024)S(1)} %copy-done.48, f32[512]{0:T(512)S(1)} %add_rsqrt_fusion.1, ...), kind=kOutput, calls=%fused_computation.281 | convolution fusion | flops 4850318848 | bytes 14182400 | tf_op jit(solution)/shard_map/dot_general | solution.py:1011
  461.5 27.5 %shard_map.501.hidden_ref = bf16[4,512,768]{2,1,0:T(8,128)(2,1)} custom-call(bf16[512,768]{1,0:T(8,128)(2,1)} %add_convert_fusion.1.refs_0_), custom_call_target="tpu_custom_call" | custom-call | tf_op jit(solution)/shard_map/pallas_call | solution.py:445
  490.9 49.5 %shard_map.502 = (bf16[4,512,7680]{2,1,0:T(8,128)(2,1)}, f32[8,2048]{1,0:T(8,128)S(1)}) custom-call(s32[4]{0:T(128)S(1)} %slice_reduce_fusion.1.group_ref, bf16[4,512,768]{2,1,0:T(8,128)(2,1)S(1)} %copy-done, bf16[3,768,7680]{2,1,0:T(8,128)(2,1)} %table_ref.1), custom_call_target="tpu_custom_call" | custom-call | tf_op jit(solution)/shard_map/pallas_call | solution.py:789
  540.4 5.8 all-gather
  549.6 48.4 %shard_map.503 = (f32[2048,512]{1,0:T(8,128)}, f32[512,7680]{1,0:T(8,128)}) custom-call(bf16[4,512,7680]{2,1,0:T(8,128)(2,1)} %get-tuple-element.55.teacher_ref, bf16[512,2048]{1,0:T(8,128)(2,1)} %get-tuple-element.56.turned_ref, bf16[512,7680]{1,0:T(8,128)(2,1)} %bitcast.189, f32[2048,1]{1,0:T(8,128)} %copy.187.lse_ref, f32[2048,1]{1,0:T(8,128)} %copy.188.weight_ref, ...), custom_call_target="tpu_custom_call" | custom-call | tf_op jit(solution)/shard_map/pallas_call | solution.py:840
  598.0 7.2 multiply_reduce_fusion.1
  608.1 17.1 %shard_map.504 = f32[512,512]{1,0:T(8,128)S(1)} custom-call(bf16[2,2,512,512]{3,2,1,0:T(8,128)(2,1)S(1)} %bitcast.185), custom_call_target="tpu_custom_call" | custom-call | tf_op jit(solution)/shard_map/pallas_call | solution.py:506
  631.7 5.3 fusion.32
  656.0 14.0 %fusion.85 = bf16[8,64,512]{2,1,0:T(8,128)(2,1)} fusion(bf16[512,8,64]{0,2,1:T(8,128)(2,1)S(1)} %bitcast.203, f32[8,512,512]{1,2,0:T(8,128)} %fusion.190, f32[8,512,512]{1,2,0:T(8,128)} %copy-done.3, f32[8,512]{1,0:T(8,128)S(1)} %log_add_fusion, pred[512,512]{0,1:T(8,128)(4,1)S(1)} %broadcast_compare_fusion), kind=kOutput, calls=%fused_computation.100 | convolution fusion | flops 291770880 | bytes 18104320 | tf_op jit(solution)/shard_map/hqk,khd->qhd/dot_general | solution.py:991
  670.1 14.7 %fusion.88 = bf16[8,64,512]{2,1,0:T(8,128)(2,1)} fusion(bf16[512,8,64]{0,2,1:T(8,128)(2,1)} %bitcast.201, f32[8,512,512]{1,2,0:T(8,128)} %fusion.190, f32[8,512,512]{1,2,0:T(8,128)} %copy-done.3, f32[8,512]{1,0:T(8,128)S(1)} %log_add_fusion, pred[512,512]{0,1:T(8,128)(4,1)S(1)} %broadcast_compare_fusion), kind=kOutput, calls=%fused_computation.101 | convolution fusion | flops 291770880 | bytes 18104320 | tf_op jit(solution)/shard_map/hqk,qhd->khd/dot_general | solution.py:992
  693.2 17.6 %shard_map.505.turned_ref = bf16[4,512,512]{2,1,0:T(8,128)(2,1)} custom-call(bf16[512,512]{1,0:T(8,128)(2,1)} %bitcast.206), custom_call_target="tpu_custom_call" | custom-call | tf_op jit(solution)/shard_map/pallas_call | solution.py:445
  712.3 37.0 %shard_map.506 = bf16[512,7680]{1,0:T(8,128)(2,1)} custom-call(s32[2048,1]{1,0:T(8,128)S(1)} %bitcast.184, bf16[4,512,512]{2,1,0:T(8,128)(2,1)S(1)} %copy-done.1, f32[512,7680]{1,0:T(8,128)} %get-tuple-element.60.grad_ref), custom_call_target="tpu_custom_call" | custom-call | tf_op jit(solution)/shard_map/pallas_call | solution.py:912
  749.3 5.5 slice_bitcast_fusion
  754.8 112.1 %shard_map.507 = (f32[32,7680]{1,0:T(8,128)}, f32[32,7680]{1,0:T(8,128)}, f32[16,2048]{1,0:T(8,128)}, f32[16,2048]{1,0:T(8,128)}, f32[64,512]{1,0:T(8,128)}, /*index=5*/f32[16,512]{1,0:T(8,128)}) custom-call(bf16[8,32,7680]{2,1,0:T(8,128)(2,1)} %get-tuple-element.110.refs_0_, bf16[8,32,7680]{2,1,0:T(8,128)(2,1)} %get-tuple-element.109.refs_1_, ...), custom_call_target="tpu_custom_call" | custom-call | tf_op jit(solution)/shard_map/pallas_call | solution.py:376
  882.9 10.8 %shard_map.508 = f32[8,512]{1,0:T(8,128)} custom-call(f32[8,512]{1,0:T(8,128)} %concatenate.51.in_ref), custom_call_target="tpu_custom_call" | custom-call | tf_op jit(solution)/shard_map/pallas_call | solution.py:561
  904.7 5.7 multiply_subtract_fusion
  (245 shorter events, 135.3 us)
Async XLA Ops:
  0.7 21.0 %copy-start.8 = (f32[7680,64]{0,1:T(8,128)S(1)}, f32[7680,64]{0,1:T(8,128)}, u32[]{:S(2)}) copy-start(f32[7680,64]{0,1:T(8,128)} %param.47) | copy-start | bytes 5898244
  4.3 182.5 %copy-start.46 = (s32[512]{0:T(512)}, s32[512]{0:T(512)S(1)}, u32[]{:S(2)}) copy-start(s32[512]{0:T(512)S(1)} %iota_subtract_fusion) | copy-start | bytes 6148
  10.0 194.0 %copy-start.51 = (f32[1,512]{1,0:T(1,128)}, f32[1,512]{1,0:T(1,128)S(1)}, u32[]{:S(2)}) copy-start(f32[1,512]{1,0:T(1,128)S(1)} %get-tuple-element.136) | copy-start | bytes 6148
  188.5 15.5 %copy-start.4 = (f32[512,512]{0,1:T(8,128)}, f32[512,512]{0,1:T(8,128)S(1)}, u32[]{:S(2)}) copy-start(f32[512,512]{0,1:T(8,128)S(1)} %get-tuple-element.140) | copy-start | bytes 3145732
  670.1 14.7 %copy-start.5 = (f32[512,512]{0,1:T(8,128)S(1)}, f32[512,512]{0,1:T(8,128)}, u32[]{:S(2)}) copy-start(f32[512,512]{0,1:T(8,128)} %copy-done.4) | copy-start | bytes 3145732
  866.9 30.8 %copy-start.41 = (f32[6,512]{1,0:T(8,128)S(1)}, f32[6,512]{1,0:T(8,128)}, u32[]{:S(2)}) copy-start(f32[6,512]{1,0:T(8,128)} %param.65) | copy-start | bytes 36868
  867.0 30.8 %copy-start.44 = (f32[6,512]{1,0:T(8,128)S(1)}, f32[6,512]{1,0:T(8,128)}, u32[]{:S(2)}) copy-start(f32[6,512]{1,0:T(8,128)} %param.67) | copy-start | bytes 36868
  867.0 30.8 %copy-start.45 = (f32[6,512]{1,0:T(8,128)S(1)}, f32[6,512]{1,0:T(8,128)}, u32[]{:S(2)}) copy-start(f32[6,512]{1,0:T(8,128)} %param.66) | copy-start | bytes 36868
  867.0 32.3 %copy-start.33 = (f32[16,512]{1,0:T(8,128)S(1)}, f32[16,512]{1,0:T(8,128)}, u32[]{:S(2)}) copy-start(f32[16,512]{1,0:T(8,128)} %param.50) | copy-start | bytes 98308
  867.0 32.3 %copy-start.35 = (f32[16,512]{1,0:T(8,128)S(1)}, f32[16,512]{1,0:T(8,128)}, u32[]{:S(2)}) copy-start(f32[16,512]{1,0:T(8,128)} %get-tuple-element.66) | copy-start | bytes 98308
  867.0 32.3 %copy-start.42 = (f32[16,512]{1,0:T(8,128)S(1)}, f32[16,512]{1,0:T(8,128)}, u32[]{:S(2)}) copy-start(f32[16,512]{1,0:T(8,128)} %param.52) | copy-start | bytes 98308
  867.0 32.3 %copy-start.43 = (f32[16,512]{1,0:T(8,128)S(1)}, f32[16,512]{1,0:T(8,128)}, u32[]{:S(2)}) copy-start(f32[16,512]{1,0:T(8,128)} %param.51) | copy-start | bytes 98308
  867.0 33.0 %copy-start.25 = (f32[16,2048]{1,0:T(8,128)S(1)}, f32[16,2048]{1,0:T(8,128)}, u32[]{:S(2)}) copy-start(f32[16,2048]{1,0:T(8,128)} %get-tuple-element.63) | copy-start | bytes 393220
  867.0 33.0 %copy-start.34 = (f32[16,512]{1,0:T(8,128)S(1)}, f32[16,512]{1,0:T(8,128)}, u32[]{:S(2)}) copy-start(f32[16,512]{1,0:T(8,128)} %param.56) | copy-start | bytes 98308
  867.1 34.4 %copy-start.32 = (f32[16,1536]{1,0:T(8,128)S(1)}, f32[16,1536]{1,0:T(8,128)}, u32[]{:S(2)}) copy-start(f32[16,1536]{1,0:T(8,128)} %param.53) | copy-start | bytes 294916
  867.1 34.4 %copy-start.40 = (f32[16,1536]{1,0:T(8,128)S(1)}, f32[16,1536]{1,0:T(8,128)}, u32[]{:S(2)}) copy-start(f32[16,1536]{1,0:T(8,128)} %param.55) | copy-start | bytes 294916
  867.1 36.0 %copy-start.26 = (f32[16,2048]{1,0:T(8,128)S(1)}, f32[16,2048]{1,0:T(8,128)}, u32[]{:S(2)}) copy-start(f32[16,2048]{1,0:T(8,128)} %param.59) | copy-start | bytes 393220
  867.1 36.0 %copy-start.29 = (f32[16,2048]{1,0:T(8,128)S(1)}, f32[16,2048]{1,0:T(8,128)}, u32[]{:S(2)}) copy-start(f32[16,2048]{1,0:T(8,128)} %get-tuple-element.64) | copy-start | bytes 393220
  867.1 36.0 %copy-start.36 = (f32[16,2048]{1,0:T(8,128)S(1)}, f32[16,2048]{1,0:T(8,128)}, u32[]{:S(2)}) copy-start(f32[16,2048]{1,0:T(8,128)} %param.61) | copy-start | bytes 393220
  867.1 36.0 %copy-start.37 = (f32[16,2048]{1,0:T(8,128)S(1)}, f32[16,2048]{1,0:T(8,128)}, u32[]{:S(2)}) copy-start(f32[16,2048]{1,0:T(8,128)} %param.60) | copy-start | bytes 393220
  871.7 32.2 %copy-start.27 = (f32[64,512]{1,0:T(8,128)S(1)}, f32[64,512]{1,0:T(8,128)}, u32[]{:S(2)}) copy-start(f32[64,512]{1,0:T(8,128)} %param.62) | copy-start | bytes 393220
  871.7 32.2 %copy-start.28 = (f32[64,512]{1,0:T(8,128)S(1)}, f32[64,512]{1,0:T(8,128)}, u32[]{:S(2)}) copy-start(f32[64,512]{1,0:T(8,128)} %get-tuple-element.65) | copy-start | bytes 393220
  871.7 32.2 %copy-start.38 = (f32[64,512]{1,0:T(8,128)S(1)}, f32[64,512]{1,0:T(8,128)}, u32[]{:S(2)}) copy-start(f32[64,512]{1,0:T(8,128)} %param.64) | copy-start | bytes 393220
  871.7 32.2 %copy-start.39 = (f32[64,512]{1,0:T(8,128)S(1)}, f32[64,512]{1,0:T(8,128)}, u32[]{:S(2)}) copy-start(f32[64,512]{1,0:T(8,128)} %param.63) | copy-start | bytes 393220
  (36 other events, 149.7 us)

commit v3 on v2

--- a/solution.py
+++ b/solution.py
@@ -109,6 +109,8 @@
             for turn, hops in zip((0, 1), ring.hops(piece[4])):
                 self.streams.append((piece, ring, turn, hops, number))
         self.longest = max(s[3] for s in self.streams)
+        most = {w: max(r.hops(0)) for w, r in rings.items()}
+        self.every = {w: max(1, self.longest // max(m, 1)) for w, m in most.items()}
 
     def dst(self, piece, slot):
         which, k, lead, _, _ = piece
@@ -159,10 +161,12 @@
     def within(self, s, hops):
         return True if hops == self.longest else s <= hops
 
-    def serve(self, s):
+    def serve(self, step):
         for i, stream in enumerate(self.streams):
-
-            def take(i=i, stream=stream):
+            every = self.every[stream[0][3]]
+            s = step // every
+
+            def take(i=i, stream=stream, s=s):
                 slot = self.origin(stream, s)
                 block = self.dst(stream[0], slot)
                 self.remote(i, s - 1, block, slot).wait_recv()
@@ -170,7 +174,10 @@
                 if not stream[1].over_dp:
                     self.across(i, s, block, slot).start()
 
-            on_condition(self.within(s, stream[3]), take)
+            condition = self.within(s, stream[3])
+            if every > 1:
+                condition = (lax.rem(step, every) == 0) & (s <= stream[3])
+            on_condition(condition, take)
 
     def serve_range(self, low, high):
         def body(s, carry):
@@ -239,150 +246,260 @@
     )(*arrays)
 
 
-def scatter_kernel(D, V, spec, *refs):
-    count = len(spec)
-    ins, outs = refs[:count], refs[count : 2 * count]
-    scratch = list(refs[2 * count :])
-    ssem, rsem, xssem, xrsem = scratch[-4:]
-    rings = {w: Ring(D, V, w) for w in dict.fromkeys(p[0] for p in spec)}
-    core = lax.rem(lax.axis_index("vocab"), 2)
-    sib = sibling()
-    nexts = {w: (r.at(1), r.at(-1)) for w, r in rings.items()}
-    crossing = any(w != "dp" for w in rings)
-    greet(
-        [r.device(place) for w, r in rings.items() for place in nexts[w]]
-        + ([sib] if crossing else [])
-    )
-    sums, slots = [], []
-    for number, (which, parity) in enumerate(spec):
-        if which == "dp":
-            sums.append(ins[number])
-        else:
-            sums.append(scratch.pop(0))
-        slots.append((scratch.pop(0), scratch.pop(0)))
-    streams = []
-    for number, (which, parity) in enumerate(spec):
-        for turn, hops in zip((0, 1), rings[which].hops(parity)):
-            streams.append((number, rings[which], turn, hops, which))
-    streams = [s for s in streams if s[3] > 0]
-
-    def place(stream, ahead):
+class Scatter:
+    def __init__(self, pieces, sems):
+        self.pieces = pieces
+        self.ssem, self.rsem = sems
+        self.streams = []
+        for number, (ring, parity, _, _) in enumerate(pieces):
+            for turn, hops in zip((0, 1), ring.hops(parity)):
+                if hops:
+                    self.streams.append((number, ring, turn, hops))
+        self.longest = max(s[3] for s in self.streams)
+
+    def place(self, stream, ahead):
         return stream[1].at(ahead) if stream[2] == 0 else stream[1].at(-ahead)
 
-    def remote(i, s, src):
-        number, ring, turn, hops, which = streams[i]
+    def slots(self, stream):
+        return self.pieces[stream[0]][3][stream[2]]
+
+    def remote(self, i, s, src):
+        stream = self.streams[i]
         return pltpu.make_async_remote_copy(
             src_ref=src,
-            dst_ref=slots[number][turn].at[s],
-            send_sem=ssem.at[s, i],
-            recv_sem=rsem.at[s, i],
-            device_id=ring.device(nexts[which][turn]),
+            dst_ref=self.slots(stream).at[s],
+            send_sem=self.ssem.at[s, i],
+            recv_sem=self.rsem.at[s, i],
+            device_id=stream[1].device(self.place(stream, 1)),
             device_id_type=MESH,
         )
 
-    def across(number):
+    def first(self, i):
+        stream = self.streams[i]
+        return self.remote(i, 0, self.pieces[stream[0]][2].at[self.place(stream, stream[3])])
+
+    def begin(self, number):
+        for i, stream in enumerate(self.streams):
+            if stream[0] == number:
+                self.first(i).start()
+
+    def serve(self, s):
+        for i, stream in enumerate(self.streams):
+            hops = stream[3]
+
+            def take(i=i, stream=stream, hops=hops):
+                block = self.slots(stream).at[s - 1]
+                self.remote(i, s - 1, block).wait_recv()
+
+                def onward():
+                    mine = self.pieces[stream[0]][2].at[self.place(stream, hops - s)]
+                    block[...] = (block[...].astype(F32) + mine[...].astype(F32)).astype(B16)
+                    self.remote(i, s, block).start()
+
+                pl.when(s < hops)(onward)
+
+            on_condition(True if hops == self.longest else s <= hops, take)
+
+    def serve_range(self, low, high):
+        def body(s, carry):
+            self.serve(s)
+            return carry
+
+        lax.fori_loop(low, high, body, 0)
+
+    def total(self, number):
+        ring, parity, terms, slots = self.pieces[number]
+        total = terms[ring.me].astype(F32)
+        for turn, hops in zip((0, 1), ring.hops(parity)):
+            if hops:
+                total = total + slots[turn][hops - 1].astype(F32)
+        return total
+
+    def finish(self):
+        for i, stream in enumerate(self.streams):
+            self.first(i).wait_send()
+
+            def sent(s, carry, i=i, stream=stream):
+                self.remote(i, s, self.slots(stream).at[s - 1]).wait_send()
+                return carry
+
+            lax.fori_loop(1, stream[3], sent, 0)
+
+
+def settle_kernel(D, V, rings, *refs):
+    count = len(rings)
+    table_in, dx_ref, ids_ref, gains_ref = refs[:4]
+    dense_in, refs = refs[4 : 4 + count], refs[4 + count :]
+    table_out, totals_out = refs[:2]
+    dense_out, refs = refs[2 : 2 + count], refs[2 + count :]
+    dx_all, table_sums, table_slots, first, second = refs[:5]
+    dense_sums, refs = refs[5 : 5 + count], refs[5 + count :]
+    dense_slots, refs = refs[: 2 * count], refs[2 * count :]
+    ts, tr, ds, dr, cs, cr, hs, hr, xs, xr, ns, nr = refs
+    d, v = lax.axis_index("dp"), lax.axis_index("vocab")
+    half = V // 2
+    core, chip = lax.rem(v, 2), v // 2
+    sib = sibling()
+    width, length = dx_ref.shape
+    chunks, _, columns, tile = table_sums.shape
+    over_dp = Ring(D, V, "dp")
+    chips = {w: Ring(D, V, w) for w in dict.fromkeys(rings)}
+    more, less = over_dp.hops(0)
+    table = Scatter(
+        [
+            (over_dp, c % 2, table_sums.at[c], (table_slots.at[c], table_slots.at[c, pl.ds(over_dp.hops(c % 2)[0], over_dp.hops(c % 2)[1])]))
+            for c in range(chunks)
+        ],
+        (ts, tr),
+    )
+    dense = Scatter(
+        [
+            (chips[w], k % 2, dense_sums[k], (dense_slots[2 * k], dense_slots[2 * k + 1]))
+            for k, w in enumerate(rings)
+        ],
+        (ds, dr),
+    )
+    peers = [(d, lax.rem(v + k, V)) for k in range(1, V)]
+    peers += [(lax.rem(d + k, D), v) for k in range(1, D)]
+    near = [r.device(r.at(k)) for r in (over_dp, *chips.values()) for k in (1, -1)]
+    greet(near + peers)
+
+    def other(k):
+        return lax.rem(chip + k + half, half) * 2 + core
+
+    def send(k):
         return pltpu.make_async_remote_copy(
-            src_ref=ins[number].at[:, 1 - core],
-            dst_ref=sums[number],
-            send_sem=xssem.at[number],
-            recv_sem=xrsem.at[number],
-            device_id=sib,
-            device_id_type=MESH,
+            src_ref=dx_ref, dst_ref=dx_all.at[v], send_sem=hs.at[k], recv_sem=hr.at[k],
+            device_id=(d, other(k)), device_id_type=MESH,
         )
 
-    def first(i):
-        number, _, _, hops, _ = streams[i]
-        return remote(i, 0, sums[number].at[place(streams[i], hops)])
-
-    for number, (which, _) in enumerate(spec):
-        if which != "dp":
-            across(number).start()
-    for i, stream in enumerate(streams):
-        if stream[4] == "dp":
-            first(i).start()
-    for number, (which, _) in enumerate(spec):
-        if which != "dp":
-            across(number).wait_recv()
-
-            def add(k, carry, number=number):
-                total = sums[number][k].astype(F32) + ins[number][k, core].astype(F32)
-                sums[number][k] = total.astype(B16)
-                return carry
-
-            lax.fori_loop(0, rings[which].n, add, 0)
-            for i, stream in enumerate(streams):
-                if stream[0] == number:
-                    first(i).start()
-    longest = max(s[3] for s in streams)
-    stride = {w: max(1, longest // max(max(r.hops(0)), 1)) for w, r in rings.items()}
-
-    def body(s, carry):
-        for i, stream in enumerate(streams):
-            number, ring, turn, hops, which = stream
-            by = stride[which]
-
-            def take(i=i, stream=stream, number=number, turn=turn, hops=hops, by=by):
-                step = s // by
-                block = slots[number][turn].at[step - 1]
-                remote(i, step - 1, block).wait_recv()
-
-                def onward():
-                    mine = sums[number].at[place(stream, hops - step)]
-                    block[...] = (block[...].astype(F32) + mine[...].astype(F32)).astype(B16)
-                    remote(i, step, block).start()
-
-                pl.when(step < hops)(onward)
-
-            condition = True
-            if by > 1 or hops * by < longest:
-                condition = (lax.rem(s, by) == 0) & (s // by <= hops)
-            on_condition(condition, take)
-        return carry
-
-    lax.fori_loop(1, longest + 1, body, 0)
-    for number, (which, parity) in enumerate(spec):
-        total = sums[number][rings[which].me].astype(F32)
-        for turn, hops in zip((0, 1), rings[which].hops(parity)):
-            if hops > 0:
-                total = total + slots[number][turn][hops - 1].astype(F32)
-        outs[number][...] = total
-    for i, stream in enumerate(streams):
-        number, ring, turn, hops, which = stream
-        first(i).wait_send()
-
-        def sent(s, carry, i=i, number=number, turn=turn):
-            remote(i, s, slots[number][turn].at[s - 1]).wait_send()
+    def across(k, src, slot):
+        return pltpu.make_async_remote_copy(
+            src_ref=src, dst_ref=dx_all.at[slot], send_sem=xs.at[k], recv_sem=xr.at[k],
+            device_id=sib, device_id_type=MESH,
+        )
+
+    def crossing(k):
+        return pltpu.make_async_remote_copy(
+            src_ref=dense_in[k].at[:, 1 - core], dst_ref=dense_sums[k], send_sem=cs.at[k], recv_sem=cr.at[k],
+            device_id=sib, device_id_type=MESH,
+        )
+
+    for k in range(1, half):
+        send(k).start()
+    for k in range(count):
+        crossing(k).start()
+    across(0, dx_ref, v).start()
+    dx_all[v] = dx_ref[...]
+    for k in range(count):
+        crossing(k).wait_recv()
+
+        def add(place, carry, k=k):
+            total = dense_sums[k][place].astype(F32) + dense_in[k][place, core].astype(F32)
+            dense_sums[k][place] = total.astype(B16)
             return carry
 
-        lax.fori_loop(1, hops, sent, 0)
-    for number, (which, _) in enumerate(spec):
-        if which != "dp":
-            across(number).wait_send()
-
-
-def ring_scatter(D, V, arrays, spec, ident):
-    scratch, shapes = [], []
-    for array, (which, parity) in zip(arrays, spec):
-        block = array.shape[-2:]
-        n = D if which == "dp" else D * V // 2
-        if which != "dp":
-            scratch.append(pltpu.VMEM((n,) + block, B16))
-        more, less = n // 2, n - 1 - n // 2
-        scratch += [pltpu.VMEM((max(k, 1),) + block, B16) for k in ((more, less), (less, more))[parity]]
-        shapes.append(jax.ShapeDtypeStruct(block, F32))
-    longest = max((D if w == "dp" else D * V // 2) // 2 for w, _ in spec)
-    sems = pltpu.SemaphoreType.DMA((longest, 2 * len(spec)))
-    single = pltpu.SemaphoreType.DMA((len(spec),))
+        lax.fori_loop(0, D * half, add, 0)
+        dense.begin(k)
+    for k in range(1, half):
+        slot = other(-k)
+        send(k).wait_recv()
+        across(k, dx_all.at[slot], slot).start()
+    for k in range(half):
+        across(k, dx_ref, other(-k) + 1 - 2 * core).wait_recv()
+
+    for c in range(chunks):
+        grad = table_in[:, c * tile : (c + 1) * tile].astype(F32)
+        lane = lax.broadcasted_iota(jnp.int32, (length, tile), 1) + c * tile
+        for k in range(V):
+            hit = jnp.where(lane == ids_ref[k * length : (k + 1) * length, :], 1.0, 0.0).astype(B16)
+            grad = grad + mm(dx_all[k], hit)
+        table_sums[c] = grad.astype(B16).reshape(D, columns, tile)
+        table.begin(c)
+        dense.serve_range(1 + c * dense.longest // chunks, 1 + (c + 1) * dense.longest // chunks)
+    squares = jnp.zeros((1, 1), F32)
+    for k in range(count):
+        total = dense.total(k)
+        dense_out[k][...] = total
+        squares += jnp.sum(jnp.sum(total * total, 1, keepdims=True), 0, keepdims=True)
+    table.serve_range(1, table.longest + 1)
+    for c in range(chunks):
+        total = table.total(c)
+        table_out[:, c * tile : (c + 1) * tile] = total
+        squares += jnp.sum(jnp.sum(total * total, 1, keepdims=True), 0, keepdims=True)
+    row = lax.broadcasted_iota(jnp.int32, gains_ref.shape, 0)
+    lane = lax.broadcasted_iota(jnp.int32, gains_ref.shape, 1)
+    local = jnp.where((row == gains_ref.shape[0] - 1) & (lane == 0), squares, gains_ref[...])
+
+    def tell(k):
+        over, mine = (first, v) if k < V - 1 else (second, d)
+        return pltpu.make_async_remote_copy(
+            src_ref=over.at[mine], dst_ref=over.at[mine], send_sem=ns.at[k], recv_sem=nr.at[k],
+            device_id=peers[k], device_id_type=MESH,
+        )
+
+    def stage(slots, mine, value, low, high):
+        slots[mine] = value
+        for k in range(low, high):
+            tell(k).start()
+        for k in range(low, high):
+            tell(k).wait_recv()
+        total = slots[0]
+        for k in range(1, slots.shape[0]):
+            total = total + slots[k]
+        return total
+
+    local = stage(first, v, local, 0, V - 1)
+    totals_out[...] = stage(second, d, local, V - 1, V + D - 2)
+    for k in range(V + D - 2):
+        tell(k).wait_send()
+    for k in range(1, half):
+        send(k).wait_send()
+    for k in range(half):
+        across(k, dx_ref, v).wait_send()
+    for k in range(count):
+        crossing(k).wait_send()
+    dense.finish()
+    table.finish()
+
+
+def settle(D, V, grad, dx, ids, gains, dense, rings, ident):
+    width, size = grad.shape
+    length = dx.shape[1]
+    tile = tile_of(size, V * length)
+    chunks, columns = size // tile, width // D
+    n = D * V // 2
+    count = len(dense)
+    blocks = [a.shape[-2:] for a in dense]
+    more, less = n // 2, n - 1 - n // 2
+    slots = []
+    for k, block in enumerate(blocks):
+        slots += [pltpu.VMEM((h,) + block, B16) for h in ((more, less), (less, more))[k % 2]]
+    sems = lambda *shape: pltpu.SemaphoreType.DMA(shape)
     return pl.pallas_call(
-        functools.partial(scatter_kernel, D, V, spec),
-        out_shape=shapes,
-        in_specs=[IN_VMEM] * len(arrays),
-        out_specs=[IN_VMEM] * len(arrays),
-        scratch_shapes=scratch + [sems, sems, single, single],
+        functools.partial(settle_kernel, D, V, rings),
+        out_shape=[jax.ShapeDtypeStruct((columns, size), F32), jax.ShapeDtypeStruct(gains.shape, F32)]
+        + [jax.ShapeDtypeStruct(block, F32) for block in blocks],
+        in_specs=[IN_VMEM] * (4 + count),
+        out_specs=[IN_VMEM] * (2 + count),
+        scratch_shapes=[
+            pltpu.VMEM((V, width, length), B16),
+            pltpu.VMEM((chunks, D, columns, tile), B16),
+            pltpu.VMEM((chunks, D - 1, columns, tile), B16),
+            pltpu.VMEM((V,) + gains.shape, F32),
+            pltpu.VMEM((D,) + gains.shape, F32),
+        ]
+        + [pltpu.VMEM((n,) + block, B16) for block in blocks]
+        + slots
+        + [sems(D // 2, 2 * chunks)] * 2
+        + [sems(n // 2, 2 * count)] * 2
+        + [sems(count)] * 2
+        + [sems(V // 2)] * 4
+        + [sems(V + D - 2)] * 2,
         compiler_params=pltpu.CompilerParams(
-            collective_id=ident, has_side_effects=True, vmem_limit_bytes=56 * MIB
+            collective_id=ident, has_side_effects=True, vmem_limit_bytes=62 * MIB
         ),
-    )(*arrays)
+    )(grad, dx, ids, gains, *dense)
 
 
 def vocab_gather_kernel(V, count, *refs):
@@ -519,53 +636,6 @@
             collective_id=ident, has_side_effects=True, vmem_limit_bytes=40 * MIB
         ),
     )(array.reshape((half, 2) + block))
-
-
-def total_kernel(D, V, in_ref, out_ref, first, second, ssem, rsem):
-    d, v = lax.axis_index("dp"), lax.axis_index("vocab")
-    peers = [(d, lax.rem(v + k, V)) for k in range(1, V)]
-    peers += [(lax.rem(d + k, D), v) for k in range(1, D)]
-    greet(peers)
-
-    def send(k):
-        over = first if k < V - 1 else second
-        mine = v if k < V - 1 else d
-        return pltpu.make_async_remote_copy(
-            src_ref=over.at[mine],
-            dst_ref=over.at[mine],
-            send_sem=ssem.at[k],
-            recv_sem=rsem.at[k],
-            device_id=peers[k],
-            device_id_type=MESH,
-        )
-
-    def stage(slots, mine, value, low, high):
-        slots[mine] = value
-        for k in range(low, high):
-            send(k).start()
-        for k in range(low, high):
-            send(k).wait_recv()
-        total = slots[0]
-        for k in range(1, slots.shape[0]):
-            total = total + slots[k]
-        return total
-
-    total = stage(first, v, in_ref[...], 0, V - 1)
-    out_ref[...] = stage(second, d, total, V - 1, V + D - 2)
-    for k in range(V + D - 2):
-        send(k).wait_send()
-
-
-def total_all(D, V, array, ident):
-    sems = pltpu.SemaphoreType.DMA((V + D - 2,))
-    return pl.pallas_call(
-        functools.partial(total_kernel, D, V),
-        out_shape=jax.ShapeDtypeStruct(array.shape, F32),
-        in_specs=[IN_VMEM],
-        out_specs=IN_VMEM,
-        scratch_shapes=[pltpu.VMEM((V,) + array.shape, F32), pltpu.VMEM((D,) + array.shape, F32), sems, sems],
-        compiler_params=pltpu.CompilerParams(collective_id=ident, has_side_effects=True),
-    )(array)
 
 
 def tile_of(size, tokens=1):
@@ -756,23 +826,28 @@
 
 
 def teacher_stats_kernel(group_ref, hidden_ref, table_ref, out_ref, stats_ref, top_ref, sum_ref, cross_ref):
-    step, row = pl.program_id(0), pl.program_id(1)
-    length = hidden_ref.shape[1]
-    rows = pl.ds(pl.multiple_of(row * length, length), length)
+    step = pl.program_id(0)
+    count, length = hidden_ref.shape[:2]
+    block = min(256, length)
 
     @pl.when(step == 0)
     def _():
-        top_ref[rows, :] = jnp.full((length, 128), -jnp.inf, F32)
-        sum_ref[rows, :] = jnp.zeros((length, 128), F32)
-        cross_ref[rows, :] = jnp.zeros((length, 128), F32)
-
-    rounded = jnp.dot(hidden_ref[0], table_ref[0], preferred_element_type=F32).astype(B16)
-    out_ref[0] = rounded
-    values = rounded.astype(F32)
-    expd, fade = running(values, top_ref, sum_ref, rows)
-    cross_ref[rows, :] = cross_ref[rows, :] * fade + lane_fold(expd * values, jnp.add)
-
-    @pl.when((step == pl.num_programs(0) - 1) & (row == pl.num_programs(1) - 1))
+        top_ref[...] = jnp.full(top_ref.shape, -jnp.inf, F32)
+        sum_ref[...] = jnp.zeros(sum_ref.shape, F32)
+        cross_ref[...] = jnp.zeros(cross_ref.shape, F32)
+
+    for row in range(count):
+        table = table_ref[group_ref[row]]
+        for k in range(length // block):
+            inside = slice(k * block, (k + 1) * block)
+            rows = slice(row * length + k * block, row * length + (k + 1) * block)
+            rounded = mm(hidden_ref[row, inside, :], table).astype(B16)
+            out_ref[row, inside, :] = rounded
+            values = rounded.astype(F32)
+            expd, fade = running(values, top_ref, sum_ref, rows)
+            cross_ref[rows, :] = cross_ref[rows, :] * fade + lane_fold(expd * values, jnp.add)
+
+    @pl.when(step == pl.num_programs(0) - 1)
     def _():
         top = jnp.max(top_ref[...], 1, keepdims=True)
         scale = jnp.exp(top_ref[...] - top)
@@ -783,21 +858,21 @@
 
 def teacher_stats(groups, hidden, tables):
     count, length, width = hidden.shape
-    size = tables.shape[2]
-    tile = tile_of(size)
+    kinds, _, size = tables.shape
     tokens = count * length
+    tile = tile_of(size, tokens)
     return pl.pallas_call(
         teacher_stats_kernel,
         grid_spec=pltpu.PrefetchScalarGridSpec(
             num_scalar_prefetch=1,
-            grid=(size // tile, count),
+            grid=(size // tile,),
             in_specs=[
-                pl.BlockSpec((1, length, width), lambda j, r, g: (r, 0, 0)),
-                pl.BlockSpec((1, width, tile), lambda j, r, g: (g[r], 0, j)),
+                pl.BlockSpec((count, length, width), lambda j, g: (0, 0, 0)),
+                pl.BlockSpec((kinds, width, tile), lambda j, g: (0, 0, j)),
             ],
             out_specs=[
-                pl.BlockSpec((1, length, tile), lambda j, r, g: (r, 0, j)),
-                pl.BlockSpec((8, tokens), lambda j, r, g: (0, 0)),
+                pl.BlockSpec((count, length, tile), lambda j, g: (0, 0, j)),
+                pl.BlockSpec((8, tokens), lambda j, g: (0, 0)),
             ],
             scratch_shapes=[pltpu.VMEM((tokens, 128), F32)] * 3,
         ),
@@ -805,53 +880,61 @@
             jax.ShapeDtypeStruct((count, length, size), B16),
             jax.ShapeDtypeStruct((8, tokens), F32),
         ],
-        compiler_params=pltpu.CompilerParams(vmem_limit_bytes=48 * MIB),
+        compiler_params=pltpu.CompilerParams(vmem_limit_bytes=60 * MIB),
     )(groups, hidden, tables)
 
 
-def teacher_grad_kernel(teacher_ref, turned_ref, table_ref, lse_ref, weight_ref, gradin_ref, dh_ref, grad_ref):
+def teacher_grad_kernel(
+    teacher_ref, turned_ref, hidden_ref, table_ref, given_ref, dhin_ref, gradin_ref,
+    dh_ref, grad_ref, cross_ref, dl_ref, sum_ref,
+):
     step = pl.program_id(0)
     count, length = teacher_ref.shape[:2]
+    block = min(256, length)
 
     @pl.when(step == 0)
     def _():
-        dh_ref[...] = jnp.zeros(dh_ref.shape, F32)
-
-    grad_ref[...] = gradin_ref[...].astype(F32)
-
-    def one(k, carry):
-        rows = pl.ds(pl.multiple_of(k * length, length), length)
-        target = jnp.exp(teacher_ref[k].astype(F32) - lse_ref[rows, :])
-        dlogits = ((-MIX_ALPHA * weight_ref[rows, :]) * target).astype(B16)
-        dh_ref[rows, :] += lax.dot_general(
-            dlogits, table_ref[...], (((1,), (1,)), ((), ())), preferred_element_type=F32
-        )
-        grad_ref[...] += jnp.dot(turned_ref[:, rows], dlogits, preferred_element_type=F32)
-        return carry
-
-    lax.fori_loop(0, count, one, 0)
-
-
-def teacher_grad(teacher, turned, table, lse, weight, grad):
+        sum_ref[...] = dhin_ref[...]
+
+    for row in range(count):
+        for k in range(length // block):
+            inside = slice(k * block, (k + 1) * block)
+            rows = slice(row * length + k * block, row * length + (k + 1) * block)
+            target = jnp.exp(teacher_ref[row, inside, :].astype(F32) - given_ref[rows, 1:2])
+            dl_ref[rows, :] = ((-MIX_ALPHA * given_ref[rows, 0:1]) * target).astype(B16)
+        rows = slice(row * length, (row + 1) * length)
+        sum_ref[rows, :] += mm(dl_ref[rows, :], table_ref[...], (1, 1))
+    grad_ref[...] = (gradin_ref[...].astype(F32) + mm(turned_ref[...], dl_ref[...])).astype(grad_ref.dtype)
+
+    @pl.when(step == pl.num_programs(0) - 1)
+    def _():
+        dh_ref[...] = sum_ref[...].astype(B16)
+        part = jnp.sum(hidden_ref[...].astype(F32) * (sum_ref[...] - dhin_ref[...]), 1, keepdims=True)
+        cross_ref[...] = jnp.broadcast_to(jnp.sum(part, 0, keepdims=True), cross_ref.shape)
+
+
+def teacher_grad(teacher, turned, hidden, table, given, dh, grad):
     count, length, size = teacher.shape
     width, tokens = turned.shape
-    tile = tile_of(size)
+    tile = tile_of(size, tokens)
     whole = lambda *shape: pl.BlockSpec(shape, lambda j: (0, 0))
+    striped = pl.BlockSpec((width, tile), lambda j: (0, j))
     return pl.pallas_call(
         teacher_grad_kernel,
         grid=(size // tile,),
-        out_shape=[jax.ShapeDtypeStruct((tokens, width), F32), jax.ShapeDtypeStruct((width, size), F32)],
+        out_shape=[
+            jax.ShapeDtypeStruct((tokens, width), B16),
+            jax.ShapeDtypeStruct((width, size), B16),
+            jax.ShapeDtypeStruct((8, 128), F32),
+        ],
         in_specs=[
             pl.BlockSpec((count, length, tile), lambda j: (0, 0, j)),
-            whole(width, tokens),
-            pl.BlockSpec((width, tile), lambda j: (0, j)),
-            whole(tokens, 1),
-            whole(tokens, 1),
-            pl.BlockSpec((width, tile), lambda j: (0, j)),
+            whole(width, tokens), whole(tokens, width), striped, whole(tokens, 2), whole(tokens, width), striped,
         ],
-        out_specs=[whole(tokens, width), pl.BlockSpec((width, tile), lambda j: (0, j))],
+        out_specs=[whole(tokens, width), striped, whole(8, 128)],
+        scratch_shapes=[pltpu.VMEM((tokens, tile), B16), pltpu.VMEM((tokens, width), F32)],
         compiler_params=pltpu.CompilerParams(vmem_limit_bytes=60 * MIB),
-    )(teacher, turned, table, lse, weight, grad)
+    )(teacher, turned, hidden, table, given, dh, grad)
 
 
 def pick_kernel(block, ids_ref, table_ref, out_ref):
@@ -871,7 +954,7 @@
         )
         return carry
 
-    lax.fori_loop(0, ids_ref.shape[0] // block, one, 0)
+    lax.fori_loop(0, ids_ref.shape[0] // block, one, 0, unroll=True)
 
 
 def pick_rows(ids, table):
@@ -891,36 +974,8 @@
     )(ids, table)
 
 
-def spread_kernel(ids_ref, turned_ref, grad_ref, out_ref):
-    step = pl.program_id(0)
-    tile = grad_ref.shape[1]
-    count, _, length = turned_ref.shape
-
-    def one(k, total):
-        rows = pl.ds(pl.multiple_of(k * length, length), length)
-        lane = lax.broadcasted_iota(jnp.int32, (length, tile), 1)
-        hit = jnp.where(lane == ids_ref[rows, :] - step * tile, 1.0, 0.0).astype(B16)
-        return total + jnp.dot(turned_ref[k], hit, preferred_element_type=F32)
-
-    out_ref[...] = lax.fori_loop(0, count, one, grad_ref[...]).astype(B16)
-
-
-def spread_rows(ids, turned, grad):
-    tokens = ids.shape[0]
-    width, size = grad.shape
-    tile = tile_of(size)
-    return pl.pallas_call(
-        spread_kernel,
-        grid=(size // tile,),
-        out_shape=jax.ShapeDtypeStruct((width, size), B16),
-        in_specs=[
-            pl.BlockSpec((tokens, 1), lambda j: (0, 0)),
-            pl.BlockSpec(turned.shape, lambda j: (0, 0, 0)),
-            pl.BlockSpec((width, tile), lambda j: (0, j)),
-        ],
-        out_specs=pl.BlockSpec((width, tile), lambda j: (0, j)),
-        compiler_params=pltpu.CompilerParams(vmem_limit_bytes=48 * MIB),
-    )(ids, turned, grad)
+def mm(a, b, over=(1, 0)):
+    return lax.dot_general(a, b, (((over[0],), (over[1],)), ((), ())), preferred_element_type=F32)
 
 
 def norm_rows(values, gain, shift):
@@ -937,102 +992,222 @@
         - jnp.mean(scaled, -1, keepdims=True)
         - normed * jnp.mean(scaled * normed, -1, keepdims=True)
     )
-    return (inward, jnp.sum(grad * normed, 0), jnp.sum(grad, 0))
-
-
-def gelu_tanh(values):
-    return 0.5 * values * (1.0 + jnp.tanh(GELU_C * (values + 0.044715 * values * values * values)))
-
-
-def gelu_slope(values):
-    tangent = jnp.tanh(GELU_C * (values + 0.044715 * values * values * values))
-    return 0.5 * (1.0 + tangent) + 0.5 * values * (1.0 - tangent * tangent) * GELU_C * (
-        1.0 + 3.0 * 0.044715 * values * values
+    return (inward, jnp.sum(grad * normed, 0, keepdims=True), jnp.sum(grad, 0, keepdims=True))
+
+
+def gelu_both(values):
+    square = values * values
+    tangent = jnp.tanh(GELU_C * values * (1.0 + 0.044715 * square))
+    half = 0.5 * (1.0 + tangent)
+    slope = half + 0.5 * values * (1.0 - tangent * tangent) * (GELU_C * (1.0 + 3.0 * 0.044715 * square))
+    return values * half, slope
+
+
+def bias_of(segment_ref, bias_ref):
+    length = segment_ref.shape[1]
+    row = segment_ref[...]
+    column = jnp.broadcast_to(row, (128, length)).T[:, :1]
+    bias_ref[...] = jnp.where(column == row, 0.0, -1e30)
+    place = lax.broadcasted_iota(jnp.int32, (length, 1), 0)
+    for code in range(SEGS):
+        start = jnp.sum((row < code).astype(jnp.int32), 1, keepdims=True)
+        place = place - jnp.where(column == code, start, 0)
+    return place
+
+
+def softmax(queries, keys, bias):
+    scores = mm(queries, keys, (1, 1)) * 0.125 + bias
+    expd = jnp.exp(scores - jnp.max(scores, -1, keepdims=True))
+    return expd / jnp.sum(expd, -1, keepdims=True)
+
+
+def pair_of(ref, part, pair, width):
+    return ref[:, pl.ds(pl.multiple_of(part * width + pair * 128, 128), 128)]
+
+
+def layer_forward(x, weights, gains_ref, bias_ref, packed_ref, context_ref):
+    qkv_ref, out_ref, up_ref, down_ref = weights
+    length, width = x.shape
+    gain = lambda k: gains_ref[k : k + 1, :]
+    h_zero, normed_a, scaler_a = norm_rows(x, gain(0), gain(1))
+    packed_ref[...] = mm(h_zero.astype(B16), qkv_ref[...]).astype(B16)
+    low = lax.broadcasted_iota(jnp.int32, (length, 128), 1) < 64
+
+    def heads(pair, carry):
+        queries, keys, values = (pair_of(packed_ref, part, pair, width) for part in range(3))
+        none = jnp.zeros_like(queries)
+        parts = []
+        for picked in (jnp.where(low, queries, none), jnp.where(low, none, queries)):
+            parts.append(mm(softmax(picked, keys, bias_ref[...]).astype(B16), values))
+        context_ref[:, pl.ds(pl.multiple_of(pair * 128, 128), 128)] = jnp.where(low, *parts).astype(B16)
+        return carry
+
+    lax.fori_loop(0, width // 128, heads, 0)
+    h_one, normed_b, scaler_b = norm_rows(h_zero + mm(context_ref[...], out_ref[...]), gain(2), gain(3))
+    one_b = h_one.astype(B16)
+    total = h_one
+    chunk = 512
+    for c in range(up_ref.shape[1] // chunk):
+        part = slice(c * chunk, (c + 1) * chunk)
+        active = gelu_both(mm(one_b, up_ref[:, part]))[0].astype(B16)
+        total = total + mm(active, down_ref[part, :])
+    h_two, normed_c, scaler_c = norm_rows(total, gain(4), gain(5))
+    return h_two, (normed_a, normed_b, normed_c), (scaler_a, scaler_b, scaler_c)
+
+
+def teach_kernel(group_ref, x_ref, segment_ref, first_ref, second_ref, gains_ref, top_ref, bias_ref, packed_ref, context_ref):
+    width = x_ref.shape[2]
+    bias_of(segment_ref, bias_ref)
+    first, second = first_ref.at[0], second_ref.at[0]
+    weights = (first.at[:, : 3 * width], first.at[:, 3 * width : 4 * width], first.at[:, 4 * width :], second)
+    h_two, _, _ = layer_forward(
+        x_ref[0].astype(F32), weights, gains_ref.at[0], bias_ref, packed_ref, context_ref
     )
-
-
-def positions(segment):
-    codes = jnp.arange(SEGS, dtype=jnp.int32)
-    starts = jnp.sum((segment[None, :] < codes[:, None]).astype(jnp.int32), 1)
-    member = (segment[:, None] == codes[None, :]).astype(jnp.int32)
-    return jnp.arange(segment.shape[0], dtype=jnp.int32) - jnp.sum(member * starts[None, :], 1)
-
-
-def split_heads(packed):
-    width = packed.shape[1] // 3
-    return [packed[:, i * width : (i + 1) * width].reshape(packed.shape[0], -1, 64) for i in range(3)]
-
-
-def masked_scores(queries, keys, segment):
-    scores = jnp.einsum("qhd,khd->hqk", queries, keys, preferred_element_type=F32) * 0.125
-    return jnp.where((segment[:, None] == segment[None, :])[None], scores, -1e30)
-
-
-def attend(packed, segment):
-    queries, keys, values = split_heads(packed)
-    scores = masked_scores(queries, keys, segment)
-    top = jnp.max(scores, -1, keepdims=True)
-    expd = jnp.exp(scores - top)
-    total = jnp.sum(expd, -1, keepdims=True)
-    probs = (expd / total).astype(B16)
-    context = jnp.einsum("hqk,khd->qhd", probs, values, preferred_element_type=F32)
-    return context.reshape(packed.shape[0], -1).astype(B16), (top + jnp.log(total))[..., 0]
-
-
-def attend_back(packed, segment, lse, dcontext):
-    queries, keys, values = split_heads(packed)
-    length = packed.shape[0]
-    grads = dcontext.reshape(queries.shape)
-    probs = jnp.exp(masked_scores(queries, keys, segment) - lse[..., None])
-    dprobs = jnp.einsum("qhd,khd->hqk", grads, values, preferred_element_type=F32)
-    inner = jnp.sum(probs * dprobs, -1, keepdims=True)
-    dscore = (probs * (dprobs - inner) * 0.125).astype(B16)
-    parts = (
-        jnp.einsum("hqk,khd->qhd", dscore, keys, preferred_element_type=F32),
-        jnp.einsum("hqk,qhd->khd", dscore, queries, preferred_element_type=F32),
-        jnp.einsum("hqk,qhd->khd", probs.astype(B16), grads, preferred_element_type=F32),
-    )
-    return jnp.concatenate([p.reshape(length, -1) for p in parts], 1)
-
-
-def layer_forward(hidden, segment, weights, gains):
-    qkv_t, out_t, up_t, down_t = weights
-    h_zero, normed_a, scaler_a = norm_rows(hidden, gains[0], gains[1])
-    zero_b = h_zero.astype(B16)
-    packed = jnp.dot(zero_b, qkv_t, preferred_element_type=F32).astype(B16)
-    context_b, lse = attend(packed, segment)
-    h_one, normed_b, scaler_b = norm_rows(
-        h_zero + jnp.dot(context_b, out_t, preferred_element_type=F32), gains[2], gains[3]
-    )
-    one_b = h_one.astype(B16)
-    inner = jnp.dot(one_b, up_t, preferred_element_type=F32)
-    active = gelu_tanh(inner).astype(B16)
-    h_two, normed_c, scaler_c = norm_rows(
-        h_one + jnp.dot(active, down_t, preferred_element_type=F32), gains[4], gains[5]
-    )
-    kept = (normed_a, scaler_a, zero_b, packed, lse, context_b, normed_b, scaler_b, one_b, inner, active, normed_c, scaler_c)
-    return (kept, h_two)
-
-
-def layer_backward(dtwo, segment, weights, gains, kept):
-    qkv_t, out_t, up_t, down_t = weights
-    (normed_a, scaler_a, zero_b, packed, lse, context_b, normed_b, scaler_b, one_b, inner, active, normed_c, scaler_c) = kept
-    dz_two, gain_c, shift_c = norm_back(dtwo, normed_c, scaler_c, gains[4])
+    top_ref[...] = h_two.astype(B16)
+
+
+def teach(group, x, segment, first, second, gains):
+    _, length, width = x.shape
+    chosen = lambda shape: pl.BlockSpec((1,) + shape[1:], lambda i, g: (g[0], 0, 0))
+    return pl.pallas_call(
+        teach_kernel,
+        grid_spec=pltpu.PrefetchScalarGridSpec(
+            num_scalar_prefetch=1,
+            grid=(1,),
+            in_specs=[
+                pl.BlockSpec((1, length, width), lambda i, g: (0, 0, 0)),
+                pl.BlockSpec((1, length), lambda i, g: (0, 0)),
+                chosen(first.shape),
+                chosen(second.shape),
+                chosen(gains.shape),
+            ],
+            out_specs=pl.BlockSpec((length, width), lambda i, g: (0, 0)),
+            scratch_shapes=[
+                pltpu.VMEM((length, length), F32),
+                pltpu.VMEM((length, 3 * width), B16),
+                pltpu.VMEM((length, width), B16),
+            ],
+        ),
+        out_shape=jax.ShapeDtypeStruct((length, width), B16),
+        compiler_params=pltpu.CompilerParams(vmem_limit_bytes=60 * MIB),
+    )(group, x, segment, first, second, gains)
+
+
+def learn_kernel(
+    rows_ref, segment_ref, pos_ref, attention_ref, up_ref, down_ref, gains_ref,
+    top_ref, na_ref, nb_ref, nc_ref, scalers_ref, packed_ref, context_ref, bias_ref,
+):
+    length, width = rows_ref.shape
+    place = bias_of(segment_ref, bias_ref)
+    lane = lax.broadcasted_iota(jnp.int32, (length, pos_ref.shape[0]), 1)
+    onehot = jnp.where(lane == place, 1.0, 0.0).astype(B16)
+    x = rows_ref[...] + mm(onehot, pos_ref[...])
+    weights = (attention_ref.at[:, : 3 * width], attention_ref.at[:, 3 * width :], up_ref, down_ref)
+    h_two, normed, scalers = layer_forward(x, weights, gains_ref, bias_ref, packed_ref, context_ref)
+    top_ref[...] = h_two.astype(B16)
+    for ref, value in zip((na_ref, nb_ref, nc_ref), normed):
+        ref[...] = value
+    lane = lax.broadcasted_iota(jnp.int32, (length, 128), 1)
+    scalers_ref[...] = jnp.where(lane == 0, scalers[0], jnp.where(lane == 1, scalers[1], scalers[2]))
+
+
+def learn(rows, segment, pos, attention, up, down, gains):
+    length, width = rows.shape
+    square = jax.ShapeDtypeStruct((length, width), F32)
+    half = jax.ShapeDtypeStruct((length, width), B16)
+    return pl.pallas_call(
+        learn_kernel,
+        in_specs=[IN_VMEM] * 7,
+        out_specs=[IN_VMEM] * 7,
+        out_shape=[
+            half, square, square, square,
+            jax.ShapeDtypeStruct((length, 128), F32),
+            jax.ShapeDtypeStruct((length, 3 * width), B16),
+            half,
+        ],
+        scratch_shapes=[pltpu.VMEM((length, length), F32)],
+        compiler_params=pltpu.CompilerParams(vmem_limit_bytes=56 * MIB),
+    )(rows, segment, pos, attention, up, down, gains)
+
+
+def back_kernel(
+    dtwo_ref, segment_ref, attention_ref, up_ref, down_ref, gains_ref,
+    na_ref, nb_ref, nc_ref, scalers_ref, packed_ref, context_ref,
+    dx_ref, dattention_ref, dup_ref, ddown_ref, dpos_ref, dgains_ref, bias_ref, dpacked_ref, dcontext_ref,
+):
+    length, width = dtwo_ref.shape
+    gain = lambda k: gains_ref[k : k + 1, :]
+    place = bias_of(segment_ref, bias_ref)
+    dz_two, gain_c, shift_c = norm_back(dtwo_ref[...], nc_ref[...], scalers_ref[:, 2:3], gain(4))
     dbranch = dz_two.astype(B16)
-    grad_down = jnp.einsum("nf,nd->fd", active, dbranch, preferred_element_type=F32)
-    dinner = (jnp.dot(dbranch, down_t.T, preferred_element_type=F32) * gelu_slope(inner)).astype(B16)
-    grad_up = jnp.einsum("nd,nf->df", one_b, dinner, preferred_element_type=F32)
-    dh_one = dz_two + jnp.dot(dinner, up_t.T, preferred_element_type=F32)
-    dz_one, gain_b, shift_b = norm_back(dh_one, normed_b, scaler_b, gains[2])
+    one_b = (nb_ref[...] * gain(2) + gain(3)).astype(B16)
+    dh_one = dz_two
+    chunk = 512
+    for c in range(up_ref.shape[1] // chunk):
+        part = slice(c * chunk, (c + 1) * chunk)
+        active, slope = gelu_both(mm(one_b, up_ref[:, part]))
+        ddown_ref[part, :] = mm(active.astype(B16), dbranch, (0, 0)).astype(B16)
+        dinner = (mm(dbranch, down_ref[part, :], (1, 1)) * slope).astype(B16)
+        dup_ref[:, part] = mm(one_b, dinner, (0, 0)).astype(B16)
+        dh_one = dh_one + mm(dinner, up_ref[:, part], (1, 1))
+    dz_one, gain_b, shift_b = norm_back(dh_one, nb_ref[...], scalers_ref[:, 1:2], gain(2))
     dproj = dz_one.astype(B16)
-    grad_out = jnp.einsum("nc,nd->cd", context_b, dproj, preferred_element_type=F32)
-    dcontext = jnp.dot(dproj, out_t.T, preferred_element_type=F32).astype(B16)
-    dpacked = attend_back(packed, segment, lse, dcontext).astype(B16)
-    grad_qkv = jnp.einsum("nd,ne->de", zero_b, dpacked, preferred_element_type=F32)
-    dh_zero = dz_one + jnp.dot(dpacked, qkv_t.T, preferred_element_type=F32)
-    dhidden, gain_a, shift_a = norm_back(dh_zero, normed_a, scaler_a, gains[0])
-    grad_gains = jnp.stack([gain_a, shift_a, gain_b, shift_b, gain_c, shift_c])
-    return (dhidden, (grad_qkv, grad_out, grad_up, grad_down), grad_gains)
+    dattention_ref[:, 3 * width :] = mm(context_ref[...], dproj, (0, 0)).astype(B16)
+    dcontext_ref[...] = mm(dproj, attention_ref[:, 3 * width :], (1, 1)).astype(B16)
+    low = lax.broadcasted_iota(jnp.int32, (length, 128), 1) < 64
+
+    def heads(pair, carry):
+        queries, keys, values = (pair_of(packed_ref, part, pair, width) for part in range(3))
+        grads = pair_of(dcontext_ref, 0, pair, width)
+        none = jnp.zeros_like(queries)
+        parts = []
+        for first in (True, False):
+            pick = lambda a: jnp.where(low, a, none) if first else jnp.where(low, none, a)
+            probs = softmax(pick(queries), keys, bias_ref[...])
+            dprobs = mm(pick(grads), values, (1, 1))
+            inner = jnp.sum(probs * dprobs, -1, keepdims=True)
+            dscore = (probs * (dprobs - inner) * 0.125).astype(B16)
+            parts.append(
+                (mm(dscore, keys), mm(dscore, queries, (0, 0)), mm(probs.astype(B16), grads, (0, 0)))
+            )
+        for part in range(3):
+            columns = pl.ds(pl.multiple_of(part * width + pair * 128, 128), 128)
+            dpacked_ref[:, columns] = jnp.where(low, parts[0][part], parts[1][part]).astype(B16)
+        return carry
+
+    lax.fori_loop(0, width // 128, heads, 0)
+    zero_b = (na_ref[...] * gain(0) + gain(1)).astype(B16)
+    dattention_ref[:, : 3 * width] = mm(zero_b, dpacked_ref[...], (0, 0)).astype(B16)
+    dh_zero = dz_one + mm(dpacked_ref[...], attention_ref[:, : 3 * width], (1, 1))
+    dx, gain_a, shift_a = norm_back(dh_zero, na_ref[...], scalers_ref[:, 0:1], gain(0))
+    dx_b = dx.astype(B16)
+    lane = lax.broadcasted_iota(jnp.int32, (length, dpos_ref.shape[0]), 1)
+    onehot = jnp.where(lane == place, 1.0, 0.0).astype(B16)
+    dpos_ref[...] = mm(onehot, dx_b, (0, 0)).astype(B16)
+    dx_ref[...] = dx_b.T
+    for k, row in enumerate((gain_a, shift_a, gain_b, shift_b, gain_c, shift_c)):
+        dgains_ref[k : k + 1, :] = row
+
+
+def back(dtwo, segment, pos_count, attention, up, down, gains, kept):
+    length, width = dtwo.shape
+    inputs = (dtwo, segment, attention, up, down, gains) + tuple(kept)
+    half = lambda *shape: jax.ShapeDtypeStruct(shape, B16)
+    return pl.pallas_call(
+        back_kernel,
+        in_specs=[IN_VMEM] * len(inputs),
+        out_specs=[IN_VMEM] * 6,
+        out_shape=[
+            half(width, length), half(*attention.shape), half(*up.shape), half(*down.shape),
+            half(pos_count, width), jax.ShapeDtypeStruct(gains.shape, F32),
+        ],
+        scratch_shapes=[
+            pltpu.VMEM((length, length), F32),
+            pltpu.VMEM((length, 3 * width), B16),
+            pltpu.VMEM((length, width), B16),
+        ],
+        compiler_params=pltpu.CompilerParams(vmem_limit_bytes=60 * MIB),
+    )(*inputs)
 
 
 def adam(weight, first, second, grad, fix_one, fix_two, rate):
@@ -1053,7 +1228,6 @@
     slice_len, columns = embed_w.shape
     width = gains_w.shape[1]
     d, v = lax.axis_index("dp"), lax.axis_index("vocab")
-    segment = segment_ids[0]
 
     turned_table = embed_w.astype(B16).T.reshape(2, columns // 2, slice_len)
     attention = jnp.concatenate([qkv_w, out_w], 1).astype(B16)[None]
@@ -1070,9 +1244,7 @@
     )
     table = table.reshape(width, slice_len)
     attention = attention.reshape(width, -1)
-    qkv_t, out_t = attention[:, : 3 * width], attention[:, 3 * width :]
     up_t, down_t, pos_t = up_t.reshape(width, -1), down_t.reshape(-1, width), pos_t.reshape(-1, width)
-    weights = (qkv_t, out_t, up_t, down_t)
     integers = integers.reshape(D, V, 8, length)
     counted = jnp.maximum(jnp.sum(integers[:, :, 2].astype(F32)), 1.0)
     group_ints = lax.dynamic_index_in_dim(integers, d, 0, False)
@@ -1084,11 +1256,7 @@
 
     picked = pick_rows(ids_here, table).astype(B16).reshape(V, length, width)
     embedded = vocab_scatter(V, picked, 2)
-    places = positions(segment)
-    onehot = (places[:, None] == jnp.arange(pos_t.shape[0], dtype=jnp.int32)[None, :]).astype(B16)
-    hidden = embedded + jnp.dot(onehot, pos_t, preferred_element_type=F32)
-    kept, h_two = layer_forward(hidden, segment, weights, gains_w)
-    two_b = h_two.astype(B16)
+    two_b, *kept = learn(embedded, segment_ids, pos_t, attention, up_t, down_t, gains_w)
 
     weight = counts / counted
     given = jnp.concatenate([weight[:, None], labels_here.astype(F32)], 1)
@@ -1097,14 +1265,11 @@
         D, V, first, teacher_down, two_b, table, given, 4
     )
     student_lse, picked = told[0], told[1]
-    mine = teacher_group[0]
-    tw = teacher_qkv.shape[2] // 3
-    first = lax.dynamic_index_in_dim(first, mine, 0, False).reshape(tw, -1)
-    second = lax.dynamic_index_in_dim(second, mine, 0, False).reshape(-1, tw)
-    chosen = (first[:, : 3 * tw], first[:, 3 * tw : 4 * tw], first[:, 4 * tw :], second)
-    gains_row = lax.dynamic_index_in_dim(teacher_gains, mine, 0, False)
-    _, teacher_top = layer_forward(teacher_inputs[0].astype(F32), segment, chosen, gains_row)
-    (teacher_hidden,) = vocab_gather(V, [teacher_top.astype(B16)], 5)
+    tw = teacher_gains.shape[2]
+    top = teach(
+        teacher_group, teacher_inputs, segment_ids, first.reshape(3, tw, -1), second.reshape(3, -1, tw), teacher_gains
+    )
+    (teacher_hidden,) = vocab_gather(V, [top], 5)
 
     teacher, stats = teacher_stats(groups, teacher_hidden, teacher_table)
     stats = lax.all_gather(stats, "vocab")
@@ -1113,39 +1278,25 @@
     tsum = jnp.sum(stats[:, 1] * scale, 0)
     tcross = jnp.sum(stats[:, 2] * scale, 0) / tsum
     teacher_lse = top + jnp.log(tsum)
-    dh_teacher, grad_head = teacher_grad(
-        teacher, turned, table, teacher_lse[:, None], weight[:, None], grad_head
+    given = jnp.concatenate([weight[:, None], teacher_lse[:, None]], 1)
+    dh, grad_head, cross = teacher_grad(teacher, turned, hidden_all, table, given, dh_student, grad_head)
+    once = jnp.sum(weight * (MIX_ALPHA * (tcross - teacher_lse + student_lse) + student_lse))
+    loss_part = cross[0, 0] - jnp.sum(weight * picked) + jnp.where(v == 0, once, 0.0)
+
+    dtwo = vocab_scatter(V, dh.reshape(V, length, width), 6)
+    turned_dx, grad_attention, grad_up, grad_down, grad_pos, grad_gains = back(
+        dtwo, segment_ids, pos_t.shape[0], attention, up_t, down_t, gains_w, kept
     )
-    everywhere = jnp.sum(hidden_all.astype(F32) * dh_teacher) - jnp.sum(weight * picked)
-    once = jnp.sum(weight * (MIX_ALPHA * (tcross - teacher_lse + student_lse) + student_lse))
-    loss_part = everywhere + jnp.where(v == 0, once, 0.0)
-
-    dtwo = vocab_scatter(V, (dh_student + dh_teacher).astype(B16).reshape(V, length, width), 6)
-    dhidden, dense_grads, grad_gains = layer_backward(dtwo, segment, weights, gains_w, kept)
-    dhidden_b = dhidden.astype(B16)
-    grad_pos = lax.dot_general(onehot, dhidden_b, (((0,), (0,)), ((), ())), preferred_element_type=F32)
-    (turned_grads,) = vocab_gather(V, [dhidden_b.T], 7)
-    grad_embed = spread_rows(ids_here, turned_grads, grad_head)
-
-    grad_qkv, grad_out, grad_up, grad_down = dense_grads
-    owners = lambda g: g.astype(B16).reshape(D * V // 2, 2, -1, g.shape[1])
-    grad_embed = grad_embed.reshape(D, 2, columns // 2, slice_len)
-    sums = ring_scatter(
-        D, V,
-        [grad_embed[:, 0], grad_embed[:, 1], owners(jnp.concatenate([grad_qkv, grad_out], 1)), owners(grad_up),
-         owners(grad_down), owners(grad_pos)],
-        (("dp", 0), ("dp", 1), (0, 0), (1, 1), (2, 0), (1, 0)),
-        8,
+
+    lane = lax.broadcasted_iota(jnp.int32, (2, width), 1)
+    scalars = jnp.where(lane == 1, loss_part, 0.0)
+    owners = lambda g: g.reshape(D * V // 2, 2, -1, g.shape[1])
+    grad_embed, totals, owned_attention, owned_up, owned_down, owned_pos = settle(
+        D, V, grad_head, turned_dx, ids_here, jnp.concatenate([grad_gains, scalars], 0),
+        [owners(grad_attention), owners(grad_up), owners(grad_down), owners(grad_pos)], (0, 1, 2, 1), 7,
     )
-    grad_embed = jnp.concatenate(sums[:2], 0)
-    owned = (sums[5], sums[2][:, : 3 * width], sums[2][:, 3 * width :], sums[3], sums[4])
-    squares = jnp.sum(grad_embed * grad_embed)
-    for grad in (sums[2], sums[3], sums[4], sums[5]):
-        squares = squares + jnp.sum(grad * grad)
-    lane = lax.broadcasted_iota(jnp.int32, (2, width), 1)
-    scalars = jnp.where(lane == 0, squares, jnp.where(lane == 1, loss_part, 0.0))
-    totals = total_all(D, V, jnp.concatenate([grad_gains, scalars], 0), 9)
-    gains_grad, squares, loss = totals[:6], totals[6, 0], totals[6, 1]
+    owned = (owned_pos, owned_attention[:, : 3 * width], owned_attention[:, 3 * width :], owned_up, owned_down)
+    gains_grad, squares, loss = totals[:6], totals[7, 0], totals[7, 1]
 
     grad_norm = jnp.sqrt(squares + jnp.sum(gains_grad * gains_grad))
     factor = CLIP_NORM / jnp.maximum(grad_norm, CLIP_NORM)

time: 924 us -> 740 us (0.80)
  matrix products: 107 us -> 0 us
  local copies, waits for them, and re-layouts: 57.7 us -> 13.2 us
  other arithmetic: 64.1 us -> 26.4 us
  Pallas kernels: 665 us -> 679 us
    dot_general x24 -> x0, matrix products: 96.8 us -> none  [the longest x1 14.7 us: attend_back(): jnp.einsum('hqk,qhd->khd', dscore, queries, preferred_element_type=F32)]
    pallas_call x3 -> x4, Pallas kernels: 160 us -> 209 us  [the longest x1 142 us: settle(): pl.pallas_call(functools.partial(settle_kernel, D, V, rings), out_shape=[...]
    reduce_sum x18 -> x0, other arithmetic: 26.2 us -> none  [the longest x1 7.25 us: on_device(): jnp.sum(hidden_all.astype(F32) * dh_teacher) - jnp.sum(weight * picked)]
    pallas_call x2 -> x1, Pallas kernels: 45 us -> 26.8 us  [vocab_gather(): pl.pallas_call(functools.partial(vocab_gather_kernel, V, count), out_shap...]
    slice x11 -> x2, local copies, waits for them, and re-layouts: 16.1 us -> 2.61 us  [the longest x1 1.41 us: on_device(): gains_grad, squares, loss = (totals[:6], totals[7, 0], totals[7, 1])]
    dynamic_slice x2 -> x0, local copies, waits for them, and re-layouts: 13.4 us -> none  [the longest x1 8.58 us: on_device(): first = lax.dynamic_index_in_dim(first, mine, 0, False).reshape(tw, -1)]
    sub x1 -> x0, matrix products: 10.6 us -> none  [attend(): expd = jnp.exp(scores - top)]
where the time goes in v3:
time: 740 us; the launch traced here: 733 us
  Pallas kernels  679 us (92%)
  other arithmetic  26.4 us (4%)
  local copies, waits for them, and re-layouts  13.2 us (2%)
  between operations  8.12 us (1%)
    pallas_call x1, Pallas kernels, study(): pl.pallas_call(functools.partial(study_kernel, D, V, spec), out_shape=sha...  189 us
    pallas_call x1, Pallas kernels, settle(): pl.pallas_call(functools.partial(settle_kernel, D, V, rings), out_shape=[...  142 us
    pallas_call x1, Pallas kernels, ring_gather(): pl.pallas_call(functools.partial(gather_kernel, D, V, spec, len(arrays)),...  114 us
    pallas_call x1, Pallas kernels, teacher_grad(): pl.pallas_call(teacher_grad_kernel, grid=(size // tile,), out_shape=[jax....  45.8 us
    pallas_call x1, Pallas kernels, teacher_stats(): pl.pallas_call(teacher_stats_kernel, grid_spec=pltpu.PrefetchScalarGridSp...  40.5 us
    pallas_call x2, Pallas kernels, vocab_scatter(): pl.pallas_call(functools.partial(vocab_scatter_kernel, V), out_shape=jax....  34.3 us
    pallas_call x1, Pallas kernels, vocab_gather(): pl.pallas_call(functools.partial(vocab_gather_kernel, V, count), out_shap...  26.8 us
    pallas_call x1, Pallas kernels, back(): pl.pallas_call(back_kernel, in_specs=[IN_VMEM] * len(inputs), out_specs=[...  26.7 us

profile of v3, /device:TPU:0, one launch (start us, length us, event | category | flops | bytes accessed | tf_op | source)
XLA Modules:
  0.0 732.9 jit_solution(9544384282873712490)
XLA Ops:
  2.8 2.6 convert_element_type.57
  7.9 114.2 %shard_map.497 = (bf16[8,2,32,7680]{3,2,1,0:T(8,128)(2,1)}, bf16[1,32,16,2048]{3,2,1,0:T(8,128)(2,1)}, bf16[1,32,16,2048]{3,2,1,0:T(8,128)(2,1)}, bf16[1,32,64,5...) custom-call(bf16[2,32,7680]{2,1,0:T(8,128)(2,1)} %bitcast.100, ...), custom_call_target="tpu_custom_call" | custom-call | tf_op jit(solution)/shard_map/pallas_call | solution.py:239
  123.4 19.6 %shard_map.498 = f32[2048,512]{1,0:T(8,128)S(1)} custom-call(s32[2048,1]{1,0:T(8,128)S(1)} %bitcast.85, bf16[512,7680]{1,0:T(8,128)(2,1)} %bitcast.89), custom_call_target="tpu_custom_call" | custom-call | tf_op jit(solution)/shard_map/pallas_call | solution.py:964
  143.3 17.2 %shard_map.499.rows_ref = f32[512,512]{1,0:T(8,128)S(1)} custom-call(bf16[2,2,512,512]{3,2,1,0:T(8,128)(2,1)S(1)} %bitcast.87), custom_call_target="tpu_custom_call" | custom-call | tf_op jit(solution)/shard_map/pallas_call | solution.py:623
  161.5 16.0 %shard_map.500 = (bf16[512,512]{1,0:T(8,128)(2,1)}, f32[512,512]{1,0:T(8,128)}, f32[512,512]{1,0:T(8,128)}, f32[512,512]{1,0:T(8,128)}, f32[512,128]{1,0:T(8,128...) custom-call(f32[512,512]{1,0:T(8,128)} %copy-done.1, s32[1,512]{1,0:T(1,128)} %segment_ref.5, ...), custom_call_target="tpu_custom_call" | custom-call | tf_op jit(solution)/shard_map/pallas_call | solution.py:1118
  177.5 1.8 fusion.5
  180.0 1.3 copy.85.refs_4_
  182.4 188.9 %shard_map.501 = (bf16[3,32,24,6144]{3,2,1,0:T(8,128)(2,1)}, bf16[3,32,96,768]{3,2,1,0:T(8,128)(2,1)}, bf16[2048,512]{1,0:T(8,128)(2,1)}, bf16[512,2048]{1,0:T(8...) custom-call(bf16[3,24,6144]{2,1,0:T(8,128)(2,1)} %pad_maximum_fusion.refs_0_, ...), custom_call_target="tpu_custom_call" | custom-call | tf_op jit(solution)/shard_map/pallas_call | solution.py:805
  371.2 24.5 %shard_map.502.refs_0_ = bf16[512,768]{1,0:T(8,128)(2,1)} custom-call(s32[1]{0:T(128)} %copy.116.group_ref, bf16[1,512,768]{2,1,0:T(8,128)(2,1)} %x_ref.1, s32[1,512]{1,0:T(1,128)} %segment_ref.5, bf16[3,768,6144]{2,1,0:T(8,128)(2,1)} %bitcast.92, bf16[3,3072,768]{2,1,0:T(8,128)(2,1)} %bitcast.93, f32[3,6,768]{2,1,0:T(8,128)} %gains_ref.4), custom_call_target="tpu_custom_call" | custom-call | tf_op jit(solution)/shard_map/pallas_call | solution.py:1072
  395.7 26.8 %shard_map.503.hidden_ref = bf16[4,512,768]{2,1,0:T(8,128)(2,1)} custom-call(bf16[512,768]{1,0:T(8,128)(2,1)} %shard_map.502.refs_0_), custom_call_target="tpu_custom_call" | custom-call | tf_op jit(solution)/shard_map/pallas_call | solution.py:562
  423.2 40.5 %shard_map.504 = (bf16[4,512,7680]{2,1,0:T(8,128)(2,1)}, f32[8,2048]{1,0:T(8,128)}) custom-call(s32[4]{0:T(128)} %slice_reduce_fusion.1.group_ref, bf16[4,512,768]{2,1,0:T(8,128)(2,1)} %shard_map.503.hidden_ref, bf16[3,768,7680]{2,1,0:T(8,128)(2,1)} %table_ref.1), custom_call_target="tpu_custom_call" | custom-call | tf_op jit(solution)/shard_map/pallas_call | solution.py:864
  463.7 6.0 all-gather
  473.4 45.8 %shard_map.505 = (bf16[2048,512]{1,0:T(8,128)(2,1)}, bf16[512,7680]{1,0:T(8,128)(2,1)}, f32[8,128]{1,0:T(8,128)}) custom-call(bf16[4,512,7680]{2,1,0:T(8,128)(2,1)} %get-tuple-element.69.teacher_ref, bf16[512,2048]{1,0:T(8,128)(2,1)} %get-tuple-element.70.turned_ref, bf16[2048,512]{1,0:T(8,128)(2,1)} %get-tuple-element.71.hidden_ref, ...), custom_call_target="tpu_custom_call" | custom-call | tf_op jit(solution)/shard_map/pallas_call | solution.py:922
  522.4 1.6 copy-done.3
  524.0 17.1 %shard_map.506.dtwo_ref = f32[512,512]{1,0:T(8,128)S(1)} custom-call(bf16[2,2,512,512]{3,2,1,0:T(8,128)(2,1)S(1)} %bitcast.88), custom_call_target="tpu_custom_call" | custom-call | tf_op jit(solution)/shard_map/pallas_call | solution.py:623
  542.1 26.7 %shard_map.507 = (bf16[512,512]{1,0:T(8,128)(2,1)}, bf16[512,2048]{1,0:T(8,128)(2,1)}, bf16[512,2048]{1,0:T(8,128)(2,1)}, bf16[2048,512]{1,0:T(8,128)(2,1)}, bf16[512,512]{1,0:T(8,128)(2,1)}, /*index=5*/f32[6,512]{1,0:T(8,128)}) custom-call(f32[512,512]{1,0:T(8,128)} %copy-done.2, s32[1,512]{1,0:T(1,128)} %segment_ref.5, bf16[512,2048]{1,0:T(8,128)(2,1)} %bitcast.95, ...), custom_call_target="tpu_custom_call" | custom-call | tf_op jit(solution)/shard_map/pallas_call | solution.py:1196
  570.2 142.0 %shard_map.508 = (f32[64,7680]{1,0:T(8,128)}, f32[8,512]{1,0:T(8,128)}, f32[16,2048]{1,0:T(8,128)}, f32[16,2048]{1,0:T(8,128)}, f32[64,512]{1,0:T(8,128)}, /*index=5*/f32[16,512]{1,0:T(8,128)}) custom-call(bf16[512,7680]{1,0:T(8,128)(2,1)} %get-tuple-element.75.refs_0_, bf16[512,512]{1,0:T(8,128)(2,1)} %get-tuple-element.83.refs_1_, s32[2048,1]{1,0:T(8,128)} %bitcast.86, ...), custom_call_target="tpu_custom_call" | custom-call | tf_op jit(solution)/shard_map/pallas_call | solution.py:479
  712.3 1.4 fusion.30
  717.2 1.4 multiply_subtract_fusion.6
  718.5 1.7 multiply_subtract_fusion.1
  720.2 1.7 multiply_subtract_fusion.2
  721.9 1.6 multiply_subtract_fusion.3
  723.6 1.5 multiply_subtract_fusion.4
  725.1 6.3 multiply_subtract_fusion
  (90 shorter events, 16.7 us)
Async XLA Ops:
  0.7 4.7 copy-start.8
  0.7 4.7 copy-start.11
  0.7 5.4 copy-start.5
  0.7 6.0 copy-start.6
  0.7 6.6 copy-start.12
  123.4 19.6 %copy-start = (s32[1,2048]{0,1:T(8,128)}, s32[1,2048]{0,1:T(8,128)S(1)}, u32[]{:S(2)}) copy-start(s32[1,2048]{0,1:T(8,128)S(1)} %copy.95) | copy-start | bytes 24580
  161.5 19.9 %copy-start.7 = (bf16[3,24,3072]{2,1,0:T(8,128)(2,1)S(1)}, bf16[3,24,3072]{2,1,0:T(8,128)(2,1)}, u32[]{:S(2)}) copy-start(bf16[3,24,3072]{2,1,0:T(8,128)(2,1)} %param.43) | copy-start | bytes 1327108
  161.5 19.9 %copy-start.9 = (bf16[3,24,2304]{2,1,0:T(8,128)(2,1)S(1)}, bf16[3,24,2304]{2,1,0:T(8,128)(2,1)}, u32[]{:S(2)}) copy-start(bf16[3,24,2304]{2,1,0:T(8,128)(2,1)} %param.41) | copy-start | bytes 995332
  161.5 19.9 %copy-start.17 = (bf16[3,24,768]{2,1,0:T(8,128)(2,1)S(1)}, bf16[3,24,768]{2,1,0:T(8,128)(2,1)}, u32[]{:S(2)}) copy-start(bf16[3,24,768]{2,1,0:T(8,128)(2,1)} %param.42) | copy-start | bytes 331780
  570.1 147.0 %copy-start.10 = (f32[6,512]{1,0:T(8,128)S(1)}, f32[6,512]{1,0:T(8,128)}, u32[]{:S(2)}) copy-start(f32[6,512]{1,0:T(8,128)} %gains_ref.5) | copy-start | bytes 36868
  570.1 147.1 %copy-start.25 = (f32[6,512]{1,0:T(8,128)S(1)}, f32[6,512]{1,0:T(8,128)}, u32[]{:S(2)}) copy-start(f32[6,512]{1,0:T(8,128)} %param.67) | copy-start | bytes 36868
  570.1 147.1 %copy-start.26 = (f32[6,512]{1,0:T(8,128)S(1)}, f32[6,512]{1,0:T(8,128)}, u32[]{:S(2)}) copy-start(f32[6,512]{1,0:T(8,128)} %param.66) | copy-start | bytes 36868
  570.1 148.4 %copy-start.13 = (f32[64,512]{1,0:T(8,128)S(1)}, f32[64,512]{1,0:T(8,128)}, u32[]{:S(2)}) copy-start(f32[64,512]{1,0:T(8,128)} %param.64) | copy-start | bytes 393220
  570.1 148.4 %copy-start.14 = (f32[64,512]{1,0:T(8,128)S(1)}, f32[64,512]{1,0:T(8,128)}, u32[]{:S(2)}) copy-start(f32[64,512]{1,0:T(8,128)} %param.63) | copy-start | bytes 393220
  570.1 150.1 %copy-start.15 = (f32[16,2048]{1,0:T(8,128)S(1)}, f32[16,2048]{1,0:T(8,128)}, u32[]{:S(2)}) copy-start(f32[16,2048]{1,0:T(8,128)} %param.61) | copy-start | bytes 393220
  570.1 150.1 %copy-start.16 = (f32[16,2048]{1,0:T(8,128)S(1)}, f32[16,2048]{1,0:T(8,128)}, u32[]{:S(2)}) copy-start(f32[16,2048]{1,0:T(8,128)} %param.60) | copy-start | bytes 393220
  570.2 151.8 %copy-start.18 = (f32[16,1536]{1,0:T(8,128)S(1)}, f32[16,1536]{1,0:T(8,128)}, u32[]{:S(2)}) copy-start(f32[16,1536]{1,0:T(8,128)} %param.55) | copy-start | bytes 294916
  570.2 151.8 %copy-start.19 = (f32[16,1536]{1,0:T(8,128)S(1)}, f32[16,1536]{1,0:T(8,128)}, u32[]{:S(2)}) copy-start(f32[16,1536]{1,0:T(8,128)} %param.54) | copy-start | bytes 294916
  712.2 11.4 %copy-start.20 = (f32[16,512]{1,0:T(8,128)S(1)}, f32[16,512]{1,0:T(8,128)}, u32[]{:S(2)}) copy-start(f32[16,512]{1,0:T(8,128)} %param.58) | copy-start | bytes 98308
  712.2 11.4 %copy-start.21 = (f32[16,512]{1,0:T(8,128)S(1)}, f32[16,512]{1,0:T(8,128)}, u32[]{:S(2)}) copy-start(f32[16,512]{1,0:T(8,128)} %param.57) | copy-start | bytes 98308
  712.2 11.3 %copy-start.22 = (f32[16,512]{1,0:T(8,128)S(1)}, f32[16,512]{1,0:T(8,128)}, u32[]{:S(2)}) copy-start(f32[16,512]{1,0:T(8,128)} %param.52) | copy-start | bytes 98308
  712.3 11.3 %copy-start.23 = (f32[16,512]{1,0:T(8,128)S(1)}, f32[16,512]{1,0:T(8,128)}, u32[]{:S(2)}) copy-start(f32[16,512]{1,0:T(8,128)} %param.51) | copy-start | bytes 98308
  712.3 11.3 %copy-start.24 = (f32[16,512]{1,0:T(8,128)S(1)}, f32[16,512]{1,0:T(8,128)}, u32[]{:S(2)}) copy-start(f32[16,512]{1,0:T(8,128)} %get-tuple-element.93) | copy-start | bytes 98308
  712.3 12.8 %copy-start.4 = (f32[7680,64]{0,1:T(8,128)S(1)}, f32[7680,64]{0,1:T(8,128)}, u32[]{:S(2)}) copy-start(f32[7680,64]{0,1:T(8,128)} %param.47) | copy-start | bytes 5898244
  (3 other events, 3.5 us)

commit v4 on v3

--- a/solution.py
+++ b/solution.py
@@ -93,7 +93,7 @@
 
 
 class Gather:
-    def __init__(self, D, V, spec, ins, outs, sems):
+    def __init__(self, D, V, spec, ins, outs, sems, staggered=False):
         self.spec, self.ins, self.outs = spec, ins, outs
         self.ssem, self.rsem, self.xssem, self.xrsem, self.lsem = sems
         rings = {w: Ring(D, V, w) for w in dict.fromkeys(p[3] for p in spec)}
@@ -111,6 +111,8 @@
         self.longest = max(s[3] for s in self.streams)
         most = {w: max(r.hops(0)) for w, r in rings.items()}
         self.every = {w: max(1, self.longest // max(m, 1)) for w, m in most.items()}
+        self.groups = len(ins) if staggered else 1
+        self.units = self.longest * self.groups
 
     def dst(self, piece, slot):
         which, k, lead, _, _ = piece
@@ -148,10 +150,12 @@
         piece, ring, _, _, _ = self.streams[i]
         return self.ins[piece[0]].at[piece[1]], self.slot_of(ring, ring.me)
 
-    def begin(self):
-        for i in range(len(self.streams)):
+    def begin(self, group=None):
+        wanted = [i for i, stream in enumerate(self.streams) if group in (None, stream[0][0])]
+        for i in wanted:
             self.remote(i, 0, *self.own(i)).start()
-        for i, stream in enumerate(self.streams):
+        for i in wanted:
+            stream = self.streams[i]
             if stream[2] == 0:
                 src, slot = self.own(i)
                 pltpu.make_async_copy(src, self.dst(stream[0], slot), self.lsem.at[stream[4]]).start()
@@ -161,7 +165,8 @@
     def within(self, s, hops):
         return True if hops == self.longest else s <= hops
 
-    def serve(self, step):
+    def serve(self, unit):
+        step = unit // self.groups + 1
         for i, stream in enumerate(self.streams):
             every = self.every[stream[0][3]]
             s = step // every
@@ -177,6 +182,9 @@
             condition = self.within(s, stream[3])
             if every > 1:
                 condition = (lax.rem(step, every) == 0) & (s <= stream[3])
+            if self.groups > 1:
+                turn = lax.rem(unit, self.groups) == stream[0][0]
+                condition = turn if condition is True else turn & condition
             on_condition(condition, take)
 
     def serve_range(self, low, high):
@@ -217,7 +225,7 @@
     gather = Gather(D, V, spec, refs[:count], refs[count : 2 * count], refs[2 * count :])
     greet(gather.neighbours)
     gather.begin()
-    gather.serve_range(1, gather.longest + 1)
+    gather.serve_range(0, gather.units)
     gather.finish()
 
 
@@ -502,142 +510,6 @@
     )(grad, dx, ids, gains, *dense)
 
 
-def vocab_gather_kernel(V, count, *refs):
-    ins, outs = refs[:count], refs[count : 2 * count]
-    ssem, rsem, xssem, xrsem, lsem = refs[2 * count :]
-    d, v = lax.axis_index("dp"), lax.axis_index("vocab")
-    half = V // 2
-    core, chip = lax.rem(v, 2), v // 2
-    sib = sibling()
-
-    def other(k):
-        return lax.rem(chip + k + half, half) * 2 + core
-
-    greet([(d, other(k)) for k in range(1, half)] + [sib])
-
-    def send(q, k):
-        return pltpu.make_async_remote_copy(
-            src_ref=ins[q],
-            dst_ref=outs[q].at[v],
-            send_sem=ssem.at[q, k],
-            recv_sem=rsem.at[q, k],
-            device_id=(d, other(k)),
-            device_id_type=MESH,
-        )
-
-    def across(q, k, src, slot):
-        return pltpu.make_async_remote_copy(
-            src_ref=src,
-            dst_ref=outs[q].at[slot],
-            send_sem=xssem.at[q, k],
-            recv_sem=xrsem.at[q, k],
-            device_id=sib,
-            device_id_type=MESH,
-        )
-
-    for q in range(count):
-        for k in range(1, half):
-            send(q, k).start()
-    for q in range(count):
-        across(q, 0, ins[q], v).start()
-        pltpu.make_async_copy(ins[q], outs[q].at[v], lsem.at[q]).start()
-    for q in range(count):
-        for k in range(1, half):
-            slot = other(-k)
-            send(q, k).wait_recv()
-            across(q, k, outs[q].at[slot], slot).start()
-    for q in range(count):
-        pltpu.make_async_copy(ins[q], outs[q].at[v], lsem.at[q]).wait()
-        for k in range(half):
-            slot = other(-k)
-            if k:
-                send(q, k).wait_send()
-            across(q, k, outs[q].at[slot], slot).wait_send()
-            across(q, k, outs[q].at[slot], slot + 1 - 2 * core).wait_recv()
-
-
-def vocab_gather(V, arrays, ident):
-    count = len(arrays)
-    sems = pltpu.SemaphoreType.DMA((count, V // 2))
-    return pl.pallas_call(
-        functools.partial(vocab_gather_kernel, V, count),
-        out_shape=[jax.ShapeDtypeStruct((V,) + a.shape, a.dtype) for a in arrays],
-        in_specs=[ANYWHERE] * count,
-        out_specs=[ANYWHERE] * count,
-        scratch_shapes=[sems] * 4 + [pltpu.SemaphoreType.DMA((count,))],
-        compiler_params=pltpu.CompilerParams(collective_id=ident, has_side_effects=True),
-    )(*arrays)
-
-
-def vocab_scatter_kernel(V, in_ref, out_ref, sums, taken, ssem, rsem, xsem):
-    d, v = lax.axis_index("dp"), lax.axis_index("vocab")
-    half = V // 2
-    core, chip = lax.rem(v, 2), v // 2
-    sib = sibling()
-
-    def other(k):
-        return lax.rem(chip + k + half, half)
-
-    greet([(d, other(k) * 2 + core) for k in range(1, half)] + [sib])
-    across = pltpu.make_async_remote_copy(
-        src_ref=in_ref.at[:, 1 - core],
-        dst_ref=sums,
-        send_sem=xsem.at[0],
-        recv_sem=xsem.at[1],
-        device_id=sib,
-        device_id_type=MESH,
-    )
-    across.start()
-    across.wait_recv()
-
-    def send(k):
-        return pltpu.make_async_remote_copy(
-            src_ref=sums.at[other(k)],
-            dst_ref=taken.at[k - 1],
-            send_sem=ssem.at[k - 1],
-            recv_sem=rsem.at[k - 1],
-            device_id=(d, other(k) * 2 + core),
-            device_id_type=MESH,
-        )
-
-    for k in [*range(1, half), 0]:
-        to = other(k)
-        total = sums[to].astype(F32) + in_ref[to, core].astype(F32)
-        sums[to] = total.astype(B16)
-        if k:
-            send(k).start()
-    total = sums[chip].astype(F32)
-    for k in range(1, half):
-        send(k).wait_recv()
-        total = total + taken[k - 1].astype(F32)
-    out_ref[...] = total
-    for k in range(1, half):
-        send(k).wait_send()
-    across.wait_send()
-
-
-def vocab_scatter(V, array, ident):
-    half = V // 2
-    block = array.shape[1:]
-    sems = pltpu.SemaphoreType.DMA((max(half - 1, 1),))
-    return pl.pallas_call(
-        functools.partial(vocab_scatter_kernel, V),
-        out_shape=jax.ShapeDtypeStruct(block, F32),
-        in_specs=[IN_VMEM],
-        out_specs=IN_VMEM,
-        scratch_shapes=[
-            pltpu.VMEM((half,) + block, B16),
-            pltpu.VMEM((max(half - 1, 1),) + block, B16),
-            sems,
-            sems,
-            pltpu.SemaphoreType.DMA((2,)),
-        ],
-        compiler_params=pltpu.CompilerParams(
-            collective_id=ident, has_side_effects=True, vmem_limit_bytes=40 * MIB
-        ),
-    )(array.reshape((half, 2) + block))
-
-
 def tile_of(size, tokens=1):
     return next(t for t in (1280, 768, 640, 512, 256, 128) if size % t == 0 and (t * tokens <= 1280 * 2048 or t == 128))
 
@@ -670,10 +542,12 @@
 
 
 def study_kernel(D, V, spec, *refs):
-    first_ref, second_ref, own_ref, table_ref, given_ref = refs[:5]
-    first_out, second_out, hidden_ref, turned_out, dh_ref, grad_ref, rows_out = refs[5:12]
-    top_ref, sum_ref, dl_ref, slots, hs, hr, xs, xr, ps, pr = refs[12:22]
-    gather = Gather(D, V, spec, (first_ref, second_ref), (first_out, second_out), refs[22:])
+    first_ref, mid_ref, second_ref, table_ref, given_ref, segment_ref, pos_ref, attention_ref, up_ref, down_ref, gains_ref = refs[:11]
+    first_out, mid_out, second_out, hidden_ref, turned_out, rows_out = refs[11:17]
+    kept, refs = refs[17:23], refs[23:]
+    top_ref, sum_ref, pick_ref, dh_ref, dl_ref, slots, own_ref, bias_ref, sums, taken = refs[:10]
+    hs, hr, xs, xr, es, er, fs, fr, ps, pr = refs[10:20]
+    gather = Gather(D, V, spec, (first_ref, mid_ref, second_ref), (first_out, mid_out, second_out), refs[20:], True)
     d, v = lax.axis_index("dp"), lax.axis_index("vocab")
     half = V // 2
     core, chip = lax.rem(v, 2), v // 2
@@ -683,9 +557,82 @@
     tiles, blocks = size // tile, tokens // block
     peers = [(d, lax.rem(v + k, V)) for k in range(1, V)]
     greet(gather.neighbours + peers)
+    marks = [k * gather.units // 24 for k in range(25)]
+    gather.begin(0)
 
     def other(k):
         return lax.rem(chip + k + half, half) * 2 + core
+
+    def columns(t):
+        return pl.ds(pl.multiple_of(t * tile, tile), tile)
+
+    def rows_of(slot, part=0, size=length):
+        return pl.ds(pl.multiple_of(slot * length + part * size, size), size)
+
+    dh_ref[...] = jnp.zeros(dh_ref.shape, F32)
+
+    def pick_for(k, low, high):
+        slots_of = [other(k) - core + c for c in range(2)]
+
+        def pick(t, carry):
+            for slot in slots_of:
+                lane = lax.broadcasted_iota(jnp.int32, (length, tile), 1)
+                hit = lane == given_ref[rows_of(slot), 2:3].astype(jnp.int32) - t * tile
+                hit = jnp.where(hit, 1.0, 0.0).astype(B16)
+                dh_ref[rows_of(slot), :] += mm(hit, table_ref[:, columns(t)], (1, 1))
+            return carry
+
+        lax.fori_loop(low, high, pick, 0)
+        if high == tiles:
+            for slot in slots_of:
+                dl_ref[rows_of(slot), :] = dh_ref[rows_of(slot), :].astype(B16)
+
+    def slab(slot):
+        return dl_ref.at[rows_of(slot)]
+
+    def swap(k):
+        to = other(k)
+        return pltpu.make_async_remote_copy(
+            src_ref=slab(to + 1 - 2 * core), dst_ref=sums.at[to // 2], send_sem=es.at[k], recv_sem=er.at[k],
+            device_id=sibling(), device_id_type=MESH,
+        )
+
+    def pass_on(k):
+        return pltpu.make_async_remote_copy(
+            src_ref=sums.at[other(k) // 2], dst_ref=taken.at[k - 1], send_sem=fs.at[k], recv_sem=fr.at[k],
+            device_id=(d, other(k)), device_id_type=MESH,
+        )
+
+    def join(k):
+        swap(k).wait()
+        to = other(k)
+        sums[to // 2] = (sums[to // 2].astype(F32) + slab(to)[...].astype(F32)).astype(B16)
+
+    for k in range(1, half):
+        pick_for(k, 0, tiles)
+        swap(k).start()
+    gather.begin(1)
+    gather.serve_range(marks[0], marks[1])
+    for k in range(1, half):
+        join(k)
+        pass_on(k).start()
+    pick_for(0, 0, tiles // 2)
+    gather.begin(2)
+    pick_for(0, tiles // 2, tiles)
+    swap(0).start()
+    gather.serve_range(marks[1], marks[3])
+    join(0)
+    x = sums[chip].astype(F32)
+    for k in range(1, half):
+        pass_on(k).wait_recv()
+        x = x + taken[k - 1].astype(F32)
+    place_of = bias_of(segment_ref, bias_ref)
+    lane = lax.broadcasted_iota(jnp.int32, (length, pos_ref.shape[0]), 1)
+    x = x + mm(jnp.where(lane == place_of, 1.0, 0.0).astype(B16), pos_ref[...])
+    gather.serve_range(marks[3], marks[4])
+    between = lambda: gather.serve_range(marks[4], marks[6])
+    learn(x, attention_ref, up_ref, down_ref, gains_ref, bias_ref, own_ref, kept, between)
+    gather.serve_range(marks[6], marks[7])
 
     def place(slot):
         return hidden_ref.at[pl.ds(pl.multiple_of(slot * length, length), length)]
@@ -705,36 +652,42 @@
     for k in range(1, half):
         send(k).start()
     across(0, own_ref, v).start()
-    gather.begin()
     place(v)[...] = own_ref[...]
     top_ref[...] = jnp.full(top_ref.shape, -jnp.inf, F32)
     sum_ref[...] = jnp.zeros(sum_ref.shape, F32)
-    dh_ref[...] = jnp.zeros(dh_ref.shape, F32)
+    pick_ref[...] = jnp.zeros(pick_ref.shape, F32)
+    across(0, own_ref, v + 1 - 2 * core).wait_recv()
+
+    def due(t, parts, low, high):
+        return low + t * (high - low) // parts
+
+    def pass_one(u, carry):
+        near = lax.rem(chip + u // tiles, half) * 2
+        t = lax.rem(u, tiles)
+        for slot in (near, near + 1):
+            for k in range(length // block):
+                rows = rows_of(slot, k, block)
+                logits = mm(hidden_ref[rows, :], table_ref[:, columns(t)])
+                running(logits, top_ref, sum_ref, rows)
+                lane = lax.broadcasted_iota(jnp.int32, logits.shape, 1)
+                hit = lane == given_ref[rows, 1:2].astype(jnp.int32) - t * tile
+                pick_ref[rows, :] += lane_fold(jnp.where(hit, logits, 0.0), jnp.add)
+        parts = half * tiles
+        gather.serve_range(due(u, parts, marks[7], marks[19]), due(u + 1, parts, marks[7], marks[19]))
+        return carry
+
+    lax.fori_loop(0, tiles, pass_one, 0)
     for k in range(1, half):
         slot = other(-k)
         send(k).wait_recv()
         across(k, place(slot), slot).start()
-    for k in range(half):
+    for k in range(1, half):
         across(k, place(other(-k)), other(-k) + 1 - 2 * core).wait_recv()
-
-    def columns(t):
-        return pl.ds(pl.multiple_of(t * tile, tile), tile)
-
-    early = max(1, gather.longest // 4)
-    late = gather.longest - early
-
-    def pass_one(t, carry):
-        for k in range(blocks):
-            rows = slice(k * block, (k + 1) * block)
-            logits = jnp.dot(hidden_ref[rows, :], table_ref[:, columns(t)], preferred_element_type=F32)
-            running(logits, top_ref, sum_ref, rows)
-        gather.serve_range(1 + t * early // tiles, 1 + (t + 1) * early // tiles)
-        return carry
-
-    lax.fori_loop(0, tiles, pass_one, 0)
+    lax.fori_loop(tiles, half * tiles, pass_one, 0)
     top = jnp.max(top_ref[...], 1, keepdims=True)
     total = jnp.sum(sum_ref[...] * jnp.exp(top_ref[...] - top), 1, keepdims=True)
-    slots[v] = pack_rows([top, total])
+    picked = jnp.sum(pick_ref[...], 1, keepdims=True)
+    slots[v] = pack_rows([top, total, picked])
 
     def tell(k):
         return pltpu.make_async_remote_copy(
@@ -752,40 +705,15 @@
     top = slots[0, 0:1, :]
     for k in range(1, V):
         top = jnp.maximum(top, slots[k, 0:1, :])
-    total = jnp.zeros(top.shape, F32)
+    total, picked = jnp.zeros(top.shape, F32), jnp.zeros(top.shape, F32)
     for k in range(V):
         total = total + slots[k, 1:2, :] * jnp.exp(slots[k, 0:1, :] - top)
-    lse = top + jnp.log(total)
-    rows_out[...] = jnp.broadcast_to(lse, rows_out.shape)
-    lse_ref, pick_ref = top_ref, sum_ref
-    lse_ref[...] = jnp.broadcast_to(lse, (128, tokens)).T
-    pick_ref[...] = jnp.zeros(pick_ref.shape, F32)
-
-    def pass_two(t, carry):
-        for k in range(blocks):
-            rows = slice(k * block, (k + 1) * block)
-            logits = jnp.dot(hidden_ref[rows, :], table_ref[:, columns(t)], preferred_element_type=F32)
-            weight = given_ref[rows, 0:1]
-            soft = jnp.exp(logits - lse_ref[rows, :1]) * ((1.0 + MIX_ALPHA) * weight)
-            lane = lax.broadcasted_iota(jnp.int32, logits.shape, 1)
-            hit = lane == given_ref[rows, 1:2].astype(jnp.int32) - t * tile
-            dl_ref[rows, :] = jnp.where(hit, soft - weight, soft).astype(B16)
-            pick_ref[rows, :] += lane_fold(jnp.where(hit, logits, 0.0), jnp.add)
-        for k in range(tokens // length):
-            rows = slice(k * length, (k + 1) * length)
-            dh_ref[rows, :] += lax.dot_general(
-                dl_ref[rows, :], table_ref[:, columns(t)], (((1,), (1,)), ((), ())), preferred_element_type=F32
-            )
-        grad_ref[:, columns(t)] = jnp.dot(
-            turned_out[...], dl_ref[...], preferred_element_type=F32
-        ).astype(B16)
-        gather.serve_range(1 + early + t * late // tiles, 1 + early + (t + 1) * late // tiles)
-        return carry
-
-    lax.fori_loop(0, tiles, pass_two, 0)
-    picks = pack_rows([jnp.sum(pick_ref[...], 1, keepdims=True)])
-    rows_out[1:2, :] = picks[0:1]
+        picked = picked + slots[k, 2:3, :]
+    rows_out[...] = jnp.broadcast_to(top + jnp.log(total), rows_out.shape)
+    rows_out[1:2, :] = picked
+    gather.serve_range(marks[19], marks[24])
     for k in range(1, half):
+        pass_on(k).wait_send()
         send(k).wait_send()
     for k in range(half):
         across(k, place(other(-k)), other(-k)).wait_send()
@@ -794,55 +722,121 @@
     gather.finish()
 
 
-def study(D, V, first, second, own, table, given, ident):
-    spec = tuple((q, r, True, r, q) for r in range(3) for q in range(2))
-    shapes, sems = gather_plan(D, V, [first, second], spec)
-    length, width = own.shape
+def study(D, V, layers, table, given, segment, pos, attention, up, down, gains, ident):
+    spec = tuple((q, r, True, r, (q + r) % 2) for r in range(3) for q in range(3))
+    shapes, sems = gather_plan(D, V, layers, spec)
+    length, width = segment.shape[1], gains.shape[1]
     tokens, size = V * length, table.shape[1]
     tile = tile_of(size, tokens)
     halves, singles = pltpu.SemaphoreType.DMA((V // 2,)), pltpu.SemaphoreType.DMA((V,))
     column = pltpu.VMEM((tokens, 128), F32)
+    square, half = jax.ShapeDtypeStruct((length, width), F32), jax.ShapeDtypeStruct((length, width), B16)
     return pl.pallas_call(
         functools.partial(study_kernel, D, V, spec),
         out_shape=shapes
         + [
             jax.ShapeDtypeStruct((tokens, width), B16),
             jax.ShapeDtypeStruct((width, tokens), B16),
-            jax.ShapeDtypeStruct((tokens, width), F32),
-            jax.ShapeDtypeStruct((width, size), B16),
             jax.ShapeDtypeStruct((8, tokens), F32),
+            square, square, square,
+            jax.ShapeDtypeStruct((length, 128), F32),
+            jax.ShapeDtypeStruct((length, 3 * width), B16),
+            half,
         ],
-        in_specs=[ANYWHERE] * 2 + [IN_VMEM] * 3,
-        out_specs=[ANYWHERE] * 2 + [IN_VMEM] * 5,
-        scratch_shapes=[column] * 2
-        + [pltpu.VMEM((tokens, tile), B16), pltpu.VMEM((V, 8, tokens), F32)]
-        + [halves] * 4
+        in_specs=[ANYWHERE] * 3 + [IN_VMEM] * 8,
+        out_specs=[ANYWHERE] * 3 + [IN_VMEM] * 9,
+        scratch_shapes=[column] * 3
+        + [
+            pltpu.VMEM((tokens, width), F32),
+            pltpu.VMEM((tokens, width), B16),
+            pltpu.VMEM((V, 8, tokens), F32),
+            pltpu.VMEM((length, width), B16),
+            pltpu.VMEM((length, length), F32),
+            pltpu.VMEM((V // 2, length, width), B16),
+            pltpu.VMEM((max(V // 2 - 1, 1), length, width), B16),
+        ]
+        + [halves] * 8
         + [singles] * 2
         + sems,
         compiler_params=pltpu.CompilerParams(
-            collective_id=ident, has_side_effects=True, vmem_limit_bytes=60 * MIB
+            collective_id=ident, has_side_effects=True, vmem_limit_bytes=63 * MIB
         ),
-    )(first, second, own, table, given)
-
-
-def teacher_stats_kernel(group_ref, hidden_ref, table_ref, out_ref, stats_ref, top_ref, sum_ref, cross_ref):
+    )(*layers, table, given, segment, pos, attention, up, down, gains)
+
+
+def share_rows(V, slots, values, send, recv):
+    d, v = lax.axis_index("dp"), lax.axis_index("vocab")
+
+    def tell(k):
+        return pltpu.make_async_remote_copy(
+            src_ref=slots.at[v], dst_ref=slots.at[v], send_sem=send.at[k], recv_sem=recv.at[k],
+            device_id=(d, lax.rem(v + k + 1, V)), device_id_type=MESH,
+        )
+
+    slots[v] = values
+    for k in range(V - 1):
+        tell(k).start()
+    for k in range(V - 1):
+        tell(k).wait()
+
+
+def teacher_stats_kernel(
+    V, group_ref, own_ref, table_ref, out_ref, rows_ref,
+    hidden_ref, top_ref, sum_ref, cross_ref, slots, hs, hr, xs, xr, ps, pr,
+):
     step = pl.program_id(0)
-    count, length = hidden_ref.shape[:2]
+    half = V // 2
+    tiles = pl.num_programs(0) // half
+    d, v = lax.axis_index("dp"), lax.axis_index("vocab")
+    core, chip = lax.rem(v, 2), v // 2
+    length = own_ref.shape[0]
     block = min(256, length)
+
+    def other(k):
+        return lax.rem(chip + k + half, half) * 2 + core
+
+    def send(k):
+        return pltpu.make_async_remote_copy(
+            src_ref=own_ref, dst_ref=hidden_ref.at[v], send_sem=hs.at[k], recv_sem=hr.at[k],
+            device_id=(d, other(k)), device_id_type=MESH,
+        )
+
+    def across(k, src, slot):
+        return pltpu.make_async_remote_copy(
+            src_ref=src, dst_ref=hidden_ref.at[slot], send_sem=xs.at[k], recv_sem=xr.at[k],
+            device_id=sibling(), device_id_type=MESH,
+        )
 
     @pl.when(step == 0)
     def _():
+        greet([(d, lax.rem(v + k, V)) for k in range(1, V)])
+        for k in range(1, half):
+            send(k).start()
+        across(0, own_ref, v).start()
+        hidden_ref[v] = own_ref[...]
         top_ref[...] = jnp.full(top_ref.shape, -jnp.inf, F32)
         sum_ref[...] = jnp.zeros(sum_ref.shape, F32)
         cross_ref[...] = jnp.zeros(cross_ref.shape, F32)
-
-    for row in range(count):
-        table = table_ref[group_ref[row]]
+        across(0, own_ref, v + 1 - 2 * core).wait_recv()
+
+    for part in range(1, half):
+        k = half - part
+
+        @pl.when(step == part * tiles)
+        def _(k=k):
+            slot = other(-k)
+            send(k).wait_recv()
+            across(k, hidden_ref.at[slot], slot).start()
+            across(k, hidden_ref.at[slot], slot + 1 - 2 * core).wait_recv()
+
+    for c in range(2):
+        slot = lax.rem(chip + step // tiles, half) * 2 + c
+        table = table_ref[group_ref[slot]]
         for k in range(length // block):
             inside = slice(k * block, (k + 1) * block)
-            rows = slice(row * length + k * block, row * length + (k + 1) * block)
-            rounded = mm(hidden_ref[row, inside, :], table).astype(B16)
-            out_ref[row, inside, :] = rounded
+            rows = pl.ds(pl.multiple_of(slot * length + k * block, block), block)
+            rounded = mm(hidden_ref[slot, inside, :], table).astype(B16)
+            out_ref[c, inside, :] = rounded
             values = rounded.astype(F32)
             expd, fade = running(values, top_ref, sum_ref, rows)
             cross_ref[rows, :] = cross_ref[rows, :] * fade + lane_fold(expd * values, jnp.add)
@@ -853,125 +847,168 @@
         scale = jnp.exp(top_ref[...] - top)
         total = jnp.sum(sum_ref[...] * scale, 1, keepdims=True)
         cross = jnp.sum(cross_ref[...] * scale, 1, keepdims=True)
-        stats_ref[...] = pack_rows([top, total, cross])
-
-
-def teacher_stats(groups, hidden, tables):
-    count, length, width = hidden.shape
+        share_rows(V, slots, pack_rows([top, total, cross]), ps, pr)
+        top = slots[0, 0:1, :]
+        for k in range(1, V):
+            top = jnp.maximum(top, slots[k, 0:1, :])
+        total, cross = jnp.zeros(top.shape, F32), jnp.zeros(top.shape, F32)
+        for k in range(V):
+            scale = jnp.exp(slots[k, 0:1, :] - top)
+            total = total + slots[k, 1:2, :] * scale
+            cross = cross + slots[k, 2:3, :] * scale
+        rows_ref[...] = jnp.broadcast_to(top + jnp.log(total), rows_ref.shape)
+        rows_ref[1:2, :] = cross / total
+        for k in range(1, half):
+            send(k).wait_send()
+        for k in range(half):
+            across(k, own_ref, v).wait_send()
+
+
+def teacher_stats(V, groups, own, tables, ident):
+    length, width = own.shape
     kinds, _, size = tables.shape
-    tokens = count * length
+    tokens = V * length
     tile = tile_of(size, tokens)
+    tiles = size // tile
+    halves = pltpu.SemaphoreType.DMA((V // 2,))
+    singles = pltpu.SemaphoreType.DMA((V,))
     return pl.pallas_call(
-        teacher_stats_kernel,
-        grid_spec=pltpu.PrefetchScalarGridSpec(
-            num_scalar_prefetch=1,
-            grid=(size // tile,),
-            in_specs=[
-                pl.BlockSpec((count, length, width), lambda j, g: (0, 0, 0)),
-                pl.BlockSpec((kinds, width, tile), lambda j, g: (0, 0, j)),
-            ],
-            out_specs=[
-                pl.BlockSpec((count, length, tile), lambda j, g: (0, 0, j)),
-                pl.BlockSpec((8, tokens), lambda j, g: (0, 0)),
-            ],
-            scratch_shapes=[pltpu.VMEM((tokens, 128), F32)] * 3,
-        ),
+        functools.partial(teacher_stats_kernel, V),
+        grid=(V // 2 * tiles,),
+        in_specs=[
+            pl.BlockSpec(memory_space=pltpu.SMEM),
+            pl.BlockSpec((length, width), lambda i: (0, 0)),
+            pl.BlockSpec((kinds, width, tile), lambda i: (0, 0, i % tiles)),
+        ],
+        out_specs=[
+            pl.BlockSpec((2, length, tile), lambda i: (i // tiles, 0, i % tiles)),
+            pl.BlockSpec((8, tokens), lambda i: (0, 0)),
+        ],
         out_shape=[
-            jax.ShapeDtypeStruct((count, length, size), B16),
+            jax.ShapeDtypeStruct((V, length, size), B16),
             jax.ShapeDtypeStruct((8, tokens), F32),
         ],
-        compiler_params=pltpu.CompilerParams(vmem_limit_bytes=60 * MIB),
-    )(groups, hidden, tables)
-
-
-def teacher_grad_kernel(
-    teacher_ref, turned_ref, hidden_ref, table_ref, given_ref, dhin_ref, gradin_ref,
-    dh_ref, grad_ref, cross_ref, dl_ref, sum_ref,
+        scratch_shapes=[pltpu.VMEM((V, length, width), B16)]
+        + [pltpu.VMEM((tokens, 128), F32)] * 3
+        + [pltpu.VMEM((V, 8, tokens), F32)]
+        + [halves] * 4
+        + [singles] * 2,
+        compiler_params=pltpu.CompilerParams(
+            collective_id=ident, has_side_effects=True, vmem_limit_bytes=60 * MIB
+        ),
+    )(groups, own, tables)
+
+
+def head_grad_kernel(
+    V, teacher_ref, hidden_ref, turned_ref, table_ref, given_ref, dtwo_ref, grad_ref, rows_ref,
+    dl_ref, sum_ref, cross_ref, dh_ref, sums, taken, es, er, fs, fr,
 ):
     step = pl.program_id(0)
+    tile = table_ref.shape[1]
+    half = V // 2
+    d, v = lax.axis_index("dp"), lax.axis_index("vocab")
+    core, chip = lax.rem(v, 2), v // 2
+
+    def other(k):
+        return lax.rem(chip + k + half, half) * 2 + core
     count, length = teacher_ref.shape[:2]
     block = min(256, length)
 
     @pl.when(step == 0)
     def _():
-        sum_ref[...] = dhin_ref[...]
+        greet([(d, other(k)) for k in range(1, half)] + [sibling()])
+        sum_ref[...] = jnp.zeros(sum_ref.shape, F32)
+        cross_ref[...] = jnp.zeros(cross_ref.shape, F32)
 
     for row in range(count):
+        near = lax.rem(row // 2 - chip + half, half) * 2 + row % 2
         for k in range(length // block):
             inside = slice(k * block, (k + 1) * block)
             rows = slice(row * length + k * block, row * length + (k + 1) * block)
-            target = jnp.exp(teacher_ref[row, inside, :].astype(F32) - given_ref[rows, 1:2])
-            dl_ref[rows, :] = ((-MIX_ALPHA * given_ref[rows, 0:1]) * target).astype(B16)
+            logits = mm(hidden_ref[rows, :], table_ref[...])
+            weight = given_ref[rows, 0:1]
+            target = jnp.exp(teacher_ref[near, inside, :].astype(F32) - given_ref[rows, 3:4])
+            soft = jnp.exp(logits - given_ref[rows, 2:3])
+            cross_ref[rows, :] += lane_fold(target * logits, jnp.add)
+            lane = lax.broadcasted_iota(jnp.int32, logits.shape, 1)
+            hit = lane == given_ref[rows, 1:2].astype(jnp.int32) - step * tile
+            both = soft * ((1.0 + MIX_ALPHA) * weight) - target * (MIX_ALPHA * weight)
+            dl_ref[rows, :] = jnp.where(hit, both - weight, both).astype(B16)
         rows = slice(row * length, (row + 1) * length)
         sum_ref[rows, :] += mm(dl_ref[rows, :], table_ref[...], (1, 1))
-    grad_ref[...] = (gradin_ref[...].astype(F32) + mm(turned_ref[...], dl_ref[...])).astype(grad_ref.dtype)
+    grad_ref[...] = mm(turned_ref[...], dl_ref[...]).astype(B16)
 
     @pl.when(step == pl.num_programs(0) - 1)
     def _():
         dh_ref[...] = sum_ref[...].astype(B16)
-        part = jnp.sum(hidden_ref[...].astype(F32) * (sum_ref[...] - dhin_ref[...]), 1, keepdims=True)
-        cross_ref[...] = jnp.broadcast_to(jnp.sum(part, 0, keepdims=True), cross_ref.shape)
-
-
-def teacher_grad(teacher, turned, hidden, table, given, dh, grad):
+
+        def slab(slot):
+            return dh_ref.at[pl.ds(pl.multiple_of(slot * length, length), length)]
+
+        def swap(k):
+            to = other(k)
+            return pltpu.make_async_remote_copy(
+                src_ref=slab(to + 1 - 2 * core), dst_ref=sums.at[to // 2], send_sem=es.at[k], recv_sem=er.at[k],
+                device_id=sibling(), device_id_type=MESH,
+            )
+
+        def pass_on(k):
+            return pltpu.make_async_remote_copy(
+                src_ref=sums.at[other(k) // 2], dst_ref=taken.at[k - 1], send_sem=fs.at[k], recv_sem=fr.at[k],
+                device_id=(d, other(k)), device_id_type=MESH,
+            )
+
+        order = [*range(1, half), 0]
+        for k in order:
+            swap(k).start()
+        for k in order:
+            swap(k).wait()
+            to = other(k)
+            sums[to // 2] = (sums[to // 2].astype(F32) + slab(to)[...].astype(F32)).astype(B16)
+            if k:
+                pass_on(k).start()
+        rows_ref[...] = pack_rows([jnp.sum(cross_ref[...], 1, keepdims=True)])
+        total = sums[chip].astype(F32)
+        for k in range(1, half):
+            pass_on(k).wait_recv()
+            total = total + taken[k - 1].astype(F32)
+        dtwo_ref[...] = total
+        for k in range(1, half):
+            pass_on(k).wait_send()
+
+
+def head_grad(V, teacher, hidden, turned, table, given, ident):
     count, length, size = teacher.shape
     width, tokens = turned.shape
     tile = tile_of(size, tokens)
     whole = lambda *shape: pl.BlockSpec(shape, lambda j: (0, 0))
     striped = pl.BlockSpec((width, tile), lambda j: (0, j))
     return pl.pallas_call(
-        teacher_grad_kernel,
+        functools.partial(head_grad_kernel, V),
         grid=(size // tile,),
         out_shape=[
-            jax.ShapeDtypeStruct((tokens, width), B16),
+            jax.ShapeDtypeStruct((length, width), F32),
             jax.ShapeDtypeStruct((width, size), B16),
-            jax.ShapeDtypeStruct((8, 128), F32),
+            jax.ShapeDtypeStruct((8, tokens), F32),
         ],
         in_specs=[
             pl.BlockSpec((count, length, tile), lambda j: (0, 0, j)),
-            whole(width, tokens), whole(tokens, width), striped, whole(tokens, 2), whole(tokens, width), striped,
+            whole(tokens, width), whole(width, tokens), striped, whole(tokens, 4),
         ],
-        out_specs=[whole(tokens, width), striped, whole(8, 128)],
-        scratch_shapes=[pltpu.VMEM((tokens, tile), B16), pltpu.VMEM((tokens, width), F32)],
-        compiler_params=pltpu.CompilerParams(vmem_limit_bytes=60 * MIB),
-    )(teacher, turned, hidden, table, given, dh, grad)
-
-
-def pick_kernel(block, ids_ref, table_ref, out_ref):
-    step = pl.program_id(0)
-    tile = table_ref.shape[1]
-
-    @pl.when(step == 0)
-    def _():
-        out_ref[...] = jnp.zeros(out_ref.shape, F32)
-
-    def one(k, carry):
-        rows = pl.ds(pl.multiple_of(k * block, block), block)
-        lane = lax.broadcasted_iota(jnp.int32, (block, tile), 1)
-        hit = jnp.where(lane == ids_ref[rows, :] - step * tile, 1.0, 0.0).astype(B16)
-        out_ref[rows, :] += lax.dot_general(
-            hit, table_ref[...], (((1,), (1,)), ((), ())), preferred_element_type=F32
-        )
-        return carry
-
-    lax.fori_loop(0, ids_ref.shape[0] // block, one, 0, unroll=True)
-
-
-def pick_rows(ids, table):
-    tokens = ids.shape[0]
-    width, size = table.shape
-    tile = tile_of(size)
-    return pl.pallas_call(
-        functools.partial(pick_kernel, 512),
-        grid=(size // tile,),
-        out_shape=jax.ShapeDtypeStruct((tokens, width), F32),
-        in_specs=[
-            pl.BlockSpec((tokens, 1), lambda j: (0, 0)),
-            pl.BlockSpec((width, tile), lambda j: (0, j)),
-        ],
-        out_specs=pl.BlockSpec((tokens, width), lambda j: (0, 0)),
-        compiler_params=pltpu.CompilerParams(vmem_limit_bytes=48 * MIB),
-    )(ids, table)
+        out_specs=[whole(length, width), striped, whole(8, tokens)],
+        scratch_shapes=[
+            pltpu.VMEM((tokens, tile), B16),
+            pltpu.VMEM((tokens, width), F32),
+            pltpu.VMEM((tokens, 128), F32),
+            pltpu.VMEM((tokens, width), B16),
+            pltpu.VMEM((V // 2, length, width), B16),
+            pltpu.VMEM((max(V // 2 - 1, 1), length, width), B16),
+        ]
+        + [pltpu.SemaphoreType.DMA((V // 2,))] * 4,
+        compiler_params=pltpu.CompilerParams(
+            collective_id=ident, has_side_effects=True, vmem_limit_bytes=62 * MIB
+        ),
+    )(teacher, hidden, turned, table, given)
 
 
 def mm(a, b, over=(1, 0)):
@@ -1025,7 +1062,7 @@
     return ref[:, pl.ds(pl.multiple_of(part * width + pair * 128, 128), 128)]
 
 
-def layer_forward(x, weights, gains_ref, bias_ref, packed_ref, context_ref):
+def layer_forward(x, weights, gains_ref, bias_ref, packed_ref, context_ref, between=lambda: None):
     qkv_ref, out_ref, up_ref, down_ref = weights
     length, width = x.shape
     gain = lambda k: gains_ref[k : k + 1, :]
@@ -1043,6 +1080,7 @@
         return carry
 
     lax.fori_loop(0, width // 128, heads, 0)
+    between()
     h_one, normed_b, scaler_b = norm_rows(h_zero + mm(context_ref[...], out_ref[...]), gain(2), gain(3))
     one_b = h_one.astype(B16)
     total = h_one
@@ -1055,18 +1093,18 @@
     return h_two, (normed_a, normed_b, normed_c), (scaler_a, scaler_b, scaler_c)
 
 
-def teach_kernel(group_ref, x_ref, segment_ref, first_ref, second_ref, gains_ref, top_ref, bias_ref, packed_ref, context_ref):
+def teach_kernel(group_ref, x_ref, segment_ref, first_ref, mid_ref, second_ref, gains_ref, top_ref, bias_ref, packed_ref, context_ref):
     width = x_ref.shape[2]
     bias_of(segment_ref, bias_ref)
     first, second = first_ref.at[0], second_ref.at[0]
-    weights = (first.at[:, : 3 * width], first.at[:, 3 * width : 4 * width], first.at[:, 4 * width :], second)
+    weights = (first.at[:, : 3 * width], first.at[:, 3 * width :], mid_ref.at[0], second)
     h_two, _, _ = layer_forward(
         x_ref[0].astype(F32), weights, gains_ref.at[0], bias_ref, packed_ref, context_ref
     )
     top_ref[...] = h_two.astype(B16)
 
 
-def teach(group, x, segment, first, second, gains):
+def teach(group, x, segment, first, mid, second, gains):
     _, length, width = x.shape
     chosen = lambda shape: pl.BlockSpec((1,) + shape[1:], lambda i, g: (g[0], 0, 0))
     return pl.pallas_call(
@@ -1078,6 +1116,7 @@
                 pl.BlockSpec((1, length, width), lambda i, g: (0, 0, 0)),
                 pl.BlockSpec((1, length), lambda i, g: (0, 0)),
                 chosen(first.shape),
+                chosen(mid.shape),
                 chosen(second.shape),
                 chosen(gains.shape),
             ],
@@ -1090,44 +1129,18 @@
         ),
         out_shape=jax.ShapeDtypeStruct((length, width), B16),
         compiler_params=pltpu.CompilerParams(vmem_limit_bytes=60 * MIB),
-    )(group, x, segment, first, second, gains)
-
-
-def learn_kernel(
-    rows_ref, segment_ref, pos_ref, attention_ref, up_ref, down_ref, gains_ref,
-    top_ref, na_ref, nb_ref, nc_ref, scalers_ref, packed_ref, context_ref, bias_ref,
-):
-    length, width = rows_ref.shape
-    place = bias_of(segment_ref, bias_ref)
-    lane = lax.broadcasted_iota(jnp.int32, (length, pos_ref.shape[0]), 1)
-    onehot = jnp.where(lane == place, 1.0, 0.0).astype(B16)
-    x = rows_ref[...] + mm(onehot, pos_ref[...])
+    )(group, x, segment, first, mid, second, gains)
+
+
+def learn(x, attention_ref, up_ref, down_ref, gains_ref, bias_ref, own_ref, kept, between):
+    length, width = x.shape
     weights = (attention_ref.at[:, : 3 * width], attention_ref.at[:, 3 * width :], up_ref, down_ref)
-    h_two, normed, scalers = layer_forward(x, weights, gains_ref, bias_ref, packed_ref, context_ref)
-    top_ref[...] = h_two.astype(B16)
-    for ref, value in zip((na_ref, nb_ref, nc_ref), normed):
+    h_two, normed, scalers = layer_forward(x, weights, gains_ref, bias_ref, kept[4], kept[5], between)
+    own_ref[...] = h_two.astype(B16)
+    for ref, value in zip(kept, normed):
         ref[...] = value
     lane = lax.broadcasted_iota(jnp.int32, (length, 128), 1)
-    scalers_ref[...] = jnp.where(lane == 0, scalers[0], jnp.where(lane == 1, scalers[1], scalers[2]))
-
-
-def learn(rows, segment, pos, attention, up, down, gains):
-    length, width = rows.shape
-    square = jax.ShapeDtypeStruct((length, width), F32)
-    half = jax.ShapeDtypeStruct((length, width), B16)
-    return pl.pallas_call(
-        learn_kernel,
-        in_specs=[IN_VMEM] * 7,
-        out_specs=[IN_VMEM] * 7,
-        out_shape=[
-            half, square, square, square,
-            jax.ShapeDtypeStruct((length, 128), F32),
-            jax.ShapeDtypeStruct((length, 3 * width), B16),
-            half,
-        ],
-        scratch_shapes=[pltpu.VMEM((length, length), F32)],
-        compiler_params=pltpu.CompilerParams(vmem_limit_bytes=56 * MIB),
-    )(rows, segment, pos, attention, up, down, gains)
+    kept[3][...] = jnp.where(lane == 0, scalers[0], jnp.where(lane == 1, scalers[1], scalers[2]))
 
 
 def back_kernel(
@@ -1254,36 +1267,26 @@
     counts = group_ints[:, 2].reshape(-1).astype(F32)
     groups = group_ints[:, 3, 0]
 
-    picked = pick_rows(ids_here, table).astype(B16).reshape(V, length, width)
-    embedded = vocab_scatter(V, picked, 2)
-    two_b, *kept = learn(embedded, segment_ids, pos_t, attention, up_t, down_t, gains_w)
-
     weight = counts / counted
-    given = jnp.concatenate([weight[:, None], labels_here.astype(F32)], 1)
-    first = jnp.concatenate([teacher_qkv, teacher_out, teacher_up], 2)
-    first, second, hidden_all, turned, dh_student, grad_head, told = study(
-        D, V, first, teacher_down, two_b, table, given, 4
+    given = jnp.concatenate([weight[:, None], labels_here.astype(F32), ids_here.astype(F32)], 1)
+    layers = [jnp.concatenate([teacher_qkv, teacher_out], 2), teacher_up, teacher_down]
+    first, mid, second, hidden_all, turned, told, *kept = study(
+        D, V, layers, table, given, segment_ids, pos_t, attention, up_t, down_t, gains_w, 4
     )
     student_lse, picked = told[0], told[1]
     tw = teacher_gains.shape[2]
     top = teach(
-        teacher_group, teacher_inputs, segment_ids, first.reshape(3, tw, -1), second.reshape(3, -1, tw), teacher_gains
+        teacher_group, teacher_inputs, segment_ids, first.reshape(3, tw, -1), mid.reshape(3, tw, -1),
+        second.reshape(3, -1, tw), teacher_gains,
     )
-    (teacher_hidden,) = vocab_gather(V, [top], 5)
-
-    teacher, stats = teacher_stats(groups, teacher_hidden, teacher_table)
-    stats = lax.all_gather(stats, "vocab")
-    top = jnp.max(stats[:, 0], 0)
-    scale = jnp.exp(stats[:, 0] - top)
-    tsum = jnp.sum(stats[:, 1] * scale, 0)
-    tcross = jnp.sum(stats[:, 2] * scale, 0) / tsum
-    teacher_lse = top + jnp.log(tsum)
-    given = jnp.concatenate([weight[:, None], teacher_lse[:, None]], 1)
-    dh, grad_head, cross = teacher_grad(teacher, turned, hidden_all, table, given, dh_student, grad_head)
-    once = jnp.sum(weight * (MIX_ALPHA * (tcross - teacher_lse + student_lse) + student_lse))
-    loss_part = cross[0, 0] - jnp.sum(weight * picked) + jnp.where(v == 0, once, 0.0)
-
-    dtwo = vocab_scatter(V, dh.reshape(V, length, width), 6)
+
+    teacher, told = teacher_stats(V, groups, top, teacher_table, 5)
+    teacher_lse, tcross = told[0], told[1]
+    given = jnp.stack([weight, labels_here[:, 0].astype(F32), student_lse, teacher_lse], 1)
+    dtwo, grad_head, cross = head_grad(V, teacher, hidden_all, turned, table, given, 6)
+    once = jnp.sum(weight * (MIX_ALPHA * (tcross - teacher_lse + student_lse) + student_lse - picked))
+    loss_part = jnp.where(v == 0, once, 0.0) - MIX_ALPHA * jnp.sum(weight * cross[0])
+
     turned_dx, grad_attention, grad_up, grad_down, grad_pos, grad_gains = back(
         dtwo, segment_ids, pos_t.shape[0], attention, up_t, down_t, gains_w, kept
     )

time: 740 us -> 698 us (0.943)
  Pallas kernels: 679 us -> 646 us
    pallas_call x7 -> x2, Pallas kernels: 183 us -> 143 us  [the longest x1 90.8 us: head_grad(): pl.pallas_call(functools.partial(head_grad_kernel, V), grid=(size // tile...]
where the time goes in v4:
time: 698 us; the launch traced here: 689 us
  Pallas kernels  646 us (93%)
  other arithmetic  26.5 us (4%)
  local copies, waits for them, and re-layouts  9.32 us (1%)
  between operations  7.17 us (1%)
    pallas_call x1, Pallas kernels, study(): pl.pallas_call(functools.partial(study_kernel, D, V, spec), out_shape=sha...  195 us
    pallas_call x1, Pallas kernels, settle(): pl.pallas_call(functools.partial(settle_kernel, D, V, rings), out_shape=[...  143 us
    pallas_call x1, Pallas kernels, ring_gather(): pl.pallas_call(functools.partial(gather_kernel, D, V, spec, len(arrays)),...  114 us
    pallas_call x1, Pallas kernels, head_grad(): pl.pallas_call(functools.partial(head_grad_kernel, V), grid=(size // tile...  90.8 us
    pallas_call x1, Pallas kernels, teacher_stats(): pl.pallas_call(functools.partial(teacher_stats_kernel, V), grid=(V // 2 *...  52 us
    pallas_call x1, Pallas kernels, back(): pl.pallas_call(back_kernel, in_specs=[IN_VMEM] * len(inputs), out_specs=[...  26.7 us
    pallas_call x1, Pallas kernels, teach(): pl.pallas_call(teach_kernel, grid_spec=pltpu.PrefetchScalarGridSpec(num_s...  24.5 us

profile of v4, /device:TPU:0, one launch (start us, length us, event | category | flops | bytes accessed | tf_op | source)
XLA Modules:
  0.0 689.3 jit_solution(11655277470314589443)
XLA Ops:
  1.4 1.3 concatenate.30
  2.8 2.6 convert_element_type.67
  7.9 114.2 %shard_map.497 = (bf16[8,2,32,7680]{3,2,1,0:T(8,128)(2,1)}, bf16[1,32,16,2048]{3,2,1,0:T(8,128)(2,1)}, bf16[1,32,16,2048]{3,2,1,0:T(8,128)(2,1)}, bf16[1,32,64,5...) custom-call(bf16[2,32,7680]{2,1,0:T(8,128)(2,1)} %bitcast.76, ...), custom_call_target="tpu_custom_call" | custom-call | tf_op jit(solution)/shard_map/pallas_call | solution.py:247
  122.1 0.9 constant_dynamic-slice_fusion
  123.0 1.8 fusion.5
  125.6 1.3 copy.84.refs_4_
  127.7 194.7 %shard_map.498 = (bf16[3,32,24,3072]{3,2,1,0:T(8,128)(2,1)}, bf16[3,32,24,3072]{3,2,1,0:T(8,128)(2,1)}, bf16[3,32,96,768]{3,2,1,0:T(8,128)(2,1)}, bf16[2048,512]...) custom-call(bf16[3,24,3072]{2,1,0:T(8,128)(2,1)} %pad_maximum_fusion, ...), custom_call_target="tpu_custom_call" | custom-call | tf_op jit(solution)/shard_map/pallas_call | solution.py:734
  322.5 24.5 %shard_map.499.own_ref = bf16[512,768]{1,0:T(8,128)(2,1)} custom-call(s32[1]{0:T(128)} %copy.93.group_ref, bf16[1,512,768]{2,1,0:T(8,128)(2,1)} %x_ref.1, s32[1,512]{1,0:T(1,128)} %segment_ref.3, bf16[3,768,3072]{2,1,0:T(8,128)(2,1)} %bitcast.67, bf16[3,768,3072]{2,1,0:T(8,128)(2,1)} %bitcast.68, bf16[3,3072,768]{2,1,0:T(8,128)(2,1)} %bitcast.69, ...), custom_call_target="tpu_custom_call" | custom-call | tf_op jit(solution)/shard_map/pallas_call | solution.py:1110
  347.6 52.0 %shard_map.500 = (bf16[4,512,7680]{2,1,0:T(8,128)(2,1)}, f32[8,2048]{1,0:T(8,128)}) custom-call(s32[4]{0:T(128)} %slice_reduce_fusion.2.group_ref, bf16[512,768]{1,0:T(8,128)(2,1)} %shard_map.499.own_ref, bf16[3,768,7680]{2,1,0:T(8,128)(2,1)} %table_ref.1), custom_call_target="tpu_custom_call" | custom-call | tf_op jit(solution)/shard_map/pallas_call | solution.py:875
  399.6 1.0 subtract_reduce_fusion
  401.3 1.3 copy.85.given_ref
  402.7 90.8 %shard_map.501 = (f32[512,512]{1,0:T(8,128)}, bf16[512,7680]{1,0:T(8,128)(2,1)}, f32[8,2048]{1,0:T(8,128)}) custom-call(bf16[4,512,7680]{2,1,0:T(8,128)(2,1)} %get-tuple-element.67.teacher_ref, bf16[2048,512]{1,0:T(8,128)(2,1)} %get-tuple-element.68.hidden_ref, bf16[512,2048]{1,0:T(8,128)(2,1)} %get-tuple-element.69.turned_ref, bf16[512,7680]{1,0:T(8,128)(2,1)} %bitcast.66, ...), custom_call_target="tpu_custom_call" | custom-call | tf_op jit(solution)/shard_map/pallas_call | solution.py:986
  493.5 0.8 slice.54
  496.2 26.7 %shard_map.502 = (bf16[512,512]{1,0:T(8,128)(2,1)}, bf16[512,2048]{1,0:T(8,128)(2,1)}, bf16[512,2048]{1,0:T(8,128)(2,1)}, bf16[2048,512]{1,0:T(8,128)(2,1)}, bf16[512,512]{1,0:T(8,128)(2,1)}, /*index=5*/f32[6,512]{1,0:T(8,128)}) custom-call(f32[512,512]{1,0:T(8,128)} %get-tuple-element.73.dtwo_ref, s32[1,512]{1,0:T(1,128)} %segment_ref.3, ...), custom_call_target="tpu_custom_call" | custom-call | tf_op jit(solution)/shard_map/pallas_call | solution.py:1209
  522.9 1.3 pad_maximum_fusion.4.refs_3_
  524.2 1.3 copy.86.refs_2_
  525.7 143.5 %shard_map.503 = (f32[64,7680]{1,0:T(8,128)}, f32[8,512]{1,0:T(8,128)}, f32[16,2048]{1,0:T(8,128)}, f32[16,2048]{1,0:T(8,128)}, f32[64,512]{1,0:T(8,128)}, /*index=5*/f32[16,512]{1,0:T(8,128)}) custom-call(bf16[512,7680]{1,0:T(8,128)(2,1)} %get-tuple-element.72.refs_0_, bf16[512,512]{1,0:T(8,128)(2,1)} %get-tuple-element.80.refs_1_, ...), custom_call_target="tpu_custom_call" | custom-call | tf_op jit(solution)/shard_map/pallas_call | solution.py:487
  669.2 1.4 fusion.24
  670.6 1.3 multiply_reduce_fusion
  674.1 1.4 multiply_subtract_fusion.6
  675.5 1.7 multiply_subtract_fusion.1
  677.2 1.7 multiply_subtract_fusion.2
  678.9 1.4 multiply_subtract_fusion.4
  681.7 6.3 multiply_subtract_fusion
  (75 shorter events, 6.9 us)
Async XLA Ops:
  0.7 4.7 copy-start.3
  0.7 4.7 copy-start.7
  0.7 5.4 copy-start.1
  0.7 6.0 copy-start.2
  0.7 6.6 copy-start.8
  5.4 121.6 %copy-start.4 = (bf16[3,24,2304]{2,1,0:T(8,128)(2,1)S(1)}, bf16[3,24,2304]{2,1,0:T(8,128)(2,1)}, u32[]{:S(2)}) copy-start(bf16[3,24,2304]{2,1,0:T(8,128)(2,1)} %param.41) | copy-start | bytes 995332
  5.4 121.6 %copy-start.13 = (bf16[3,24,768]{2,1,0:T(8,128)(2,1)S(1)}, bf16[3,24,768]{2,1,0:T(8,128)(2,1)}, u32[]{:S(2)}) copy-start(bf16[3,24,768]{2,1,0:T(8,128)(2,1)} %param.42) | copy-start | bytes 331780
  525.6 148.5 %copy-start.5 = (f32[6,512]{1,0:T(8,128)S(1)}, f32[6,512]{1,0:T(8,128)}, u32[]{:S(2)}) copy-start(f32[6,512]{1,0:T(8,128)} %gains_ref.3) | copy-start | bytes 36868
  525.6 148.5 %copy-start.21 = (f32[6,512]{1,0:T(8,128)S(1)}, f32[6,512]{1,0:T(8,128)}, u32[]{:S(2)}) copy-start(f32[6,512]{1,0:T(8,128)} %param.67) | copy-start | bytes 36868
  525.6 148.5 %copy-start.22 = (f32[6,512]{1,0:T(8,128)S(1)}, f32[6,512]{1,0:T(8,128)}, u32[]{:S(2)}) copy-start(f32[6,512]{1,0:T(8,128)} %param.66) | copy-start | bytes 36868
  525.6 149.9 %copy-start.9 = (f32[64,512]{1,0:T(8,128)S(1)}, f32[64,512]{1,0:T(8,128)}, u32[]{:S(2)}) copy-start(f32[64,512]{1,0:T(8,128)} %param.64) | copy-start | bytes 393220
  525.6 149.9 %copy-start.10 = (f32[64,512]{1,0:T(8,128)S(1)}, f32[64,512]{1,0:T(8,128)}, u32[]{:S(2)}) copy-start(f32[64,512]{1,0:T(8,128)} %param.63) | copy-start | bytes 393220
  525.6 151.6 %copy-start.11 = (f32[16,2048]{1,0:T(8,128)S(1)}, f32[16,2048]{1,0:T(8,128)}, u32[]{:S(2)}) copy-start(f32[16,2048]{1,0:T(8,128)} %param.61) | copy-start | bytes 393220
  525.6 151.6 %copy-start.12 = (f32[16,2048]{1,0:T(8,128)S(1)}, f32[16,2048]{1,0:T(8,128)}, u32[]{:S(2)}) copy-start(f32[16,2048]{1,0:T(8,128)} %param.60) | copy-start | bytes 393220
  525.6 153.3 %copy-start.16 = (f32[16,512]{1,0:T(8,128)S(1)}, f32[16,512]{1,0:T(8,128)}, u32[]{:S(2)}) copy-start(f32[16,512]{1,0:T(8,128)} %param.58) | copy-start | bytes 98308
  525.6 153.2 %copy-start.17 = (f32[16,512]{1,0:T(8,128)S(1)}, f32[16,512]{1,0:T(8,128)}, u32[]{:S(2)}) copy-start(f32[16,512]{1,0:T(8,128)} %param.57) | copy-start | bytes 98308
  525.7 154.6 %copy-start.15 = (f32[16,1536]{1,0:T(8,128)S(1)}, f32[16,1536]{1,0:T(8,128)}, u32[]{:S(2)}) copy-start(f32[16,1536]{1,0:T(8,128)} %param.54) | copy-start | bytes 294916
  669.2 11.1 %copy-start.6 = (f32[16,2048]{1,0:T(8,128)S(1)}, f32[16,2048]{1,0:T(8,128)}, u32[]{:S(2)}) copy-start(f32[16,2048]{1,0:T(8,128)} %get-tuple-element.90) | copy-start | bytes 393220
  669.2 11.1 %copy-start.14 = (f32[16,1536]{1,0:T(8,128)S(1)}, f32[16,1536]{1,0:T(8,128)}, u32[]{:S(2)}) copy-start(f32[16,1536]{1,0:T(8,128)} %param.55) | copy-start | bytes 294916
  669.2 11.9 %copy-start.18 = (f32[16,512]{1,0:T(8,128)S(1)}, f32[16,512]{1,0:T(8,128)}, u32[]{:S(2)}) copy-start(f32[16,512]{1,0:T(8,128)} %param.52) | copy-start | bytes 98308
  669.2 11.9 %copy-start.19 = (f32[16,512]{1,0:T(8,128)S(1)}, f32[16,512]{1,0:T(8,128)}, u32[]{:S(2)}) copy-start(f32[16,512]{1,0:T(8,128)} %param.51) | copy-start | bytes 98308
  669.2 11.8 %copy-start.20 = (f32[16,512]{1,0:T(8,128)S(1)}, f32[16,512]{1,0:T(8,128)}, u32[]{:S(2)}) copy-start(f32[16,512]{1,0:T(8,128)} %get-tuple-element.89) | copy-start | bytes 98308
  669.2 12.5 %copy-start = (f32[7680,64]{0,1:T(8,128)S(1)}, f32[7680,64]{0,1:T(8,128)}, u32[]{:S(2)}) copy-start(f32[7680,64]{0,1:T(8,128)} %param.47) | copy-start | bytes 5898244

commit v5 on v4

--- a/solution.py
+++ b/solution.py
@@ -291,22 +291,27 @@
             if stream[0] == number:
                 self.first(i).start()
 
+    def take(self, i, s):
+        stream = self.streams[i]
+        block = self.slots(stream).at[s - 1]
+        self.remote(i, s - 1, block).wait_recv()
+
+        def onward():
+            mine = self.pieces[stream[0]][2].at[self.place(stream, stream[3] - s)]
+            block[...] = (block[...].astype(F32) + mine[...].astype(F32)).astype(B16)
+            self.remote(i, s, block).start()
+
+        on_condition(s < stream[3], onward)
+
     def serve(self, s):
         for i, stream in enumerate(self.streams):
-            hops = stream[3]
-
-            def take(i=i, stream=stream, hops=hops):
-                block = self.slots(stream).at[s - 1]
-                self.remote(i, s - 1, block).wait_recv()
-
-                def onward():
-                    mine = self.pieces[stream[0]][2].at[self.place(stream, hops - s)]
-                    block[...] = (block[...].astype(F32) + mine[...].astype(F32)).astype(B16)
-                    self.remote(i, s, block).start()
-
-                pl.when(s < hops)(onward)
-
-            on_condition(True if hops == self.longest else s <= hops, take)
+            whole = stream[3] == self.longest
+            on_condition(True if whole else s <= stream[3], functools.partial(self.take, i, s))
+
+    def serve_piece(self, number, s):
+        for i, stream in enumerate(self.streams):
+            if stream[0] == number and s <= stream[3]:
+                self.take(i, s)
 
     def serve_range(self, low, high):
         def body(s, carry):
@@ -336,12 +341,12 @@
 
 def settle_kernel(D, V, rings, *refs):
     count = len(rings)
-    table_in, dx_ref, ids_ref, gains_ref = refs[:4]
-    dense_in, refs = refs[4 : 4 + count], refs[4 + count :]
+    dl_in, turned_ref, dx_ref, ids_ref, gains_ref = refs[:5]
+    dense_in, refs = refs[5 : 5 + count], refs[5 + count :]
     table_out, totals_out = refs[:2]
     dense_out, refs = refs[2 : 2 + count], refs[2 + count :]
-    dx_all, table_sums, table_slots, first, second = refs[:5]
-    dense_sums, refs = refs[5 : 5 + count], refs[5 + count :]
+    dl_ref, dl_sem, dx_all, table_sums, table_slots, first, second = refs[:7]
+    dense_sums, refs = refs[7 : 7 + count], refs[7 + count :]
     dense_slots, refs = refs[: 2 * count], refs[2 * count :]
     ts, tr, ds, dr, cs, cr, hs, hr, xs, xr, ns, nr = refs
     d, v = lax.axis_index("dp"), lax.axis_index("vocab")
@@ -370,6 +375,11 @@
     peers = [(d, lax.rem(v + k, V)) for k in range(1, V)]
     peers += [(lax.rem(d + k, D), v) for k in range(1, D)]
     near = [r.device(r.at(k)) for r in (over_dp, *chips.values()) for k in (1, -1)]
+
+    def load(c):
+        return pltpu.make_async_copy(dl_in.at[c], dl_ref.at[c % 2], dl_sem.at[c])
+
+    load(0).start()
     greet(near + peers)
 
     def other(k):
@@ -409,28 +419,50 @@
 
         lax.fori_loop(0, D * half, add, 0)
         dense.begin(k)
+    across(0, dx_ref, v + 1 - 2 * core).wait_recv()
+
+    def head(c):
+        if c + 1 < chunks:
+            load(c + 1).start()
+        load(c).wait()
+        return mm(turned_ref[...], dl_ref[c % 2])
+
+    def spread(grad, c, parts):
+        lane = lax.broadcasted_iota(jnp.int32, (length, tile), 1) + c * tile
+        for part in parts:
+            for slot in (lax.rem(chip + part, half) * 2, lax.rem(chip + part, half) * 2 + 1):
+                ids = ids_ref[pl.ds(pl.multiple_of(slot * length, length), length), :]
+                grad = grad + mm(dx_all[slot], jnp.where(lane == ids, 1.0, 0.0).astype(B16))
+        return grad
+
+    def store(c, grad):
+        table_sums[c] = grad.astype(B16).reshape(D, columns, tile)
+
+    early = min(2, chunks)
+    for c in range(early):
+        store(c, spread(head(c), c, [0]))
     for k in range(1, half):
         slot = other(-k)
         send(k).wait_recv()
         across(k, dx_all.at[slot], slot).start()
-    for k in range(half):
+    for k in range(1, half):
         across(k, dx_ref, other(-k) + 1 - 2 * core).wait_recv()
-
-    for c in range(chunks):
-        grad = table_in[:, c * tile : (c + 1) * tile].astype(F32)
-        lane = lax.broadcasted_iota(jnp.int32, (length, tile), 1) + c * tile
-        for k in range(V):
-            hit = jnp.where(lane == ids_ref[k * length : (k + 1) * length, :], 1.0, 0.0).astype(B16)
-            grad = grad + mm(dx_all[k], hit)
-        table_sums[c] = grad.astype(B16).reshape(D, columns, tile)
-        table.begin(c)
-        dense.serve_range(1 + c * dense.longest // chunks, 1 + (c + 1) * dense.longest // chunks)
+    waves = chunks + table.longest
+    for w in range(waves):
+        if w < early:
+            store(w, spread(table_sums[w].reshape(width, tile).astype(F32), w, range(1, half)))
+        elif w < chunks:
+            store(w, spread(head(w), w, range(half)))
+        if w < chunks:
+            table.begin(w)
+        for c in range(max(0, w - table.longest), min(w, chunks)):
+            table.serve_piece(c, w - c)
+        dense.serve_range(1 + w * dense.longest // waves, 1 + (w + 1) * dense.longest // waves)
     squares = jnp.zeros((1, 1), F32)
     for k in range(count):
         total = dense.total(k)
         dense_out[k][...] = total
         squares += jnp.sum(jnp.sum(total * total, 1, keepdims=True), 0, keepdims=True)
-    table.serve_range(1, table.longest + 1)
     for c in range(chunks):
         total = table.total(c)
         table_out[:, c * tile : (c + 1) * tile] = total
@@ -471,11 +503,10 @@
     table.finish()
 
 
-def settle(D, V, grad, dx, ids, gains, dense, rings, ident):
-    width, size = grad.shape
-    length = dx.shape[1]
-    tile = tile_of(size, V * length)
-    chunks, columns = size // tile, width // D
+def settle(D, V, dl, turned, dx, ids, gains, dense, rings, ident):
+    width, length = dx.shape
+    chunks, tokens, tile = dl.shape
+    size, columns = chunks * tile, width // D
     n = D * V // 2
     count = len(dense)
     blocks = [a.shape[-2:] for a in dense]
@@ -488,9 +519,11 @@
         functools.partial(settle_kernel, D, V, rings),
         out_shape=[jax.ShapeDtypeStruct((columns, size), F32), jax.ShapeDtypeStruct(gains.shape, F32)]
         + [jax.ShapeDtypeStruct(block, F32) for block in blocks],
-        in_specs=[IN_VMEM] * (4 + count),
+        in_specs=[ANYWHERE] + [IN_VMEM] * (4 + count),
         out_specs=[IN_VMEM] * (2 + count),
         scratch_shapes=[
+            pltpu.VMEM((2, tokens, tile), B16),
+            sems(chunks),
             pltpu.VMEM((V, width, length), B16),
             pltpu.VMEM((chunks, D, columns, tile), B16),
             pltpu.VMEM((chunks, D - 1, columns, tile), B16),
@@ -507,7 +540,7 @@
         compiler_params=pltpu.CompilerParams(
             collective_id=ident, has_side_effects=True, vmem_limit_bytes=62 * MIB
         ),
-    )(grad, dx, ids, gains, *dense)
+    )(dl, turned, dx, ids, gains, *dense)
 
 
 def tile_of(size, tokens=1):
@@ -547,7 +580,7 @@
     kept, refs = refs[17:23], refs[23:]
     top_ref, sum_ref, pick_ref, dh_ref, dl_ref, slots, own_ref, bias_ref, sums, taken = refs[:10]
     hs, hr, xs, xr, es, er, fs, fr, ps, pr = refs[10:20]
-    gather = Gather(D, V, spec, (first_ref, mid_ref, second_ref), (first_out, mid_out, second_out), refs[20:], True)
+    gather = Gather(D, V, spec, (first_ref, mid_ref, second_ref), (first_out, mid_out, second_out), refs[20:])
     d, v = lax.axis_index("dp"), lax.axis_index("vocab")
     half = V // 2
     core, chip = lax.rem(v, 2), v // 2
@@ -558,7 +591,7 @@
     peers = [(d, lax.rem(v + k, V)) for k in range(1, V)]
     greet(gather.neighbours + peers)
     marks = [k * gather.units // 24 for k in range(25)]
-    gather.begin(0)
+    gather.begin()
 
     def other(k):
         return lax.rem(chip + k + half, half) * 2 + core
@@ -611,16 +644,15 @@
     for k in range(1, half):
         pick_for(k, 0, tiles)
         swap(k).start()
-    gather.begin(1)
     gather.serve_range(marks[0], marks[1])
     for k in range(1, half):
         join(k)
         pass_on(k).start()
     pick_for(0, 0, tiles // 2)
-    gather.begin(2)
+    gather.serve_range(marks[1], marks[2])
     pick_for(0, tiles // 2, tiles)
     swap(0).start()
-    gather.serve_range(marks[1], marks[3])
+    gather.serve_range(marks[2], marks[4])
     join(0)
     x = sums[chip].astype(F32)
     for k in range(1, half):
@@ -629,10 +661,10 @@
     place_of = bias_of(segment_ref, bias_ref)
     lane = lax.broadcasted_iota(jnp.int32, (length, pos_ref.shape[0]), 1)
     x = x + mm(jnp.where(lane == place_of, 1.0, 0.0).astype(B16), pos_ref[...])
-    gather.serve_range(marks[3], marks[4])
-    between = lambda: gather.serve_range(marks[4], marks[6])
+    gather.serve_range(marks[4], marks[5])
+    between = lambda: gather.serve_range(marks[5], marks[7])
     learn(x, attention_ref, up_ref, down_ref, gains_ref, bias_ref, own_ref, kept, between)
-    gather.serve_range(marks[6], marks[7])
+    gather.serve_range(marks[7], marks[8])
 
     def place(slot):
         return hidden_ref.at[pl.ds(pl.multiple_of(slot * length, length), length)]
@@ -673,7 +705,7 @@
                 hit = lane == given_ref[rows, 1:2].astype(jnp.int32) - t * tile
                 pick_ref[rows, :] += lane_fold(jnp.where(hit, logits, 0.0), jnp.add)
         parts = half * tiles
-        gather.serve_range(due(u, parts, marks[7], marks[19]), due(u + 1, parts, marks[7], marks[19]))
+        gather.serve_range(due(u, parts, marks[8], marks[23]), due(u + 1, parts, marks[8], marks[23]))
         return carry
 
     lax.fori_loop(0, tiles, pass_one, 0)
@@ -711,7 +743,7 @@
         picked = picked + slots[k, 2:3, :]
     rows_out[...] = jnp.broadcast_to(top + jnp.log(total), rows_out.shape)
     rows_out[1:2, :] = picked
-    gather.serve_range(marks[19], marks[24])
+    gather.serve_range(marks[23], marks[24])
     for k in range(1, half):
         pass_on(k).wait_send()
         send(k).wait_send()
@@ -900,8 +932,8 @@
 
 
 def head_grad_kernel(
-    V, teacher_ref, hidden_ref, turned_ref, table_ref, given_ref, dtwo_ref, grad_ref, rows_ref,
-    dl_ref, sum_ref, cross_ref, dh_ref, sums, taken, es, er, fs, fr,
+    V, teacher_ref, hidden_ref, table_ref, given_ref, dtwo_ref, dl_ref, rows_ref,
+    sum_ref, cross_ref, dh_ref, sums, taken, es, er, fs, fr,
 ):
     step = pl.program_id(0)
     tile = table_ref.shape[1]
@@ -933,10 +965,9 @@
             lane = lax.broadcasted_iota(jnp.int32, logits.shape, 1)
             hit = lane == given_ref[rows, 1:2].astype(jnp.int32) - step * tile
             both = soft * ((1.0 + MIX_ALPHA) * weight) - target * (MIX_ALPHA * weight)
-            dl_ref[rows, :] = jnp.where(hit, both - weight, both).astype(B16)
+            dl_ref[0, rows, :] = jnp.where(hit, both - weight, both).astype(B16)
         rows = slice(row * length, (row + 1) * length)
-        sum_ref[rows, :] += mm(dl_ref[rows, :], table_ref[...], (1, 1))
-    grad_ref[...] = mm(turned_ref[...], dl_ref[...]).astype(B16)
+        sum_ref[rows, :] += mm(dl_ref[0, rows, :], table_ref[...], (1, 1))
 
     @pl.when(step == pl.num_programs(0) - 1)
     def _():
@@ -977,9 +1008,9 @@
             pass_on(k).wait_send()
 
 
-def head_grad(V, teacher, hidden, turned, table, given, ident):
+def head_grad(V, teacher, hidden, table, given, ident):
     count, length, size = teacher.shape
-    width, tokens = turned.shape
+    tokens, width = hidden.shape
     tile = tile_of(size, tokens)
     whole = lambda *shape: pl.BlockSpec(shape, lambda j: (0, 0))
     striped = pl.BlockSpec((width, tile), lambda j: (0, j))
@@ -988,16 +1019,15 @@
         grid=(size // tile,),
         out_shape=[
             jax.ShapeDtypeStruct((length, width), F32),
-            jax.ShapeDtypeStruct((width, size), B16),
+            jax.ShapeDtypeStruct((size // tile, tokens, tile), B16),
             jax.ShapeDtypeStruct((8, tokens), F32),
         ],
         in_specs=[
             pl.BlockSpec((count, length, tile), lambda j: (0, 0, j)),
-            whole(tokens, width), whole(width, tokens), striped, whole(tokens, 4),
+            whole(tokens, width), striped, whole(tokens, 4),
         ],
-        out_specs=[whole(length, width), striped, whole(8, tokens)],
+        out_specs=[whole(length, width), pl.BlockSpec((1, tokens, tile), lambda j: (j, 0, 0)), whole(8, tokens)],
         scratch_shapes=[
-            pltpu.VMEM((tokens, tile), B16),
             pltpu.VMEM((tokens, width), F32),
             pltpu.VMEM((tokens, 128), F32),
             pltpu.VMEM((tokens, width), B16),
@@ -1008,7 +1038,7 @@
         compiler_params=pltpu.CompilerParams(
             collective_id=ident, has_side_effects=True, vmem_limit_bytes=62 * MIB
         ),
-    )(teacher, hidden, turned, table, given)
+    )(teacher, hidden, table, given)
 
 
 def mm(a, b, over=(1, 0)):
@@ -1283,7 +1313,7 @@
     teacher, told = teacher_stats(V, groups, top, teacher_table, 5)
     teacher_lse, tcross = told[0], told[1]
     given = jnp.stack([weight, labels_here[:, 0].astype(F32), student_lse, teacher_lse], 1)
-    dtwo, grad_head, cross = head_grad(V, teacher, hidden_all, turned, table, given, 6)
+    dtwo, dlogits, cross = head_grad(V, teacher, hidden_all, table, given, 6)
     once = jnp.sum(weight * (MIX_ALPHA * (tcross - teacher_lse + student_lse) + student_lse - picked))
     loss_part = jnp.where(v == 0, once, 0.0) - MIX_ALPHA * jnp.sum(weight * cross[0])
 
@@ -1295,7 +1325,7 @@
     scalars = jnp.where(lane == 1, loss_part, 0.0)
     owners = lambda g: g.reshape(D * V // 2, 2, -1, g.shape[1])
     grad_embed, totals, owned_attention, owned_up, owned_down, owned_pos = settle(
-        D, V, grad_head, turned_dx, ids_here, jnp.concatenate([grad_gains, scalars], 0),
+        D, V, dlogits, turned, turned_dx, ids_here, jnp.concatenate([grad_gains, scalars], 0),
         [owners(grad_attention), owners(grad_up), owners(grad_down), owners(grad_pos)], (0, 1, 2, 1), 7,
     )
     owned = (owned_pos, owned_attention[:, : 3 * width], owned_attention[:, 3 * width :], owned_up, owned_down)

time: 698 us -> 684 us (0.980)
  Pallas kernels: 646 us -> 632 us
    pallas_call x1, Pallas kernels: 90.8 us -> 77.9 us  [head_grad(): pl.pallas_call(functools.partial(head_grad_kernel, V), grid=(size // tile...]
where the time goes in v5:
time: 684 us; the launch traced here: 675 us
  Pallas kernels  632 us (92%)
  other arithmetic  26.5 us (4%)
  local copies, waits for them, and re-layouts  9.33 us (1%)
  between operations  7.13 us (1%)
    pallas_call x1, Pallas kernels, study(): pl.pallas_call(functools.partial(study_kernel, D, V, spec), out_shape=sha...  189 us
    pallas_call x1, Pallas kernels, settle(): pl.pallas_call(functools.partial(settle_kernel, D, V, rings), out_shape=[...  148 us
    pallas_call x1, Pallas kernels, ring_gather(): pl.pallas_call(functools.partial(gather_kernel, D, V, spec, len(arrays)),...  114 us
    pallas_call x1, Pallas kernels, head_grad(): pl.pallas_call(functools.partial(head_grad_kernel, V), grid=(size // tile...  77.9 us
    pallas_call x1, Pallas kernels, teacher_stats(): pl.pallas_call(functools.partial(teacher_stats_kernel, V), grid=(V // 2 *...  52.2 us
    pallas_call x1, Pallas kernels, back(): pl.pallas_call(back_kernel, in_specs=[IN_VMEM] * len(inputs), out_specs=[...  26.7 us
    pallas_call x1, Pallas kernels, teach(): pl.pallas_call(teach_kernel, grid_spec=pltpu.PrefetchScalarGridSpec(num_s...  24.5 us
    sub x7, other arithmetic, adam(): return (first, second, weight - rate * (update + WEIGHT_DECAY * weight))  13.8 us

profile of v5, /device:TPU:0, one launch (start us, length us, event | category | flops | bytes accessed | tf_op | source)
XLA Modules:
  0.0 675.5 jit_solution(1213507540687944228)
XLA Ops:
  1.4 1.3 concatenate.30
  2.8 2.6 convert_element_type.67
  7.9 114.2 %shard_map.497 = (bf16[8,2,32,7680]{3,2,1,0:T(8,128)(2,1)}, bf16[1,32,16,2048]{3,2,1,0:T(8,128)(2,1)}, bf16[1,32,16,2048]{3,2,1,0:T(8,128)(2,1)}, bf16[1,32,64,5...) custom-call(bf16[2,32,7680]{2,1,0:T(8,128)(2,1)} %bitcast.76, ...), custom_call_target="tpu_custom_call" | custom-call | tf_op jit(solution)/shard_map/pallas_call | solution.py:247
  122.1 0.9 constant_dynamic-slice_fusion
  123.0 1.8 fusion.5
  125.6 1.3 copy.84.refs_4_
  127.7 189.5 %shard_map.498 = (bf16[3,32,24,3072]{3,2,1,0:T(8,128)(2,1)}, bf16[3,32,24,3072]{3,2,1,0:T(8,128)(2,1)}, bf16[3,32,96,768]{3,2,1,0:T(8,128)(2,1)}, bf16[2048,512]...) custom-call(bf16[3,24,3072]{2,1,0:T(8,128)(2,1)} %pad_maximum_fusion, ...), custom_call_target="tpu_custom_call" | custom-call | tf_op jit(solution)/shard_map/pallas_call | solution.py:766
  317.2 24.5 %shard_map.499.own_ref = bf16[512,768]{1,0:T(8,128)(2,1)} custom-call(s32[1]{0:T(128)} %copy.93.group_ref, bf16[1,512,768]{2,1,0:T(8,128)(2,1)} %x_ref.1, s32[1,512]{1,0:T(1,128)} %segment_ref.3, bf16[3,768,3072]{2,1,0:T(8,128)(2,1)} %bitcast.67, bf16[3,768,3072]{2,1,0:T(8,128)(2,1)} %bitcast.68, bf16[3,3072,768]{2,1,0:T(8,128)(2,1)} %bitcast.69, ...), custom_call_target="tpu_custom_call" | custom-call | tf_op jit(solution)/shard_map/pallas_call | solution.py:1140
  342.3 52.2 %shard_map.500 = (bf16[4,512,7680]{2,1,0:T(8,128)(2,1)}, f32[8,2048]{1,0:T(8,128)}) custom-call(s32[4]{0:T(128)} %slice_reduce_fusion.2.group_ref, bf16[512,768]{1,0:T(8,128)(2,1)} %shard_map.499.own_ref, bf16[3,768,7680]{2,1,0:T(8,128)(2,1)} %table_ref.1), custom_call_target="tpu_custom_call" | custom-call | tf_op jit(solution)/shard_map/pallas_call | solution.py:907
  394.6 1.0 subtract_reduce_fusion
  396.3 1.3 copy.85.given_ref
  397.6 77.9 %shard_map.501 = (f32[512,512]{1,0:T(8,128)}, bf16[6,2048,1280]{2,1,0:T(8,128)(2,1)}, f32[8,2048]{1,0:T(8,128)}) custom-call(bf16[4,512,7680]{2,1,0:T(8,128)(2,1)} %get-tuple-element.67.teacher_ref, bf16[2048,512]{1,0:T(8,128)(2,1)} %get-tuple-element.68.hidden_ref, bf16[512,7680]{1,0:T(8,128)(2,1)} %bitcast.66, f32[2048,4]{1,0:T(8,128)} %copy.85.given_ref), custom_call_target="tpu_custom_call" | custom-call | tf_op jit(solution)/shard_map/pallas_call | solution.py:1017
  475.6 0.8 slice.54
  478.3 26.7 %shard_map.502 = (bf16[512,512]{1,0:T(8,128)(2,1)}, bf16[512,2048]{1,0:T(8,128)(2,1)}, bf16[512,2048]{1,0:T(8,128)(2,1)}, bf16[2048,512]{1,0:T(8,128)(2,1)}, bf16[512,512]{1,0:T(8,128)(2,1)}, /*index=5*/f32[6,512]{1,0:T(8,128)}) custom-call(f32[512,512]{1,0:T(8,128)} %get-tuple-element.73.dtwo_ref, s32[1,512]{1,0:T(1,128)} %segment_ref.3, ...), custom_call_target="tpu_custom_call" | custom-call | tf_op jit(solution)/shard_map/pallas_call | solution.py:1239
  505.0 1.3 pad_maximum_fusion.4.refs_4_
  506.3 1.3 copy.86.refs_3_
  507.8 147.5 %shard_map.503 = (f32[64,7680]{1,0:T(8,128)}, f32[8,512]{1,0:T(8,128)}, f32[16,2048]{1,0:T(8,128)}, f32[16,2048]{1,0:T(8,128)}, f32[64,512]{1,0:T(8,128)}, /*index=5*/f32[16,512]{1,0:T(8,128)}) custom-call(bf16[6,2048,1280]{2,1,0:T(8,128)(2,1)} %get-tuple-element.71.refs_0_, bf16[512,2048]{1,0:T(8,128)(2,1)} %get-tuple-element.72.refs_1_, ...), custom_call_target="tpu_custom_call" | custom-call | tf_op jit(solution)/shard_map/pallas_call | solution.py:518
  655.4 1.4 fusion.24
  656.8 1.3 multiply_reduce_fusion
  660.3 1.4 multiply_subtract_fusion.6
  661.6 1.7 multiply_subtract_fusion.1
  663.3 1.7 multiply_subtract_fusion.2
  665.0 1.4 multiply_subtract_fusion.4
  667.9 6.3 multiply_subtract_fusion
  (75 shorter events, 6.9 us)
Async XLA Ops:
  0.7 4.7 copy-start.3
  0.7 4.7 copy-start.7
  0.7 5.4 copy-start.1
  0.7 6.0 copy-start.2
  0.7 6.6 copy-start.8
  5.4 121.6 %copy-start.4 = (bf16[3,24,2304]{2,1,0:T(8,128)(2,1)S(1)}, bf16[3,24,2304]{2,1,0:T(8,128)(2,1)}, u32[]{:S(2)}) copy-start(bf16[3,24,2304]{2,1,0:T(8,128)(2,1)} %param.41) | copy-start | bytes 995332
  5.4 121.6 %copy-start.13 = (bf16[3,24,768]{2,1,0:T(8,128)(2,1)S(1)}, bf16[3,24,768]{2,1,0:T(8,128)(2,1)}, u32[]{:S(2)}) copy-start(bf16[3,24,768]{2,1,0:T(8,128)(2,1)} %param.42) | copy-start | bytes 331780
  507.7 152.6 %copy-start.5 = (f32[6,512]{1,0:T(8,128)S(1)}, f32[6,512]{1,0:T(8,128)}, u32[]{:S(2)}) copy-start(f32[6,512]{1,0:T(8,128)} %gains_ref.3) | copy-start | bytes 36868
  507.7 152.6 %copy-start.21 = (f32[6,512]{1,0:T(8,128)S(1)}, f32[6,512]{1,0:T(8,128)}, u32[]{:S(2)}) copy-start(f32[6,512]{1,0:T(8,128)} %param.67) | copy-start | bytes 36868
  507.7 152.6 %copy-start.22 = (f32[6,512]{1,0:T(8,128)S(1)}, f32[6,512]{1,0:T(8,128)}, u32[]{:S(2)}) copy-start(f32[6,512]{1,0:T(8,128)} %param.66) | copy-start | bytes 36868
  507.7 153.9 %copy-start.9 = (f32[64,512]{1,0:T(8,128)S(1)}, f32[64,512]{1,0:T(8,128)}, u32[]{:S(2)}) copy-start(f32[64,512]{1,0:T(8,128)} %param.64) | copy-start | bytes 393220
  507.7 153.9 %copy-start.10 = (f32[64,512]{1,0:T(8,128)S(1)}, f32[64,512]{1,0:T(8,128)}, u32[]{:S(2)}) copy-start(f32[64,512]{1,0:T(8,128)} %param.63) | copy-start | bytes 393220
  507.7 155.6 %copy-start.11 = (f32[16,2048]{1,0:T(8,128)S(1)}, f32[16,2048]{1,0:T(8,128)}, u32[]{:S(2)}) copy-start(f32[16,2048]{1,0:T(8,128)} %param.61) | copy-start | bytes 393220
  507.7 155.6 %copy-start.12 = (f32[16,2048]{1,0:T(8,128)S(1)}, f32[16,2048]{1,0:T(8,128)}, u32[]{:S(2)}) copy-start(f32[16,2048]{1,0:T(8,128)} %param.60) | copy-start | bytes 393220
  507.7 157.3 %copy-start.16 = (f32[16,512]{1,0:T(8,128)S(1)}, f32[16,512]{1,0:T(8,128)}, u32[]{:S(2)}) copy-start(f32[16,512]{1,0:T(8,128)} %param.58) | copy-start | bytes 98308
  507.7 157.3 %copy-start.17 = (f32[16,512]{1,0:T(8,128)S(1)}, f32[16,512]{1,0:T(8,128)}, u32[]{:S(2)}) copy-start(f32[16,512]{1,0:T(8,128)} %param.57) | copy-start | bytes 98308
  507.8 158.7 %copy-start.15 = (f32[16,1536]{1,0:T(8,128)S(1)}, f32[16,1536]{1,0:T(8,128)}, u32[]{:S(2)}) copy-start(f32[16,1536]{1,0:T(8,128)} %param.54) | copy-start | bytes 294916
  655.3 11.1 %copy-start.6 = (f32[16,2048]{1,0:T(8,128)S(1)}, f32[16,2048]{1,0:T(8,128)}, u32[]{:S(2)}) copy-start(f32[16,2048]{1,0:T(8,128)} %get-tuple-element.90) | copy-start | bytes 393220
  655.3 11.1 %copy-start.14 = (f32[16,1536]{1,0:T(8,128)S(1)}, f32[16,1536]{1,0:T(8,128)}, u32[]{:S(2)}) copy-start(f32[16,1536]{1,0:T(8,128)} %param.55) | copy-start | bytes 294916
  655.3 11.9 %copy-start.18 = (f32[16,512]{1,0:T(8,128)S(1)}, f32[16,512]{1,0:T(8,128)}, u32[]{:S(2)}) copy-start(f32[16,512]{1,0:T(8,128)} %param.52) | copy-start | bytes 98308
  655.3 11.9 %copy-start.19 = (f32[16,512]{1,0:T(8,128)S(1)}, f32[16,512]{1,0:T(8,128)}, u32[]{:S(2)}) copy-start(f32[16,512]{1,0:T(8,128)} %param.51) | copy-start | bytes 98308
  655.4 11.9 %copy-start.20 = (f32[16,512]{1,0:T(8,128)S(1)}, f32[16,512]{1,0:T(8,128)}, u32[]{:S(2)}) copy-start(f32[16,512]{1,0:T(8,128)} %get-tuple-element.89) | copy-start | bytes 98308
  655.4 12.5 %copy-start = (f32[7680,64]{0,1:T(8,128)S(1)}, f32[7680,64]{0,1:T(8,128)}, u32[]{:S(2)}) copy-start(f32[7680,64]{0,1:T(8,128)} %param.47) | copy-start | bytes 5898244
